TPU v7x, 128 devices: a whole 4x4x4 slice. The times are simulated.
128 devices in a mesh: wide: 32 (over x, z, y_hi), narrow: 4 (over y_lo, core).
Axes of the slice: x: 4, y: 4 (y_hi: 2, y_lo: 2; y = y_hi * 2 + y_lo), z: 4, core: 2. Of those that a mesh axis runs over, the one named last changes fastest.
Arguments:
- homolog_embedding: bfloat16 [128, 5120, 256], P(('wide', 'narrow')), may hold values from -6 to 6
- presence_flags: float32 [128, 5120], P(('wide', 'narrow')), may hold values from 0.1 to 1
- standardizer_scaling: float32 [256], replicated, may hold values from 0.1 to 1.9
- standardizer_offset: float32 [256], replicated, may hold values from -3 to 3
- first_factor_coefficients: bfloat16 [256, 32], replicated, may hold values from -0.375 to 0.375
- first_factor_offset: float32 [32], replicated, may hold values from -3 to 3
- second_factor_coefficients: bfloat16 [256, 32], replicated, may hold values from -0.375 to 0.375
- second_factor_offset: float32 [32], replicated, may hold values from -3 to 3
- final_coefficients: bfloat16 [1024, 128], replicated, may hold values from -0.5 to 0.5
Outputs:
- pair_update: bfloat16 [1024, 5120, 128], P('wide', 'narrow')
All inputs are finite; a program needn't handle non-finite values.
Results may differ from a plain program's by a relative error of at most 0.0054.
Values may be sent and summed in bfloat16 or wider, within the bound.
No kernel may reach another device: no remote copies, remote signals or barrier semaphores. Data moves between devices by JAX's collectives and lax.ppermute only.
A program may use at most 128 MiB of HBM per device.

v0:
```python
import jax
import jax.numpy as jnp
from jax import lax
from jax.sharding import PartitionSpec as P

RD = 32


def standardize_features(homolog_embedding, standardizer_scaling, standardizer_offset):
    payload_elements = homolog_embedding.astype(jnp.float32)
    centre = jnp.mean(payload_elements, axis=-1, keepdims=True)
    spread = jnp.mean((payload_elements - centre) ** 2, axis=-1, keepdims=True)
    return (
        (payload_elements - centre) * lax.rsqrt(spread + 1e-05) * standardizer_scaling
        + standardizer_offset
    ).astype(jnp.bfloat16)


def affine_transform(standardized_embedding, weight, shift, mask_rows):
    shard_homolog_slice, position_numbers, channels = standardized_embedding.shape
    product = jnp.dot(
        standardized_embedding.reshape(shard_homolog_slice * position_numbers, channels),
        weight,
        preferred_element_type=jnp.float32,
    )
    product = (product.reshape(shard_homolog_slice, position_numbers, -1) + shift) * mask_rows[
        :, :, None
    ]
    return product.astype(jnp.bfloat16)


def on_device(
    homolog_embedding,
    presence_flags,
    standardizer_scaling,
    standardizer_offset,
    first_factor_coefficients,
    first_factor_offset,
    second_factor_coefficients,
    second_factor_offset,
    final_coefficients,
):
    n_wide = lax.axis_size("wide")
    n_narrow = lax.axis_size("narrow")
    shard_homolog_slice, position_numbers, ignored_element = homolog_embedding.shape
    width = first_factor_coefficients.shape[1]
    rows_all = RD * n_wide
    columns = position_numbers // n_narrow
    standardized_embedding = standardize_features(
        homolog_embedding, standardizer_scaling, standardizer_offset
    )
    first_factor_embeddings = affine_transform(
        standardized_embedding[:, :rows_all],
        first_factor_coefficients,
        first_factor_offset,
        presence_flags[:, :rows_all],
    )
    second_factor_embeddings = affine_transform(
        standardized_embedding, second_factor_coefficients, second_factor_offset, presence_flags
    )
    left_mask = presence_flags[:, :rows_all].astype(jnp.bfloat16)
    right_mask = presence_flags.astype(jnp.bfloat16)
    piece = position_numbers // (n_wide * n_narrow)
    right_order = (
        second_factor_embeddings.reshape(shard_homolog_slice, n_narrow, n_wide, piece, width)
        .transpose(0, 2, 1, 3, 4)
        .reshape(shard_homolog_slice, position_numbers, width)
    )
    mask_order = (
        right_mask.reshape(shard_homolog_slice, n_narrow, n_wide, piece)
        .transpose(0, 2, 1, 3)
        .reshape(shard_homolog_slice, position_numbers)
    )
    left_ex, lmask_ex, right_ex, rmask_ex = (
        lax.all_to_all(
            first_factor_embeddings, ("wide", "narrow"), split_axis=1, concat_axis=0, tiled=True
        ),
        lax.all_to_all(left_mask, ("wide", "narrow"), split_axis=1, concat_axis=0, tiled=True),
        lax.all_to_all(right_order, ("wide", "narrow"), split_axis=1, concat_axis=0, tiled=True),
        lax.all_to_all(mask_order, ("wide", "narrow"), split_axis=1, concat_axis=0, tiled=True),
    )
    left_all, lmask_all = (
        lax.all_gather(left_ex, "narrow", axis=1, tiled=True),
        lax.all_gather(lmask_ex, "narrow", axis=1, tiled=True),
    )
    right_all, rmask_all = (
        lax.all_gather(right_ex, "wide", axis=1, tiled=True),
        lax.all_gather(rmask_ex, "wide", axis=1, tiled=True),
    )
    count = jnp.einsum("si,sj->ij", lmask_all, rmask_all, preferred_element_type=jnp.float32)
    block = 4
    out_width = final_coefficients.shape[1]

    def pair_block(index):
        start = index * block
        left_blk = lax.dynamic_slice_in_dim(left_all, start, block, 1)
        outer = jnp.einsum(
            "sic,sje->ijce", left_blk, right_all, preferred_element_type=jnp.float32
        ).astype(jnp.bfloat16)
        mixed = jnp.dot(
            outer.reshape(block * columns, width * width),
            final_coefficients,
            preferred_element_type=jnp.float32,
        )
        mixed = mixed.reshape(block, columns, out_width)
        count_blk = lax.dynamic_slice_in_dim(count, start, block, 0)
        return (mixed / (0.001 + count_blk[:, :, None])).astype(jnp.bfloat16)

    blocks = lax.map(pair_block, jnp.arange(RD // block, dtype=jnp.int32))
    return blocks.reshape(RD, columns, out_width)


def solution(mesh):
    placed = (
        P(("wide", "narrow"), None, None),
        P(("wide", "narrow"), None),
        P(),
        P(),
        P(),
        P(),
        P(),
        P(),
        P(),
    )
    return jax.shard_map(
        on_device, mesh=mesh, in_specs=placed, out_specs=P("wide", "narrow", None), check_vma=False
    )
```

profile of v0, /device:TPU:0, one launch (start us, length us, event | category | flops | bytes accessed | tf_op | source)
XLA Modules:
  0.0 532.4 jit_solution(913692501924552094)
XLA Ops:
  25.6 29.1 %reduce.7 = bf16[5120,32]{1,0:T(8,128)(2,1)} reduce(bf16[5120,1,32]{2,1,0:T(2,128)(2,1)S(1)} %bitcast.74, bf16[]{:T(256)} %broadcast.47), dimensions={1}, to_apply=%bitcast.50.reduce_sub_computation | reduce | bytes 655362
  57.6 22.4 %all_to_all.57 = bf16[128,2,640]{2,1,0:T(2,128)(2,1)S(1)} all-to-all(bf16[128,2,640]{2,1,0:T(2,128)(2,1)S(1)} %reshape.111), channel_id=1, replica_groups=mesh['wide'=32,'narrow'=4] {'wide','narrow'}, dimensions={0} | all-to-all | bytes 655360 | tf_op jit(solution)/shard_map/all_to_all | solution.py:79
  91.8 8.4 %all-to-all-done.2 = bf16[1,128,8]{2,0,1:T(2,128)(2,1)S(1)} async-done(((bf16[1,128,8]{2,0,1:T(2,128)(2,1)}), bf16[1,128,8]{2,0,1:T(2,128)(2,1)S(1)}, u32[]{:S(2)}, u32[]{:S(2)}) %all-to-all-start.2) | async-done | bytes 2080 | tf_op jit(solution)/shard_map/all_to_all | solution.py:78
  115.1 9.8 %all-to-all-start = ((bf16[128,2,128]{2,1,0:T(2,128)(2,1)}), bf16[128,2,128]{2,1,0:T(2,128)(2,1)S(1)}, u32[]{:S(2)}, u32[]{:S(2)}) async-start(bf16[128,2,128]{2,1,0:T(2,128)(2,1)} %reshape.109), calls=%async_computation | async-start | bytes 131072 | tf_op jit(solution)/shard_map/all_to_all | solution.py:75
  124.9 98.0 %all-gather.1 = bf16[1,128,1280]{1,2,0:T(8,128)(2,1)S(1)} all-gather(bf16[1,128,40]{1,2,0:T(8,128)(2,1)S(1)} %copy.28), channel_id=3, replica_groups=mesh['wide'=32,'narrow'=4] {'wide'}, dimensions={2}, use_global_device_ids=true | all-gather | bytes 337920 | tf_op jit(solution)/shard_map/all_gather | solution.py:88
  223.5 9.2 %all_gather.12 = bf16[128,32,32]{2,1,0:T(8,128)(2,1)S(1)} all-gather(bf16[128,8,32]{2,1,0:T(8,128)(2,1)S(1)} %bitcast.80), channel_id=1, replica_groups=mesh['wide'=32,'narrow'=4] {'narrow'}, dimensions={1}, use_global_device_ids=true | all-gather | bytes 327680 | tf_op jit(solution)/shard_map/all_gather | solution.py:83
  233.8 16.4 %copy.30 = bf16[128,1280,32]{1,0,2:T(8,128)(2,1)} copy(bf16[128,1280,32]{0,2,1:T(8,128)(2,1)} %all-gather.4.cloned.1.call-done) | data formatting | bytes 20971520 | tf_op jit(solution)/shard_map/while | solution.py:109
  250.2 274.6 %while.10 = (s32[]{:T(128)}, bf16[8,4,1280,128]{3,2,1,0:T(8,128)(2,1)}, s32[8]{0:T(128)S(1)}, bf16[128,32,32]{0,2,1:T(8,128)(2,1)S(1)}, bf16[128,1280,32]{1,0,2:...) while((s32[]{:T(128)}, ...), condition=%wide.region_3.4_spmd, body=%wide.region_2.3_spmd.sunk | while | flops 2690913280 | bytes 54096556 | solution.py:109
  251.5 10.7 %fusion.37 = bf16[4,1280,32,32]{1,2,3,0:T(8,128)(2,1)} fusion(bf16[128,1280,32]{1,0,2:T(8,128)(2,1)} %get-tuple-element.140, bf16[128,32,32]{0,2,1:T(8,128)(2,1)S(1)} %get-tuple-element.139, s32[]{:T(128)S(6)} %select_n.5), kind=kOutput, calls=%fused_computation.1.clone.1 | convolution fusion | flops 1347420160 | bytes 21004292 | tf_op jit(solution)/shard_map/while/body/eval_jaxpr/sic,sje->ijce/dot_general | solution.py:97
  262.2 13.8 %copy.42 = bf16[4,1280,32,32]{1,3,2,0:T(8,128)(2,1)} copy(bf16[4,1280,32,32]{1,2,3,0:T(8,128)(2,1)} %fusion.37) | data formatting | bytes 20971520 | tf_op jit(solution)/shard_map/while/body/eval_jaxpr/convert_element_type | solution.py:99
  276.0 8.5 %fusion.38 = bf16[8,4,1280,128]{3,2,1,0:T(8,128)(2,1)} fusion(bf16[8,4,1280,128]{3,2,1,0:T(8,128)(2,1)} %get-tuple-element.126, s32[]{:T(128)} %get-tuple-element.125, bf16[4,1280,1024]{1,2,0:T(8,128)(2,1)} %bitcast.73, f32[4,1280]{1,0:T(4,128)S(1)} %dynamic-slice_add_fusion.2, bf16[1024,128]{1,0:T(8,128)(2,1)S(1)} %get-tuple-element.141), kind=kOutput, calls=%fused_computation.6.clone.1 | convolution fusion | flops 1343488000 | bytes 12079616 | tf_op jit(solution)/shard_map/while/body/eval_jaxpr/dot_general | solution.py:100
  285.8 10.7 %fusion.37 = bf16[4,1280,32,32]{1,2,3,0:T(8,128)(2,1)} fusion(bf16[128,1280,32]{1,0,2:T(8,128)(2,1)} %get-tuple-element.140, bf16[128,32,32]{0,2,1:T(8,128)(2,1)S(1)} %get-tuple-element.139, s32[]{:T(128)S(6)} %select_n.5), kind=kOutput, calls=%fused_computation.1.clone.1 | convolution fusion | flops 1347420160 | bytes 21004292 | tf_op jit(solution)/shard_map/while/body/eval_jaxpr/sic,sje->ijce/dot_general | solution.py:97
  296.5 13.8 %copy.42 = bf16[4,1280,32,32]{1,3,2,0:T(8,128)(2,1)} copy(bf16[4,1280,32,32]{1,2,3,0:T(8,128)(2,1)} %fusion.37) | data formatting | bytes 20971520 | tf_op jit(solution)/shard_map/while/body/eval_jaxpr/convert_element_type | solution.py:99
  310.3 8.5 %fusion.38 = bf16[8,4,1280,128]{3,2,1,0:T(8,128)(2,1)} fusion(bf16[8,4,1280,128]{3,2,1,0:T(8,128)(2,1)} %get-tuple-element.126, s32[]{:T(128)} %get-tuple-element.125, bf16[4,1280,1024]{1,2,0:T(8,128)(2,1)} %bitcast.73, f32[4,1280]{1,0:T(4,128)S(1)} %dynamic-slice_add_fusion.2, bf16[1024,128]{1,0:T(8,128)(2,1)S(1)} %get-tuple-element.141), kind=kOutput, calls=%fused_computation.6.clone.1 | convolution fusion | flops 1343488000 | bytes 12079616 | tf_op jit(solution)/shard_map/while/body/eval_jaxpr/dot_general | solution.py:100
  320.1 10.7 %fusion.37 = bf16[4,1280,32,32]{1,2,3,0:T(8,128)(2,1)} fusion(bf16[128,1280,32]{1,0,2:T(8,128)(2,1)} %get-tuple-element.140, bf16[128,32,32]{0,2,1:T(8,128)(2,1)S(1)} %get-tuple-element.139, s32[]{:T(128)S(6)} %select_n.5), kind=kOutput, calls=%fused_computation.1.clone.1 | convolution fusion | flops 1347420160 | bytes 21004292 | tf_op jit(solution)/shard_map/while/body/eval_jaxpr/sic,sje->ijce/dot_general | solution.py:97
  330.8 13.8 %copy.42 = bf16[4,1280,32,32]{1,3,2,0:T(8,128)(2,1)} copy(bf16[4,1280,32,32]{1,2,3,0:T(8,128)(2,1)} %fusion.37) | data formatting | bytes 20971520 | tf_op jit(solution)/shard_map/while/body/eval_jaxpr/convert_element_type | solution.py:99
  344.7 8.5 %fusion.38 = bf16[8,4,1280,128]{3,2,1,0:T(8,128)(2,1)} fusion(bf16[8,4,1280,128]{3,2,1,0:T(8,128)(2,1)} %get-tuple-element.126, s32[]{:T(128)} %get-tuple-element.125, bf16[4,1280,1024]{1,2,0:T(8,128)(2,1)} %bitcast.73, f32[4,1280]{1,0:T(4,128)S(1)} %dynamic-slice_add_fusion.2, bf16[1024,128]{1,0:T(8,128)(2,1)S(1)} %get-tuple-element.141), kind=kOutput, calls=%fused_computation.6.clone.1 | convolution fusion | flops 1343488000 | bytes 12079616 | tf_op jit(solution)/shard_map/while/body/eval_jaxpr/dot_general | solution.py:100
  354.4 10.7 %fusion.37 = bf16[4,1280,32,32]{1,2,3,0:T(8,128)(2,1)} fusion(bf16[128,1280,32]{1,0,2:T(8,128)(2,1)} %get-tuple-element.140, bf16[128,32,32]{0,2,1:T(8,128)(2,1)S(1)} %get-tuple-element.139, s32[]{:T(128)S(6)} %select_n.5), kind=kOutput, calls=%fused_computation.1.clone.1 | convolution fusion | flops 1347420160 | bytes 21004292 | tf_op jit(solution)/shard_map/while/body/eval_jaxpr/sic,sje->ijce/dot_general | solution.py:97
  365.1 13.8 %copy.42 = bf16[4,1280,32,32]{1,3,2,0:T(8,128)(2,1)} copy(bf16[4,1280,32,32]{1,2,3,0:T(8,128)(2,1)} %fusion.37) | data formatting | bytes 20971520 | tf_op jit(solution)/shard_map/while/body/eval_jaxpr/convert_element_type | solution.py:99
  379.0 8.5 %fusion.38 = bf16[8,4,1280,128]{3,2,1,0:T(8,128)(2,1)} fusion(bf16[8,4,1280,128]{3,2,1,0:T(8,128)(2,1)} %get-tuple-element.126, s32[]{:T(128)} %get-tuple-element.125, bf16[4,1280,1024]{1,2,0:T(8,128)(2,1)} %bitcast.73, f32[4,1280]{1,0:T(4,128)S(1)} %dynamic-slice_add_fusion.2, bf16[1024,128]{1,0:T(8,128)(2,1)S(1)} %get-tuple-element.141), kind=kOutput, calls=%fused_computation.6.clone.1 | convolution fusion | flops 1343488000 | bytes 12079616 | tf_op jit(solution)/shard_map/while/body/eval_jaxpr/dot_general | solution.py:100
  388.8 10.7 %fusion.37 = bf16[4,1280,32,32]{1,2,3,0:T(8,128)(2,1)} fusion(bf16[128,1280,32]{1,0,2:T(8,128)(2,1)} %get-tuple-element.140, bf16[128,32,32]{0,2,1:T(8,128)(2,1)S(1)} %get-tuple-element.139, s32[]{:T(128)S(6)} %select_n.5), kind=kOutput, calls=%fused_computation.1.clone.1 | convolution fusion | flops 1347420160 | bytes 21004292 | tf_op jit(solution)/shard_map/while/body/eval_jaxpr/sic,sje->ijce/dot_general | solution.py:97
  399.5 13.8 %copy.42 = bf16[4,1280,32,32]{1,3,2,0:T(8,128)(2,1)} copy(bf16[4,1280,32,32]{1,2,3,0:T(8,128)(2,1)} %fusion.37) | data formatting | bytes 20971520 | tf_op jit(solution)/shard_map/while/body/eval_jaxpr/convert_element_type | solution.py:99
  413.3 8.5 %fusion.38 = bf16[8,4,1280,128]{3,2,1,0:T(8,128)(2,1)} fusion(bf16[8,4,1280,128]{3,2,1,0:T(8,128)(2,1)} %get-tuple-element.126, s32[]{:T(128)} %get-tuple-element.125, bf16[4,1280,1024]{1,2,0:T(8,128)(2,1)} %bitcast.73, f32[4,1280]{1,0:T(4,128)S(1)} %dynamic-slice_add_fusion.2, bf16[1024,128]{1,0:T(8,128)(2,1)S(1)} %get-tuple-element.141), kind=kOutput, calls=%fused_computation.6.clone.1 | convolution fusion | flops 1343488000 | bytes 12079616 | tf_op jit(solution)/shard_map/while/body/eval_jaxpr/dot_general | solution.py:100
  423.1 10.7 %fusion.37 = bf16[4,1280,32,32]{1,2,3,0:T(8,128)(2,1)} fusion(bf16[128,1280,32]{1,0,2:T(8,128)(2,1)} %get-tuple-element.140, bf16[128,32,32]{0,2,1:T(8,128)(2,1)S(1)} %get-tuple-element.139, s32[]{:T(128)S(6)} %select_n.5), kind=kOutput, calls=%fused_computation.1.clone.1 | convolution fusion | flops 1347420160 | bytes 21004292 | tf_op jit(solution)/shard_map/while/body/eval_jaxpr/sic,sje->ijce/dot_general | solution.py:97
  433.8 13.8 %copy.42 = bf16[4,1280,32,32]{1,3,2,0:T(8,128)(2,1)} copy(bf16[4,1280,32,32]{1,2,3,0:T(8,128)(2,1)} %fusion.37) | data formatting | bytes 20971520 | tf_op jit(solution)/shard_map/while/body/eval_jaxpr/convert_element_type | solution.py:99
  447.6 8.5 %fusion.38 = bf16[8,4,1280,128]{3,2,1,0:T(8,128)(2,1)} fusion(bf16[8,4,1280,128]{3,2,1,0:T(8,128)(2,1)} %get-tuple-element.126, s32[]{:T(128)} %get-tuple-element.125, bf16[4,1280,1024]{1,2,0:T(8,128)(2,1)} %bitcast.73, f32[4,1280]{1,0:T(4,128)S(1)} %dynamic-slice_add_fusion.2, bf16[1024,128]{1,0:T(8,128)(2,1)S(1)} %get-tuple-element.141), kind=kOutput, calls=%fused_computation.6.clone.1 | convolution fusion | flops 1343488000 | bytes 12079616 | tf_op jit(solution)/shard_map/while/body/eval_jaxpr/dot_general | solution.py:100
  457.4 10.7 %fusion.37 = bf16[4,1280,32,32]{1,2,3,0:T(8,128)(2,1)} fusion(bf16[128,1280,32]{1,0,2:T(8,128)(2,1)} %get-tuple-element.140, bf16[128,32,32]{0,2,1:T(8,128)(2,1)S(1)} %get-tuple-element.139, s32[]{:T(128)S(6)} %select_n.5), kind=kOutput, calls=%fused_computation.1.clone.1 | convolution fusion | flops 1347420160 | bytes 21004292 | tf_op jit(solution)/shard_map/while/body/eval_jaxpr/sic,sje->ijce/dot_general | solution.py:97
  468.1 13.8 %copy.42 = bf16[4,1280,32,32]{1,3,2,0:T(8,128)(2,1)} copy(bf16[4,1280,32,32]{1,2,3,0:T(8,128)(2,1)} %fusion.37) | data formatting | bytes 20971520 | tf_op jit(solution)/shard_map/while/body/eval_jaxpr/convert_element_type | solution.py:99
  482.0 8.5 %fusion.38 = bf16[8,4,1280,128]{3,2,1,0:T(8,128)(2,1)} fusion(bf16[8,4,1280,128]{3,2,1,0:T(8,128)(2,1)} %get-tuple-element.126, s32[]{:T(128)} %get-tuple-element.125, bf16[4,1280,1024]{1,2,0:T(8,128)(2,1)} %bitcast.73, f32[4,1280]{1,0:T(4,128)S(1)} %dynamic-slice_add_fusion.2, bf16[1024,128]{1,0:T(8,128)(2,1)S(1)} %get-tuple-element.141), kind=kOutput, calls=%fused_computation.6.clone.1 | convolution fusion | flops 1343488000 | bytes 12079616 | tf_op jit(solution)/shard_map/while/body/eval_jaxpr/dot_general | solution.py:100
  491.7 10.7 %fusion.37 = bf16[4,1280,32,32]{1,2,3,0:T(8,128)(2,1)} fusion(bf16[128,1280,32]{1,0,2:T(8,128)(2,1)} %get-tuple-element.140, bf16[128,32,32]{0,2,1:T(8,128)(2,1)S(1)} %get-tuple-element.139, s32[]{:T(128)S(6)} %select_n.5), kind=kOutput, calls=%fused_computation.1.clone.1 | convolution fusion | flops 1347420160 | bytes 21004292 | tf_op jit(solution)/shard_map/while/body/eval_jaxpr/sic,sje->ijce/dot_general | solution.py:97
  502.4 13.8 %copy.42 = bf16[4,1280,32,32]{1,3,2,0:T(8,128)(2,1)} copy(bf16[4,1280,32,32]{1,2,3,0:T(8,128)(2,1)} %fusion.37) | data formatting | bytes 20971520 | tf_op jit(solution)/shard_map/while/body/eval_jaxpr/convert_element_type | solution.py:99
  516.3 8.5 %fusion.38 = bf16[8,4,1280,128]{3,2,1,0:T(8,128)(2,1)} fusion(bf16[8,4,1280,128]{3,2,1,0:T(8,128)(2,1)} %get-tuple-element.126, s32[]{:T(128)} %get-tuple-element.125, bf16[4,1280,1024]{1,2,0:T(8,128)(2,1)} %bitcast.73, f32[4,1280]{1,0:T(4,128)S(1)} %dynamic-slice_add_fusion.2, bf16[1024,128]{1,0:T(8,128)(2,1)S(1)} %get-tuple-element.141), kind=kOutput, calls=%fused_computation.6.clone.1 | convolution fusion | flops 1343488000 | bytes 12079616 | tf_op jit(solution)/shard_map/while/body/eval_jaxpr/dot_general | solution.py:100
  (80 shorter events, 55.8 us)
Async XLA Ops:
  6.5 11.4 %copy-start = (bf16[256,32]{0,1:T(8,128)(2,1)S(1)}, bf16[256,32]{0,1:T(8,128)(2,1)}, u32[]{:S(2)}) copy-start(bf16[256,32]{0,1:T(8,128)(2,1)} %param.17) | copy-start | bytes 49156
  6.5 7.0 %copy-start.2 = (bf16[1,5120,256]{2,1,0:T(8,128)(2,1)S(1)}, bf16[1,5120,256]{2,1,0:T(8,128)(2,1)}, u32[]{:S(2)}) copy-start(bf16[1,5120,256]{2,1,0:T(8,128)(2,1)} %param.11) | copy-start | bytes 7864324
  6.5 7.0 %copy-start.7 = (f32[256]{0:T(256)S(1)}, f32[256]{0:T(256)}, u32[]{:S(2)}) copy-start(f32[256]{0:T(256)} %param.13) | copy-start | bytes 3076
  6.5 7.0 %copy-start.6 = (f32[256]{0:T(256)S(1)}, f32[256]{0:T(256)}, u32[]{:S(2)}) copy-start(f32[256]{0:T(256)} %param.14) | copy-start | bytes 3076
  6.5 11.4 %copy-start.4 = (f32[1,5120]{1,0:T(1,128)S(1)}, f32[1,5120]{1,0:T(1,128)}, u32[]{:S(2)}) copy-start(f32[1,5120]{1,0:T(1,128)} %param.12) | copy-start | bytes 61444
  6.5 11.4 %copy-start.5 = (f32[32]{0:T(128)S(1)}, f32[32]{0:T(128)}, u32[]{:S(2)}) copy-start(f32[32]{0:T(128)} %param.18) | copy-start | bytes 388
  6.6 227.2 %all-gather.4.cloned.1.call-start = ((), (), s32[]{:S(2)}) async-start(), calls=%async_computation.4 | async-start | bytes 10813440 | tf_op jit(solution)/shard_map/all_gather | solution.py:87
  16.5 1.5 copy-start.3
  57.5 47.5 %copy-start.9 = (bf16[256,32]{0,1:T(8,128)(2,1)S(1)}, bf16[256,32]{0,1:T(8,128)(2,1)}, u32[]{:S(2)}) copy-start(bf16[256,32]{0,1:T(8,128)(2,1)} %param.15) | copy-start | bytes 49156
  57.6 47.5 %copy-start.10 = (f32[32]{0:T(128)S(1)}, f32[32]{0:T(128)}, u32[]{:S(2)}) copy-start(f32[32]{0:T(128)} %param.16) | copy-start | bytes 388
  86.1 14.1 %all-to-all-start.2 = ((bf16[1,128,8]{2,0,1:T(2,128)(2,1)}), bf16[1,128,8]{2,0,1:T(2,128)(2,1)S(1)}, u32[]{:S(2)}, u32[]{:S(2)}) async-start(bf16[1,128,8]{2,0,1:T(2,128)(2,1)} %all_to_all.52), calls=%async_computation.2 | async-start | bytes 131072 | tf_op jit(solution)/shard_map/all_to_all | solution.py:78
  100.2 14.9 %all-to-all-start.3 = ((bf16[1,128,40]{2,0,1:T(2,128)(2,1)}), bf16[1,128,40]{2,0,1:T(2,128)(2,1)S(1)}, u32[]{:S(2)}, u32[]{:S(2)}) async-start(bf16[1,128,40]{2,0,1:T(2,128)(2,1)} %copy.27), calls=%async_computation.3 | async-start | bytes 131072 | tf_op jit(solution)/shard_map/all_to_all | solution.py:80
  115.1 108.0 %all-to-all-start = ((bf16[128,2,128]{2,1,0:T(2,128)(2,1)}), bf16[128,2,128]{2,1,0:T(2,128)(2,1)S(1)}, u32[]{:S(2)}, u32[]{:S(2)}) async-start(bf16[128,2,128]{2,1,0:T(2,128)(2,1)} %reshape.109), calls=%async_computation | async-start | bytes 131072 | tf_op jit(solution)/shard_map/all_to_all | solution.py:75
  233.8 16.5 %copy-start.8 = (bf16[1024,128]{1,0:T(8,128)(2,1)S(1)}, bf16[1024,128]{1,0:T(8,128)(2,1)}, u32[]{:S(2)}) copy-start(bf16[1024,128]{1,0:T(8,128)(2,1)} %param.19) | copy-start | bytes 786436
  524.8 0.7 copy-start.1
Sparse Core Ops, SparseCore 0:
  85.5 116.3 all-gather.3
where the time goes:
time: 535 us; the launch traced here: 532 us
  matrix products  156 us (29%)
  local copies, waits for them, and re-layouts  153 us (29%)
  blocking collectives  135 us (25%)
  other arithmetic  41.3 us (8%)
  starting transfers between devices  19.4 us (4%)
  between operations  13.7 us (3%)
  waiting for transfers between devices  8.49 us (2%)
    convert_element_type x8, local copies, waits for them, and re-layouts, pair_block(): outer = jnp.einsum('sic,sje->ijce', left_blk, right_all, preferred_elemen...  111 us
    all_gather x1, blocking collectives, on_device(): lax.all_gather(rmask_ex, 'wide', axis=1, tiled=True)  98 us
    dot_general x8, matrix products, pair_block(): jnp.einsum('sic,sje->ijce', left_blk, right_all, preferred_element_type=j...  85.6 us
    dot_general x8, matrix products, pair_block(): jnp.dot(outer.reshape(block * columns, width * width), final_coefficients...  68.3 us
    unnamed x2, other arithmetic  31.3 us
    all_to_all x1, blocking collectives, on_device(): lax.all_to_all(right_order, ('wide', 'narrow'), split_axis=1, concat_axis...  22.4 us
    while x2, local copies, waits for them, and re-layouts, on_device(): blocks = lax.map(pair_block, jnp.arange(RD // block, dtype=jnp.int32))  17.5 us
  transfers between devices with their start and end apart: 4, of which 1 were waited for; matrix products, arithmetic and copies ran while one was open for 1% of the time, Pallas kernels for 0%

commit v1 on v0

v1 whole, which is shorter than its diff:
```python
import jax
import jax.numpy as jnp
from jax import lax
from jax.experimental import pallas as pl
from jax.experimental.pallas import tpu as pltpu
from jax.sharding import Mesh
from jax.sharding import PartitionSpec as P

RD = 32
CHUNK = 256
GROUP = 8
COLUMN = ("yh", "yl", "core")
PLANE = ("x", "z", "yh")
EVERY = ("x", "z", "yh", "yl", "core")
OFFSETS = (0, -1, 1, 2)
f32 = jnp.float32
bf16 = jnp.bfloat16


def vmem(mib):
    return pltpu.CompilerParams(vmem_limit_bytes=mib * 2**20)


def whole(*shape):
    return pl.BlockSpec(shape, lambda *_: (0,) * len(shape))


def project(x, mask, gain, bias, w_left, b_left, w_right, b_right):
    rows, features = x.shape
    quarter = rows // 4
    width = w_right.shape[0]
    left_rows = RD * 32
    sub = 256

    def kernel(x_ref, m_ref, g_ref, s_ref, wl_ref, bl_ref, wr_ref, br_ref, left_ref, right_ref):
        step = pl.program_id(0)
        for part in range(quarter // sub):
            at = slice(part * sub, (part + 1) * sub)
            v = x_ref[at, :].astype(f32)
            centre = jnp.mean(v, axis=-1, keepdims=True)
            v = v - centre
            spread = jnp.mean(v * v, axis=-1, keepdims=True)
            normed = (v * lax.rsqrt(spread + 1e-05) * g_ref[...] + s_ref[...]).astype(bf16)
            m = m_ref[0, :, at]

            def affine(w_ref, b_ref):
                y = lax.dot_general(
                    w_ref[...], normed, (((1,), (1,)), ((), ())), preferred_element_type=f32
                )
                return (y + b_ref[...]) * m

            y = affine(wr_ref, br_ref).astype(bf16)
            right_ref[0, 0, :, at] = y
            right_ref[1, 0, :, at] = y
            if (part + 1) * sub <= left_rows:

                @pl.when(step == 0)
                def _():
                    left_ref[at, :] = affine(wl_ref, bl_ref).T.astype(bf16)

    return pl.pallas_call(
        kernel,
        grid=(4,),
        out_shape=(
            jax.ShapeDtypeStruct((left_rows, width), bf16),
            jax.ShapeDtypeStruct((2, 4, width, quarter), bf16),
        ),
        in_specs=[
            pl.BlockSpec((quarter, features), lambda q: (q, 0)),
            pl.BlockSpec((1, 1, quarter), lambda q: (q, 0, 0)),
            whole(1, features),
            whole(1, features),
            whole(width, features),
            whole(width, 1),
            whole(width, features),
            whole(width, 1),
        ],
        out_specs=(whole(left_rows, width), pl.BlockSpec((2, 1, width, quarter), lambda q: (0, q, 0, 0))),
        compiler_params=vmem(40),
        name="project",
    )(x, mask.reshape(4, 1, quarter), gain, bias, w_left, b_left, w_right, b_right)


def ring(step):
    return [(i, (i + step) % 4) for i in range(4)]


def gather_ring(block, axis, low, high):
    before = lax.ppermute(block, axis, ring(1))
    after = lax.ppermute(block, axis, ring(-1))
    far_low = lax.ppermute(low(before), axis, ring(1))
    far_high = lax.ppermute(high(after), axis, ring(-1))
    return block, before, after, far_low, far_high


def interleave(first, second):
    columns = first[0].shape[-1]
    chunks = columns // CHUNK
    rows = 16 * 32

    def kernel(*refs):
        ins, outs, scratch = refs[:10], refs[10:12], refs[12]
        for half in range(2):
            own, before, after, low, high = ins[5 * half : 5 * half + 5]
            for place in range(4):
                for m in range(8):
                    if place < 3:
                        part = (own, before, after)[place][m]
                    else:
                        part = low[m] if m < 4 else high[m - 4]
                    part = part.astype(f32)
                    for lane in range(CHUNK // 128):
                        at = pl.ds(place * 8 + m, 16, stride=32)
                        scratch[half, lane, at, :] = part[:, lane * 128 : (lane + 1) * 128]
            for lane in range(CHUNK // 128):
                for eh in range(2):
                    block = scratch[half, lane, eh * 256 : (eh + 1) * 256, :].astype(bf16)
                    outs[half][eh, 0, :, lane * 128 : (lane + 1) * 128] = block

    full = pl.BlockSpec((8, 16, CHUNK), lambda j: (0, 0, j))
    part = pl.BlockSpec((4, 16, CHUNK), lambda j: (0, 0, j))
    out = jax.ShapeDtypeStruct((2, chunks, 256, CHUNK), bf16)
    return pl.pallas_call(
        kernel,
        grid=(chunks,),
        out_shape=(out, out),
        in_specs=[full, full, full, part, part] * 2,
        out_specs=(pl.BlockSpec((2, 1, 256, CHUNK), lambda j: (0, j, 0, 0)),) * 2,
        scratch_shapes=[pltpu.VMEM((2, CHUNK // 128, rows, 128), f32)],
        compiler_params=vmem(40),
        name="interleave",
    )(*first, *second)


def pair(left1, left2, weight, count, first, second):
    chunks = first[0].shape[1]
    out_width = weight.shape[0]

    def kernel(l1, l2, w_ref, n_ref, *refs):
        ins, out_ref, outer = refs[:10], refs[10], refs[11]

        def rows_of(group, _):
            at = pl.ds(pl.multiple_of(group * (GROUP * 32), GROUP * 32), GROUP * 32)
            for e in range(32):
                half, eh, e8 = e // 16, (e // 8) % 2, e % 8
                own, before, after, low, high = ins[5 * half : 5 * half + 5]
                s = slice(e8 * 32, e8 * 32 + 32)
                far = high if eh else low
                right = jnp.concatenate(
                    [own[eh, 0, s, :], before[eh, 0, s, :], after[eh, 0, s, :], far[0, s, :]], axis=0
                )
                prod = jnp.dot((l1, l2)[half][at, :], right, preferred_element_type=f32).astype(bf16)
                for i in range(GROUP):
                    outer[i, e * 32 : (e + 1) * 32, :] = prod[i * 32 : (i + 1) * 32, :]
            scale = 1.0 / (0.001 + n_ref[0, pl.ds(pl.multiple_of(group * GROUP, GROUP), GROUP), :])
            for i in range(GROUP):
                mixed = jnp.dot(w_ref[...], outer[i], preferred_element_type=f32)
                out_ref[group * GROUP + i] = (mixed * scale[i : i + 1, :]).T.astype(bf16)
            return 0

        lax.fori_loop(0, RD // GROUP, rows_of, 0)

    big = pl.BlockSpec((2, 1, 256, CHUNK), lambda j: (0, j, 0, 0))
    part = pl.BlockSpec((1, 256, CHUNK), lambda j: (j, 0, 0))
    return pl.pallas_call(
        kernel,
        grid=(chunks,),
        out_shape=jax.ShapeDtypeStruct((RD, chunks * CHUNK, out_width), bf16),
        in_specs=[
            whole(*left1.shape),
            whole(*left2.shape),
            whole(*weight.shape),
            pl.BlockSpec((1, RD, CHUNK), lambda j: (j, 0, 0)),
        ]
        + [big, big, big, part, part] * 2,
        out_specs=pl.BlockSpec((RD, CHUNK, out_width), lambda j: (0, j, 0)),
        scratch_shapes=[pltpu.VMEM((GROUP, 1024, CHUNK), bf16)],
        compiler_params=vmem(56),
        name="pair",
    )(left1, left2, weight, count, *first, *second)


def sequence_orders():
    x, z = lax.axis_index("x"), lax.axis_index("z")
    k = jnp.arange(128, dtype=jnp.int32)
    offsets = jnp.array(OFFSETS, jnp.int32)
    slow, fast, m = offsets[k // 32], offsets[(k // 8) % 4], k % 8
    first = ((x + fast) % 4) * 32 + ((z + slow) % 4) * 8 + m
    second = ((x + slow) % 4) * 32 + ((z + fast) % 4) * 8 + m
    return first, second


def on_device(x, mask, gain, bias, w_left, b_left, w_right, b_right, w_out):
    columns = x.shape[1] // 4
    width = w_left.shape[1]
    chunks = columns // CHUNK
    plane = lax.axis_index(PLANE)
    narrow = lax.axis_index(("yl", "core"))

    masks = lax.all_gather(mask.astype(bf16), EVERY, axis=0, tiled=True)

    left, right = project(
        x[0], mask, gain[None], bias[None], w_left.T, b_left[:, None], w_right.T, b_right[:, None]
    )
    right = right.reshape(8, width, columns)
    right = lax.all_to_all(right, COLUMN, 0, 0, tiled=True)

    halves = right[:, :16], right[:, 16:]
    lower, upper = (lambda t: t[:4]), (lambda t: t[4:])
    first = gather_ring(halves[0], "x", lower, upper)
    second = gather_ring(halves[1], "z", lower, upper)
    one, two = interleave(first, second)
    lower, upper = (lambda t: t[0]), (lambda t: t[1])
    first = gather_ring(one, "z", lower, upper)
    second = gather_ring(two, "x", lower, upper)

    left = lax.all_to_all(left.reshape(32, RD, width), PLANE, 0, 0, tiled=True)
    left = lax.all_gather(left, ("yl", "core"), axis=1)
    left = left.reshape(128, RD * width)
    order = jnp.concatenate(sequence_orders())
    choose = (jnp.arange(128, dtype=jnp.int32)[:, None] == order[None, :]).astype(bf16)
    left = lax.dot_general(left, choose, (((0,), (0,)), ((), ())), preferred_element_type=f32).astype(bf16)

    row_masks = lax.dynamic_slice_in_dim(masks, plane * RD, RD, 1)
    column_masks = lax.dynamic_slice_in_dim(masks, narrow * columns, columns, 1)
    count = jnp.einsum("si,sj->ij", row_masks, column_masks, preferred_element_type=f32)
    count = count.reshape(RD, chunks, CHUNK).transpose(1, 0, 2)

    weight = w_out.reshape(width, width, -1).transpose(2, 1, 0).reshape(-1, width * width)
    return pair(left[:, :128], left[:, 128:], weight, count, first, second)


def solution(mesh):
    split = Mesh(mesh.devices.reshape(4, 4, 2, 2, 2), EVERY)
    placed = (P(EVERY, None, None), P(EVERY, None)) + (P(),) * 7
    return jax.shard_map(
        on_device,
        mesh=split,
        in_specs=placed,
        out_specs=P(PLANE, ("yl", "core"), None),
        check_vma=False,
    )
```

time: 535 us -> 205 us (0.38)
  matrix products: 156 us -> 0.49 us
  local copies, waits for them, and re-layouts: 153 us -> 35.2 us
  blocking collectives: 135 us -> 27.9 us
  Pallas kernels: 0 us -> 55.7 us
  other arithmetic: 41.3 us -> 0.65 us
  waiting for transfers between devices: 8.49 us -> 40 us
  starting transfers between devices: 19.4 us -> 30.1 us
    dot_general x19 -> x2, matrix products: 156 us -> 0.49 us  [the longest x1 0.32 us: on_device(): lax.dot_general(left, choose, (((0,), (0,)), ((), ())), preferred_element...]
    convert_element_type x10 -> x0, local copies, waits for them, and re-layouts: 111 us -> none  [the longest x8 111 us: pair_block(): outer = jnp.einsum('sic,sje->ijce', left_blk, right_all, preferred_elemen...]
    all_gather x3 -> x1, blocking collectives: 112 us -> 11.7 us  [on_device(): left = lax.all_gather(left, ('yl', 'core'), axis=1)]
    pallas_call x0 -> x3, Pallas kernels: none -> 55.7 us  [the longest x1 40.7 us: pair(): pl.pallas_call(kernel, grid=(chunks,), out_shape=jax.ShapeDtypeStruct((RD...]
    unnamed x2 -> x1, other arithmetic: 31.3 us -> 0.61 us
    ppermute x0 -> x16, starting transfers between devices: none -> 24 us  [the longest x4 10.7 us: gather_ring(): after = lax.ppermute(block, axis, ring(-1))]
    ppermute x0 -> x16, waiting for transfers between devices: none -> 20.1 us  [the longest x4 11.7 us: gather_ring(): far_low = lax.ppermute(low(before), axis, ring(1))]
    while x2 -> x0, local copies, waits for them, and re-layouts: 17.5 us -> none  [on_device(): blocks = lax.map(pair_block, jnp.arange(RD // block, dtype=jnp.int32))]
  transfers between devices with their start and end apart: 4 -> 18, of which waited for: 1 -> 8; matrix products, arithmetic and copies ran while one was open for 1% -> 9% of each run, Pallas kernels for 0% -> 3%
where the time goes in v1:
time: 205 us; the launch traced here: 204 us
  Pallas kernels  55.7 us (27%)
  waiting for transfers between devices  40 us (20%)
  local copies, waits for them, and re-layouts  35.2 us (17%)
  starting transfers between devices  30.1 us (15%)
  blocking collectives  27.9 us (14%)
  between operations  13.6 us (7%)
    pallas_call x1, Pallas kernels, pair(): pl.pallas_call(kernel, grid=(chunks,), out_shape=jax.ShapeDtypeStruct((RD...  40.7 us
    all_to_all x1, waiting for transfers between devices, on_device(): left = lax.all_to_all(left.reshape(32, RD, width), PLANE, 0, 0, tiled=True)  19.9 us
    unnamed x59, local copies, waits for them, and re-layouts  18 us
    all_to_all x1, blocking collectives, on_device(): right = lax.all_to_all(right, COLUMN, 0, 0, tiled=True)  16.1 us
    all_gather x1, blocking collectives, on_device(): left = lax.all_gather(left, ('yl', 'core'), axis=1)  11.7 us
    ppermute x4, waiting for transfers between devices, gather_ring(): far_low = lax.ppermute(low(before), axis, ring(1))  11.7 us
    ppermute x4, starting transfers between devices, gather_ring(): after = lax.ppermute(block, axis, ring(-1))  10.7 us
    ppermute x4, starting transfers between devices, gather_ring(): far_high = lax.ppermute(high(after), axis, ring(-1))  10.1 us
  transfers between devices with their start and end apart: 18, of which 8 were waited for; matrix products, arithmetic and copies ran while one was open for 9% of the time, Pallas kernels for 3%

profile of v1, /device:TPU:0, one launch (start us, length us, event | category | flops | bytes accessed | tf_op | source)
XLA Modules:
  0.0 203.6 jit_solution(6452067027814867563)
XLA Ops:
  8.0 1.7 copy-done
  13.3 9.3 %project.1 = (bf16[1024,32]{1,0:T(8,128)(2,1)S(1)}, bf16[2,4,32,1280]{3,2,1,0:T(8,128)(2,1)S(1)}) custom-call(bf16[5120,256]{1,0:T(8,128)(2,1)S(1)} %bitcast.46, f32[4,1,1280]{2,1,0:T(1,128)S(1)} %bitcast.49, f32[1,256]{1,0:T(1,128)S(1)} %bitcast.52, f32[1,256]{1,0:T(1,128)S(1)} %bitcast.53, bf16[32,256]{1,0:T(8,128)(2,1)S(1)} %bitcast.50, ...), custom_call_target="tpu_custom_call" | custom-call | tf_op jit(solution)/shard_map/project/pallas_call | solution.py:61
  22.5 16.1 %all_to_all.10 = bf16[8,32,1280]{2,1,0:T(8,128)(2,1)S(1)} all-to-all(bf16[8,32,1280]{2,1,0:T(8,128)(2,1)S(1)} %bitcast.47), channel_id=1, replica_groups=mesh['x'=4,'z'=4,'yh'=2,'yl'=2,'core'=2] {'yh','yl','core'}, dimensions={0} | all-to-all | bytes 1310720 | tf_op jit(solution)/shard_map/all_to_all | solution.py:206
  38.7 4.1 %collective-permute-start.5 = (bf16[8,16,1280]{2,1,0:T(8,128)(2,1)S(1)}, bf16[8,16,1280]{2,1,0:T(8,128)(2,1)S(1)}, u32[]{:S(2)}, u32[]{:S(2)}) collective-permute-start(bf16[8,16,1280]{2,1,0:T(8,128)(2,1)S(1)} %get-tuple-element.13.refs_5_), channel_id=1, source_target_pairs={{0,24},{8,0},{16,8},{24,16},{1,25},{9,1},{17,9},{25,17},{2,26},{10... | collective-permute-start | bytes 983048 | tf_op jit(solution)/shard_map/ppermute | solution.py:90
  42.8 2.8 %collective-permute-start.1 = (bf16[8,16,1280]{2,1,0:T(8,128)(2,1)S(1)}, bf16[8,16,1280]{2,1,0:T(8,128)(2,1)S(1)}, u32[]{:S(2)}, u32[]{:S(2)}) collective-permute-start(bf16[8,16,1280]{2,1,0:T(8,128)(2,1)S(1)} %get-tuple-element.14.refs_0_), channel_id=1, source_target_pairs={{0,96},{32,0},{64,32},{96,64},{1,97},{33,1},{65,33},{97,65},{2,98}... | collective-permute-start | bytes 983048 | tf_op jit(solution)/shard_map/ppermute | solution.py:90
  45.6 4.0 %collective-permute-done.5.refs_7_ = bf16[8,16,1280]{2,1,0:T(8,128)(2,1)S(1)} collective-permute-done((bf16[8,16,1280]{2,1,0:T(8,128)(2,1)S(1)}, bf16[8,16,1280]{2,1,0:T(8,128)(2,1)S(1)}, u32[]{:S(2)}, u32[]{:S(2)}) %collective-permute-start.5) | collective-permute-done | bytes 327712 | tf_op jit(solution)/shard_map/ppermute | solution.py:90
  49.6 3.8 %collective-permute-start.7 = (bf16[4,16,1280]{2,1,0:T(8,128)(2,1)S(1)}, bf16[4,16,1280]{2,1,0:T(8,128)(2,1)S(1)}, u32[]{:S(2)}, u32[]{:S(2)}) collective-permute-start(bf16[4,16,1280]{2,1,0:T(8,128)(2,1)S(1)} %slice.65), channel_id=1, source_target_pairs={{0,24},{8,0},{16,8},{24,16},{1,25},{9,1},{17,9},{25,17},{2,26},{10... | collective-permute-start | bytes 491528 | tf_op jit(solution)/shard_map/ppermute | solution.py:92
  53.5 2.8 %collective-permute-start.3 = (bf16[4,16,1280]{2,1,0:T(8,128)(2,1)S(1)}, bf16[4,16,1280]{2,1,0:T(8,128)(2,1)S(1)}, u32[]{:S(2)}, u32[]{:S(2)}) collective-permute-start(bf16[4,16,1280]{2,1,0:T(8,128)(2,1)S(1)} %slice.62), channel_id=1, source_target_pairs={{0,96},{32,0},{64,32},{96,64},{1,97},{33,1},{65,33},{97,65},{2,98}... | collective-permute-start | bytes 491528 | tf_op jit(solution)/shard_map/ppermute | solution.py:92
  58.4 1.6 collective-permute-done.6.refs_8_
  61.3 1.6 collective-permute-done.2.refs_3_
  66.6 1.0 copy-done.10
  71.2 5.7 %interleave.1 = (bf16[2,5,256,256]{3,2,1,0:T(8,128)(2,1)S(1)}, bf16[2,5,256,256]{3,2,1,0:T(8,128)(2,1)S(1)}) custom-call(bf16[8,16,1280]{2,1,0:T(8,128)(2,1)S(1)} %get-tuple-element.14.refs_0_, bf16[8,16,1280]{2,1,0:T(8,128)(2,1)S(1)} %copy-done.10, bf16[8,16,1280]{2,1,0:T(8,128)(2,1)S(1)} %copy-done.8, bf16[4,16,1280]{2,1,0:T(8,128)(2,1)S(1)} %copy-done.18, ...), custom_call_target="tpu_custom_call" | custom-call | tf_op jit(solution)/shard_map/interleave/pallas_call | solution.py:123
  77.0 3.3 %collective-permute-start.9 = (bf16[2,5,256,256]{3,2,1,0:T(8,128)(2,1)S(1)}, bf16[2,5,256,256]{3,2,1,0:T(8,128)(2,1)}, u32[]{:S(2)}, u32[]{:S(2)}) collective-permute-start(bf16[2,5,256,256]{3,2,1,0:T(8,128)(2,1)S(1)} %get-tuple-element.11.refs_0_), channel_id=1, source_target_pairs={{0,24},{8,0},{16,8},{24,16},{1,25},{9,1},{17,9},{25,17},{2,26},{10... | collective-permute-start | bytes 3932168 | tf_op jit(solution)/shard_map/ppermute | solution.py:90
  81.7 6.1 %all-to-all-start = ((bf16[32,2,512]{2,1,0:T(2,128)(2,1)}), bf16[32,2,512]{2,1,0:T(2,128)(2,1)S(1)}, u32[]{:S(2)}, u32[]{:S(2)}) async-start(bf16[32,2,512]{2,1,0:T(2,128)(2,1)} %reshape.205), calls=%async_computation | async-start | bytes 131072 | tf_op jit(solution)/shard_map/all_to_all | solution.py:217
  87.8 1.1 copy.27
  89.7 1.8 collective-permute-start.12
  91.6 19.9 %all-to-all-done = bf16[32,2,512]{2,1,0:T(2,128)(2,1)S(1)} async-done(((bf16[32,2,512]{2,1,0:T(2,128)(2,1)}), bf16[32,2,512]{2,1,0:T(2,128)(2,1)S(1)}, u32[]{:S(2)}, u32[]{:S(2)}) %all-to-all-start) | async-done | bytes 65568 | tf_op jit(solution)/shard_map/all_to_all | solution.py:217
  111.7 11.7 %all-gather = bf16[32,128,32]{2,1,0:T(8,128)(2,1)} all-gather(bf16[32,32,32]{2,1,0:T(8,128)(2,1)S(1)} %reshape.206), channel_id=2, replica_groups=mesh['x'=4,'z'=4,'yh'=2,'yl'=2,'core'=2] {'yl','core'}, dimensions={1}, use_global_device_ids=true | all-gather | bytes 327680 | tf_op jit(solution)/shard_map/all_gather | solution.py:218
  123.4 2.3 %reshape.134 = bf16[128,1024]{1,0:T(8,128)(2,1)S(1)} reshape(bf16[32,128,32]{2,1,0:T(8,128)(2,1)} %all-gather) | data formatting | bytes 524288 | tf_op jit(solution)/shard_map/reshape | solution.py:219
  126.1 2.0 slice_bitcast_fusion.2
  128.1 1.1 collective-permute-start.11
  129.2 2.0 slice_bitcast_fusion.3
  132.1 2.0 slice_bitcast_fusion
  134.1 2.4 %collective-permute-start.15 = (bf16[5,256,256]{2,1,0:T(8,128)(2,1)}, bf16[5,256,256]{2,1,0:T(8,128)(2,1)S(1)}, u32[]{:S(2)}, u32[]{:S(2)}) collective-permute-start(bf16[5,256,256]{2,1,0:T(8,128)(2,1)} %slice_bitcast_fusion), channel_id=1, source_target_pairs={{0,96},{32,0},{64,32},{96,64},{1,97},{33,1},{65,33},{97,65},{2,98}... | collective-permute-start | bytes 1966088 | tf_op jit(solution)/shard_map/ppermute | solution.py:92
  136.5 1.1 slice_bitcast_fusion.1
  138.8 1.0 constant_dynamic-slice_fusion.1
  139.8 1.8 constant_dynamic-slice_fusion
  142.5 2.9 %collective-permute-done.11.refs_4_ = bf16[5,256,256]{2,1,0:T(8,128)(2,1)S(1)} collective-permute-done((bf16[5,256,256]{2,1,0:T(8,128)(2,1)}, bf16[5,256,256]{2,1,0:T(8,128)(2,1)S(1)}, u32[]{:S(2)}, u32[]{:S(2)}) %collective-permute-start.11) | collective-permute-done | bytes 655392 | tf_op jit(solution)/shard_map/ppermute | solution.py:92
  145.3 4.0 %collective-permute-done.10.refs_3_ = bf16[5,256,256]{2,1,0:T(8,128)(2,1)S(1)} collective-permute-done((bf16[5,256,256]{2,1,0:T(8,128)(2,1)}, bf16[5,256,256]{2,1,0:T(8,128)(2,1)S(1)}, u32[]{:S(2)}, u32[]{:S(2)}) %collective-permute-start.10) | collective-permute-done | bytes 655392 | tf_op jit(solution)/shard_map/ppermute | solution.py:91
  149.3 1.5 collective-permute-done.15.refs_9_
  150.8 4.5 %collective-permute-done.14.refs_8_ = bf16[5,256,256]{2,1,0:T(8,128)(2,1)S(1)} collective-permute-done((bf16[5,256,256]{2,1,0:T(8,128)(2,1)S(1)}, bf16[5,256,256]{2,1,0:T(8,128)(2,1)S(1)}, u32[]{:S(2)}, u32[]{:S(2)}) %collective-permute-start.14) | collective-permute-done | bytes 655392 | tf_op jit(solution)/shard_map/ppermute | solution.py:91
  156.1 40.7 %pair.1 = bf16[32,1280,128]{2,1,0:T(8,128)(2,1)} custom-call(bf16[1024,128]{1,0:T(8,128)(2,1)} %get-tuple-element.16.l1, bf16[1024,128]{1,0:T(8,128)(2,1)} %get-tuple-element.15.l2, bf16[128,1024]{1,0:T(8,128)(2,1)} %copy.31.w_ref, f32[5,32,256]{2,1,0:T(8,128)} %bitcast.55, bf16[2,5,256,256]{3,2,1,0:T(8,128)(2,1)} %copy-done.1, ...), custom_call_target="tpu_custom_call" | custom-call | tf_op jit(solution)/shard_map/pair/pallas_call | solution.py:165
  (92 shorter events, 22.4 us)
Async XLA Ops:
  6.5 132.2 %all-gather.4.cloned.1.call-start = ((), (), s32[]{:S(2)}) async-start(), calls=%async_computation.2 | async-start | bytes 2641920 | tf_op jit(solution)/shard_map/all_gather | solution.py:200
  8.0 1.7 copy-start
  38.7 10.9 %collective-permute-start.5 = (bf16[8,16,1280]{2,1,0:T(8,128)(2,1)S(1)}, bf16[8,16,1280]{2,1,0:T(8,128)(2,1)S(1)}, u32[]{:S(2)}, u32[]{:S(2)}) collective-permute-start(bf16[8,16,1280]{2,1,0:T(8,128)(2,1)S(1)} %get-tuple-element.13.refs_5_), channel_id=1, source_target_pairs={{0,24},{8,0},{16,8},{24,16},{1,25},{9,1},{17,9},{25,17},{2,26},{10... | collective-permute-start | bytes 983048 | tf_op jit(solution)/shard_map/ppermute | solution.py:90
  42.8 10.6 %collective-permute-start.4 = (bf16[8,16,1280]{2,1,0:T(8,128)(2,1)S(1)}, bf16[8,16,1280]{2,1,0:T(8,128)(2,1)S(1)}, u32[]{:S(2)}, u32[]{:S(2)}) collective-permute-start(bf16[8,16,1280]{2,1,0:T(8,128)(2,1)S(1)} %get-tuple-element.13.refs_5_), channel_id=1, source_target_pairs={{0,8},{8,16},{16,24},{24,0},{1,9},{9,17},{17,25},{25,1},{2,10},{10... | collective-permute-start | bytes 983048 | tf_op jit(solution)/shard_map/ppermute | solution.py:89
  42.8 10.7 %collective-permute-start.1 = (bf16[8,16,1280]{2,1,0:T(8,128)(2,1)S(1)}, bf16[8,16,1280]{2,1,0:T(8,128)(2,1)S(1)}, u32[]{:S(2)}, u32[]{:S(2)}) collective-permute-start(bf16[8,16,1280]{2,1,0:T(8,128)(2,1)S(1)} %get-tuple-element.14.refs_0_), channel_id=1, source_target_pairs={{0,96},{32,0},{64,32},{96,64},{1,97},{33,1},{65,33},{97,65},{2,98}... | collective-permute-start | bytes 983048 | tf_op jit(solution)/shard_map/ppermute | solution.py:90
  45.6 10.8 %collective-permute-start = (bf16[8,16,1280]{2,1,0:T(8,128)(2,1)S(1)}, bf16[8,16,1280]{2,1,0:T(8,128)(2,1)S(1)}, u32[]{:S(2)}, u32[]{:S(2)}) collective-permute-start(bf16[8,16,1280]{2,1,0:T(8,128)(2,1)S(1)} %get-tuple-element.14.refs_0_), channel_id=1, source_target_pairs={{0,32},{32,64},{64,96},{96,0},{1,33},{33,65},{65,97},{97,1},{2,34}... | collective-permute-start | bytes 983048 | tf_op jit(solution)/shard_map/ppermute | solution.py:89
  49.6 6.8 %copy-start.3 = (bf16[8,16,1280]{2,1,0:T(8,128)(2,1)}, bf16[8,16,1280]{2,1,0:T(8,128)(2,1)S(1)}, u32[]{:S(2)}) copy-start(bf16[8,16,1280]{2,1,0:T(8,128)(2,1)S(1)} %collective-permute-done.5.refs_7_) | copy-start | bytes 983044
  49.6 8.1 %collective-permute-start.7 = (bf16[4,16,1280]{2,1,0:T(8,128)(2,1)S(1)}, bf16[4,16,1280]{2,1,0:T(8,128)(2,1)S(1)}, u32[]{:S(2)}, u32[]{:S(2)}) collective-permute-start(bf16[4,16,1280]{2,1,0:T(8,128)(2,1)S(1)} %slice.65), channel_id=1, source_target_pairs={{0,24},{8,0},{16,8},{24,16},{1,25},{9,1},{17,9},{25,17},{2,26},{10... | collective-permute-start | bytes 491528 | tf_op jit(solution)/shard_map/ppermute | solution.py:92
  53.4 3.0 %copy-start.5 = (bf16[8,16,1280]{2,1,0:T(8,128)(2,1)}, bf16[8,16,1280]{2,1,0:T(8,128)(2,1)S(1)}, u32[]{:S(2)}) copy-start(bf16[8,16,1280]{2,1,0:T(8,128)(2,1)S(1)} %collective-permute-done.4.refs_6_) | copy-start | bytes 983044
  53.4 6.6 %collective-permute-start.6 = (bf16[4,16,1280]{2,1,0:T(8,128)(2,1)S(1)}, bf16[4,16,1280]{2,1,0:T(8,128)(2,1)S(1)}, u32[]{:S(2)}, u32[]{:S(2)}) collective-permute-start(bf16[4,16,1280]{2,1,0:T(8,128)(2,1)S(1)} %slice.64), channel_id=1, source_target_pairs={{0,8},{8,16},{16,24},{24,0},{1,9},{9,17},{17,25},{25,1},{2,10},{10... | collective-permute-start | bytes 491528 | tf_op jit(solution)/shard_map/ppermute | solution.py:91
  53.5 3.0 %copy-start.7 = (bf16[8,16,1280]{2,1,0:T(8,128)(2,1)}, bf16[8,16,1280]{2,1,0:T(8,128)(2,1)S(1)}, u32[]{:S(2)}) copy-start(bf16[8,16,1280]{2,1,0:T(8,128)(2,1)S(1)} %collective-permute-done.1.refs_2_) | copy-start | bytes 983044
  53.5 7.1 %collective-permute-start.3 = (bf16[4,16,1280]{2,1,0:T(8,128)(2,1)S(1)}, bf16[4,16,1280]{2,1,0:T(8,128)(2,1)S(1)}, u32[]{:S(2)}, u32[]{:S(2)}) collective-permute-start(bf16[4,16,1280]{2,1,0:T(8,128)(2,1)S(1)} %slice.62), channel_id=1, source_target_pairs={{0,96},{32,0},{64,32},{96,64},{1,97},{33,1},{65,33},{97,65},{2,98}... | collective-permute-start | bytes 491528 | tf_op jit(solution)/shard_map/ppermute | solution.py:92
  56.4 6.6 %collective-permute-start.2 = (bf16[4,16,1280]{2,1,0:T(8,128)(2,1)S(1)}, bf16[4,16,1280]{2,1,0:T(8,128)(2,1)S(1)}, u32[]{:S(2)}, u32[]{:S(2)}) collective-permute-start(bf16[4,16,1280]{2,1,0:T(8,128)(2,1)S(1)} %slice.61), channel_id=1, source_target_pairs={{0,32},{32,64},{64,96},{96,0},{1,33},{33,65},{65,97},{97,1},{2,34}... | collective-permute-start | bytes 491528 | tf_op jit(solution)/shard_map/ppermute | solution.py:91
  63.7 1.0 copy-start.4
  64.6 1.0 copy-start.6
  65.6 1.0 copy-start.8
  66.6 1.0 copy-start.10
  67.5 0.9 copy-start.12
  77.0 46.4 %copy-start.1 = (bf16[2,5,256,256]{3,2,1,0:T(8,128)(2,1)}, bf16[2,5,256,256]{3,2,1,0:T(8,128)(2,1)S(1)}, u32[]{:S(2)}) copy-start(bf16[2,5,256,256]{3,2,1,0:T(8,128)(2,1)S(1)} %get-tuple-element.11.refs_0_) | copy-start | bytes 3932164
  77.0 46.4 %copy-start.2 = (bf16[2,5,256,256]{3,2,1,0:T(8,128)(2,1)}, bf16[2,5,256,256]{3,2,1,0:T(8,128)(2,1)S(1)}, u32[]{:S(2)}) copy-start(bf16[2,5,256,256]{3,2,1,0:T(8,128)(2,1)S(1)} %get-tuple-element.12.refs_5_) | copy-start | bytes 3932164
  77.0 49.1 %collective-permute-start.9 = (bf16[2,5,256,256]{3,2,1,0:T(8,128)(2,1)S(1)}, bf16[2,5,256,256]{3,2,1,0:T(8,128)(2,1)}, u32[]{:S(2)}, u32[]{:S(2)}) collective-permute-start(bf16[2,5,256,256]{3,2,1,0:T(8,128)(2,1)S(1)} %get-tuple-element.11.refs_0_), channel_id=1, source_target_pairs={{0,24},{8,0},{16,8},{24,16},{1,25},{9,1},{17,9},{25,17},{2,26},{10... | collective-permute-start | bytes 3932168 | tf_op jit(solution)/shard_map/ppermute | solution.py:90
  80.3 49.0 %collective-permute-start.8 = (bf16[2,5,256,256]{3,2,1,0:T(8,128)(2,1)S(1)}, bf16[2,5,256,256]{3,2,1,0:T(8,128)(2,1)}, u32[]{:S(2)}, u32[]{:S(2)}) collective-permute-start(bf16[2,5,256,256]{3,2,1,0:T(8,128)(2,1)S(1)} %get-tuple-element.11.refs_0_), channel_id=1, source_target_pairs={{0,8},{8,16},{16,24},{24,0},{1,9},{9,17},{17,25},{25,1},{2,10},{10... | collective-permute-start | bytes 3932168 | tf_op jit(solution)/shard_map/ppermute | solution.py:89
  80.3 51.9 %collective-permute-start.13 = (bf16[2,5,256,256]{3,2,1,0:T(8,128)(2,1)S(1)}, bf16[2,5,256,256]{3,2,1,0:T(8,128)(2,1)}, u32[]{:S(2)}, u32[]{:S(2)}) collective-permute-start(bf16[2,5,256,256]{3,2,1,0:T(8,128)(2,1)S(1)} %get-tuple-element.12.refs_5_), channel_id=1, source_target_pairs={{0,96},{32,0},{64,32},{96,64},{1,97},{33,1},{65,33},{97,65},{2,98}... | collective-permute-start | bytes 3932168 | tf_op jit(solution)/shard_map/ppermute | solution.py:90
  81.7 29.8 %all-to-all-start = ((bf16[32,2,512]{2,1,0:T(2,128)(2,1)}), bf16[32,2,512]{2,1,0:T(2,128)(2,1)S(1)}, u32[]{:S(2)}, u32[]{:S(2)}) async-start(bf16[32,2,512]{2,1,0:T(2,128)(2,1)} %reshape.205), calls=%async_computation | async-start | bytes 131072 | tf_op jit(solution)/shard_map/all_to_all | solution.py:217
  89.7 46.8 %collective-permute-start.12 = (bf16[2,5,256,256]{3,2,1,0:T(8,128)(2,1)S(1)}, bf16[2,5,256,256]{3,2,1,0:T(8,128)(2,1)}, u32[]{:S(2)}, u32[]{:S(2)}) collective-permute-start(bf16[2,5,256,256]{3,2,1,0:T(8,128)(2,1)S(1)} %get-tuple-element.12.refs_5_), channel_id=1, source_target_pairs={{0,32},{32,64},{64,96},{96,0},{1,33},{33,65},{65,97},{97,1},{2,34}... | collective-permute-start | bytes 3932168 | tf_op jit(solution)/shard_map/ppermute | solution.py:89
  128.1 17.2 %collective-permute-start.11 = (bf16[5,256,256]{2,1,0:T(8,128)(2,1)}, bf16[5,256,256]{2,1,0:T(8,128)(2,1)S(1)}, u32[]{:S(2)}, u32[]{:S(2)}) collective-permute-start(bf16[5,256,256]{2,1,0:T(8,128)(2,1)} %slice_bitcast_fusion.2), channel_id=1, source_target_pairs={{0,24},{8,0},{16,8},{24,16},{1,25},{9,1},{17,9},{25,17},{2,26},{10... | collective-permute-start | bytes 1966088 | tf_op jit(solution)/shard_map/ppermute | solution.py:92
  131.2 18.1 %collective-permute-start.10 = (bf16[5,256,256]{2,1,0:T(8,128)(2,1)}, bf16[5,256,256]{2,1,0:T(8,128)(2,1)S(1)}, u32[]{:S(2)}, u32[]{:S(2)}) collective-permute-start(bf16[5,256,256]{2,1,0:T(8,128)(2,1)} %slice_bitcast_fusion.3), channel_id=1, source_target_pairs={{0,8},{8,16},{16,24},{24,0},{1,9},{9,17},{17,25},{25,1},{2,10},{10... | collective-permute-start | bytes 1966088 | tf_op jit(solution)/shard_map/ppermute | solution.py:91
  134.1 16.7 %collective-permute-start.15 = (bf16[5,256,256]{2,1,0:T(8,128)(2,1)}, bf16[5,256,256]{2,1,0:T(8,128)(2,1)S(1)}, u32[]{:S(2)}, u32[]{:S(2)}) collective-permute-start(bf16[5,256,256]{2,1,0:T(8,128)(2,1)} %slice_bitcast_fusion), channel_id=1, source_target_pairs={{0,96},{32,0},{64,32},{96,64},{1,97},{33,1},{65,33},{97,65},{2,98}... | collective-permute-start | bytes 1966088 | tf_op jit(solution)/shard_map/ppermute | solution.py:92
  137.7 17.6 %collective-permute-start.14 = (bf16[5,256,256]{2,1,0:T(8,128)(2,1)S(1)}, bf16[5,256,256]{2,1,0:T(8,128)(2,1)S(1)}, u32[]{:S(2)}, u32[]{:S(2)}) collective-permute-start(bf16[5,256,256]{2,1,0:T(8,128)(2,1)S(1)} %slice_bitcast_fusion.1), channel_id=1, source_target_pairs={{0,32},{32,64},{64,96},{96,0},{1,33},{33,65},{65,97},{97,1},{2,34}... | collective-permute-start | bytes 1966088 | tf_op jit(solution)/shard_map/ppermute | solution.py:91
  145.3 10.0 %copy-start.24 = (bf16[5,256,256]{2,1,0:T(8,128)(2,1)}, bf16[5,256,256]{2,1,0:T(8,128)(2,1)S(1)}, u32[]{:S(2)}) copy-start(bf16[5,256,256]{2,1,0:T(8,128)(2,1)S(1)} %collective-permute-done.11.refs_4_) | copy-start | bytes 1966084
  149.3 6.0 %copy-start.25 = (bf16[5,256,256]{2,1,0:T(8,128)(2,1)}, bf16[5,256,256]{2,1,0:T(8,128)(2,1)S(1)}, u32[]{:S(2)}) copy-start(bf16[5,256,256]{2,1,0:T(8,128)(2,1)S(1)} %collective-permute-done.10.refs_3_) | copy-start | bytes 1966084
  150.8 4.5 %copy-start.26 = (bf16[5,256,256]{2,1,0:T(8,128)(2,1)}, bf16[5,256,256]{2,1,0:T(8,128)(2,1)S(1)}, u32[]{:S(2)}) copy-start(bf16[5,256,256]{2,1,0:T(8,128)(2,1)S(1)} %collective-permute-done.15.refs_9_) | copy-start | bytes 1966084
  (14 other events, 10.5 us)
Sparse Core Ops, SparseCore 0:
  57.8 65.9 all-gather.3

commit v2 on v1

v2 whole, which is shorter than its diff:
```python
import jax
import jax.numpy as jnp
from jax import lax
from jax.experimental import pallas as pl
from jax.experimental.pallas import tpu as pltpu
from jax.sharding import Mesh
from jax.sharding import PartitionSpec as P

RD = 32
CHUNK = 256
GROUP = 8
TILE = 128
COLUMN = ("yh", "yl", "core")
PLANE = ("x", "z", "yh")
EVERY = ("x", "z", "yh", "yl", "core")
f32 = jnp.float32
bf16 = jnp.bfloat16


def vmem(mib=60):
    return pltpu.CompilerParams(vmem_limit_bytes=mib * 2**20)


def whole(*shape):
    return pl.BlockSpec(shape, lambda *_: (0,) * len(shape))


def turned(bias_ref):
    return jnp.broadcast_to(bias_ref[...], (8, bias_ref.shape[1])).T[:, :1]


def standardize(v, gain, bias):
    v = v.astype(f32)
    v = v - jnp.mean(v, axis=-1, keepdims=True)
    spread = jnp.mean(v * v, axis=-1, keepdims=True)
    return (v * lax.rsqrt(spread + 1e-05) * gain + bias).astype(bf16)


def affine(w_ref, bias, normed, mask):
    y = lax.dot_general(w_ref[...], normed, (((1,), (1,)), ((), ())), preferred_element_type=f32)
    return (y + bias) * mask


def project_left(x, mask, gain, bias, weight, shift):
    features = x.shape[1]
    width = weight.shape[0]
    rows = RD * 32
    half = width // 2
    sub = 512

    def kernel(x_ref, m_ref, g_ref, s_ref, w_ref, b_ref, out_ref, mask_ref):
        b = turned(b_ref)
        y = []
        for part in range(rows // sub):
            at = slice(part * sub, (part + 1) * sub)
            normed = standardize(x_ref[at, :], g_ref[...], s_ref[...])
            y.append(affine(w_ref, b, normed, m_ref[:, at]))
        y = jnp.concatenate(y, axis=1)

        def piece(v, px, pz, yh):
            first = (px * 8 + pz * 2 + yh) * RD
            return v[:, first : first + RD]

        for yh in range(2):
            masks = []
            for slow in range(4):
                at = slice(slow * TILE, (slow + 1) * TILE)
                one = [piece(y[:half], slow, fast, yh) for fast in range(4)]
                two = [piece(y[half:], fast, slow, yh) for fast in range(4)]
                out_ref[yh, :half, at] = jnp.concatenate(one, axis=1).astype(bf16)
                out_ref[yh, half:, at] = jnp.concatenate(two, axis=1).astype(bf16)
                masks.append(jnp.concatenate([piece(m_ref[...], slow, fast, yh) for fast in range(4)], axis=1))
            masks = jnp.concatenate(masks + [jnp.zeros((4, TILE), f32)], axis=0)
            mask_ref[yh] = masks

    return pl.pallas_call(
        kernel,
        grid=(1,),
        out_shape=(
            jax.ShapeDtypeStruct((2, width, 4 * TILE), bf16),
            jax.ShapeDtypeStruct((2, 8, TILE), f32),
        ),
        in_specs=[
            pl.BlockSpec((rows, features), lambda _: (0, 0)),
            pl.BlockSpec((1, rows), lambda _: (0, 0)),
            whole(1, features),
            whole(1, features),
            whole(width, features),
            whole(1, width),
        ],
        out_specs=(whole(2, width, 4 * TILE), whole(2, 8, TILE)),
        compiler_params=vmem(),
        name="project_left",
    )(x, mask, gain, bias, weight, shift)


def project_right(x, mask, gain, bias, weight, shift, left, left_mask):
    rows, features = x.shape
    quarter = rows // 4
    width = weight.shape[0]
    sub = 640
    total = quarter + 5 * TILE

    def kernel(x_ref, m_ref, g_ref, s_ref, w_ref, b_ref, l_ref, n_ref, out_ref):
        b = turned(b_ref)
        for part in range(quarter // sub):
            at = slice(part * sub, (part + 1) * sub)
            normed = standardize(x_ref[at, :], g_ref[...], s_ref[...])
            y = affine(w_ref, b, normed, m_ref[0, :, at]).astype(bf16)
            out_ref[0, 0, :, at] = y
            out_ref[1, 0, :, at] = y
        m = [m_ref[0, :, k * TILE : (k + 1) * TILE] for k in range(quarter // TILE)]
        zeros = jnp.zeros((width - len(m) - 4, TILE), f32)
        for yh in range(2):
            tile = jnp.concatenate(m + [n_ref[yh, :4, :], zeros], axis=0)
            out_ref[yh, 0, :, quarter : quarter + TILE] = tile.astype(bf16)
            out_ref[yh, 0, :, quarter + TILE :] = l_ref[yh]

    return pl.pallas_call(
        kernel,
        grid=(4,),
        out_shape=jax.ShapeDtypeStruct((2, 4, width, total), bf16),
        in_specs=[
            pl.BlockSpec((quarter, features), lambda q: (q, 0)),
            pl.BlockSpec((1, 1, quarter), lambda q: (q, 0, 0)),
            whole(1, features),
            whole(1, features),
            whole(width, features),
            whole(1, width),
            whole(*left.shape),
            whole(*left_mask.shape),
        ],
        out_specs=pl.BlockSpec((2, 1, width, total), lambda q: (0, q, 0, 0)),
        compiler_params=vmem(),
        name="project_right",
    )(x, mask.reshape(4, 1, quarter), gain, bias, weight, shift, left, left_mask)


def ring(step):
    return [(i, (i + step) % 4) for i in range(4)]


def interleave(position, first, second, columns, start, chunks, with_left):
    tiles = CHUNK // TILE
    mask_tile = columns // TILE
    sizes = (8, 8, 8, 4, 4)
    heights = (544, 512)
    extra = (272, 256) if with_left else (0, 0)

    def place_rows(ins, put):
        own, before, after, low, high = ins
        for place in range(4):
            for m in range(8):
                if place < 3:
                    part = (own, before, after)[place][m]
                else:
                    part = low[m] if m < 4 else high[m - 4]
                put(pl.ds(place * 8 + m, 16, stride=32), part.astype(f32))

    def kernel(pos, *refs):
        main, masks, lefts = refs[:10], refs[10:15], refs[15:-4]
        outs, (scratch, mask_rows) = refs[-4:-2], refs[-2:]

        def put_mask(at, part):
            mask_rows[at, :] = part

        place_rows(masks, put_mask)

        def masks_at(row):
            return mask_rows[pl.ds(pl.multiple_of(row * 32, 32), 32), :].astype(bf16)

        for chunk in range(chunks):
            for half in range(2):
                base = chunk * heights[half]

                def put(at, part):
                    for lane in range(tiles):
                        scratch[chunk, half, lane, at, :] = part[:, lane * TILE : (lane + 1) * TILE]

                ins = [r.at[:, :, chunk * CHUNK : (chunk + 1) * CHUNK] for r in main[5 * half : 5 * half + 5]]
                place_rows(ins, put)
                for lane in range(tiles):
                    at = slice(lane * TILE, (lane + 1) * TILE)
                    outs[half][base : base + 512, at] = scratch[chunk, half, lane].astype(bf16)
                    if half == 0:
                        outs[0][base + 512 : base + 544, at] = masks_at((start + chunk) * tiles + lane)
        if with_left:
            for half in range(2):
                base = chunks * heights[half]

                def put_left(at, part):
                    scratch[chunks, half, 0, at, :] = part

                place_rows(lefts[5 * half : 5 * half + 5], put_left)
                for lane in range(2):
                    at = slice(lane * TILE, (lane + 1) * TILE)
                    rows = scratch[chunks, half, 0, lane * 256 : (lane + 1) * 256, :]
                    outs[half][base : base + 256, at] = rows.astype(bf16)
            rows = masks_at(mask_tile + pos[0])
            base = chunks * heights[0] + 256
            outs[0][base : base + 16, :TILE] = rows[:16]
            outs[0][base : base + 16, TILE:] = rows[16:]

    def blocks(m):
        span = chunks * CHUNK
        if start * CHUNK % span == 0:
            return pl.BlockSpec((m, 16, span), lambda _, pos: (0, 0, start * CHUNK // span))
        return pl.BlockSpec((pl.Element(m), pl.Element(16), pl.Element(span)), lambda _, pos: (0, 0, start * CHUNK))

    def mask_blocks(m):
        return pl.BlockSpec((m, 16, TILE), lambda _, pos: (0, 0, mask_tile))

    def left_blocks(m, half):
        return pl.BlockSpec((m, 16, TILE), lambda _, pos: (0, 0, mask_tile + 1 + pos[half]))

    specs = [blocks(m) for m in sizes] * 2 + [mask_blocks(m) for m in sizes]
    args = (*first, *second, *first)
    if with_left:
        specs += [left_blocks(m, half) for half in range(2) for m in sizes]
        args += (*first, *second)
    shapes = [(chunks * heights[half] + extra[half], CHUNK) for half in range(2)]
    return pl.pallas_call(
        kernel,
        grid_spec=pltpu.PrefetchScalarGridSpec(
            num_scalar_prefetch=1,
            grid=(1,),
            in_specs=specs,
            out_specs=tuple(whole(*shape) for shape in shapes),
            scratch_shapes=[
                pltpu.VMEM((chunks + with_left, 2, tiles, 512, TILE), f32),
                pltpu.VMEM((512, TILE), f32),
            ],
        ),
        out_shape=tuple(jax.ShapeDtypeStruct(shape, bf16) for shape in shapes),
        compiler_params=vmem(),
        name="interleave",
    )(position, *args)


def arrange_left(position, first, second, chunks):
    def kernel(pos, *refs):
        ins, (one_ref, two_ref, mask_ref, scratch) = refs[:10], refs[10:]

        def sequences(half, rows, lane):
            at = slice(lane * TILE, (lane + 1) * TILE)
            own, before, after, low, high = ins[5 * half : 5 * half + 5]
            return [r[rows, at] for r in (own, before, after)] + [(low, high)[lane][rows, :]]

        def mine(half, values):
            wanted = lax.broadcasted_iota(jnp.int32, (RD, TILE), 0) + RD * pos[1 - half]
            pick = (lax.broadcasted_iota(jnp.int32, (RD, TILE), 1) == wanted).astype(bf16)
            return lax.dot_general(pick, values, (((1,), (1,)), ((), ())), preferred_element_type=f32)

        for half in range(2):
            for c in range(16):
                lane, row = divmod(c, 8)
                values = sequences(half, slice(row * 32, row * 32 + 32), lane)
                values = mine(half, jnp.concatenate(values, axis=0))
                scratch[pl.ds(half * 16 + c, RD, stride=32), :] = values
        masks = [sequences(0, slice(256, 272), lane) for lane in range(2)]
        masks = [masks[lane][place] for place in range(4) for lane in range(2)]
        mask_ref[...] = mine(0, jnp.concatenate(masks, axis=0)).astype(bf16)

        held = scratch[...].astype(bf16)
        k = lax.broadcasted_iota(jnp.int32, (128, 128), 0)
        swapped = (k // 8 % 4) * 32 + k // 32 * 8 + k % 8
        swap = (lax.broadcasted_iota(jnp.int32, (128, 128), 1) == swapped).astype(bf16)
        other = jnp.dot(held, swap, preferred_element_type=f32)
        own_order = lax.broadcasted_iota(jnp.int32, (RD * 32, 128), 0) % 32 < 16
        one_ref[...] = jnp.where(own_order, scratch[...], other).astype(bf16)
        two_ref[...] = jnp.where(own_order, other, scratch[...]).astype(bf16)

    def block(half, t):
        rows = (272, 256)[half]
        return pl.BlockSpec((rows, t.shape[1]), lambda _, pos: (2 * chunks, 0))

    shapes = [(RD * 32, 128), (RD * 32, 128), (RD, 128)]
    return pl.pallas_call(
        kernel,
        grid_spec=pltpu.PrefetchScalarGridSpec(
            num_scalar_prefetch=1,
            grid=(1,),
            in_specs=[block(0, t) for t in first] + [block(1, t) for t in second],
            out_specs=tuple(whole(*shape) for shape in shapes),
            scratch_shapes=[pltpu.VMEM((RD * 32, 128), f32)],
        ),
        out_shape=tuple(jax.ShapeDtypeStruct(shape, bf16) for shape in shapes),
        compiler_params=vmem(),
        name="arrange_left",
    )(position, *first, *second)


def pair(left1, left2, weight, row_mask, first, second, base, start, chunks, result, columns):
    out_width = weight.shape[0]
    skip = start - base
    earlier = () if result is None else (result,)

    def kernel(l1, l2, w_ref, n_ref, *refs):
        ins, (out_ref, outer, scale) = refs[:10], refs[-3:]

        def sequences(half, row):
            own, before, after, low, high = ins[5 * half : 5 * half + 5]
            at = slice(row * 32, row * 32 + 32)
            far = jnp.concatenate([low[at, :], high[at, :]], axis=1)
            return jnp.concatenate([own[at, :], before[at, :], after[at, :], far], axis=0)

        count = jnp.dot(n_ref[...], sequences(0, 16), preferred_element_type=f32)
        scale[...] = 1.0 / (0.001 + count)

        def rows_of(group, _):
            at = pl.ds(pl.multiple_of(group * (GROUP * 32), GROUP * 32), GROUP * 32)
            for e in range(32):
                left = (l1, l2)[e // 16][at, :]
                prod = jnp.dot(left, sequences(e // 16, e % 16), preferred_element_type=f32).astype(bf16)
                for i in range(GROUP):
                    outer[i, e * 32 : (e + 1) * 32, :] = prod[i * 32 : (i + 1) * 32, :]
            part = scale[pl.ds(pl.multiple_of(group * GROUP, GROUP), GROUP), :]
            for i in range(GROUP):
                mixed = jnp.dot(w_ref[...], outer[i], preferred_element_type=f32)
                out_ref[group * GROUP + i] = (mixed * part[i : i + 1, :]).T.astype(bf16)
            return 0

        lax.fori_loop(0, RD // GROUP, rows_of, 0)

    blocks = [pl.BlockSpec((544, t.shape[1]), lambda j: (skip + j, 0)) for t in first]
    blocks += [pl.BlockSpec((512, t.shape[1]), lambda j: (skip + j, 0)) for t in second]
    return pl.pallas_call(
        kernel,
        grid=(chunks,),
        out_shape=jax.ShapeDtypeStruct((RD, columns, out_width), bf16),
        in_specs=[
            whole(*left1.shape),
            whole(*left2.shape),
            whole(*weight.shape),
            whole(*row_mask.shape),
        ]
        + blocks
        + [pl.BlockSpec(memory_space=pl.ANY)] * len(earlier),
        out_specs=pl.BlockSpec((RD, CHUNK, out_width), lambda j: (0, start + j, 0)),
        scratch_shapes=[pltpu.VMEM((GROUP, 1024, CHUNK), bf16), pltpu.VMEM((RD, CHUNK), f32)],
        input_output_aliases={14: 0} if earlier else {},
        compiler_params=vmem(),
        name="pair",
    )(left1, left2, weight, row_mask, *first, *second, *earlier)


def send_both(blocks):
    return [
        (lax.ppermute(block, axis, ring(1)), lax.ppermute(block, axis, ring(-1))) for block, axis in blocks
    ]


def send_on(parts):
    return [
        (lax.ppermute(low, axis, ring(1)), lax.ppermute(high, axis, ring(-1))) for (low, high), axis in parts
    ]


def on_device(x, mask, gain, bias, w_left, b_left, w_right, b_right, w_out):
    columns = x.shape[1] // 4
    width = w_left.shape[1]
    chunks = columns // CHUNK
    together = lax.optimization_barrier

    position = jnp.stack([lax.axis_index("x"), lax.axis_index("z")]).astype(jnp.int32)
    norm = gain[None], bias[None]
    left = project_left(x[0], mask, *norm, w_left.T, b_left[None])
    right = project_right(x[0], mask, *norm, w_right.T, b_right[None], *left)
    right = lax.all_to_all(right.reshape(8, width, -1), COLUMN, 0, 0, tiled=True)

    halves = right[:, :16], right[:, 16:]
    got = send_both(((halves[0], "x"), (halves[1], "z")))
    far = send_on([((before[:4], after[4:]), axis) for (before, after), axis in zip(got, "xz")])
    held = [(halves[h], *got[h], *far[h]) for h in range(2)]

    mixed = [
        interleave(position, *held, columns, 0, 2, True),
        interleave(position, *held, columns, 2, chunks - 2, False),
    ]
    weight = w_out.reshape(width, width, -1).transpose(2, 1, 0).reshape(-1, width * width)

    def own_step(blocks):
        got = send_both(((blocks[0], "z"), (blocks[1], "x")))
        return got, [(before[:, :TILE], after[:, TILE:]) for before, after in got]

    def all_places(blocks, got, far):
        return [(blocks[h], *got[h], *far[h]) for h in range(2)]

    early, late = mixed
    got, onward = own_step(early)
    onward, late = together((onward, late))
    far = send_on(list(zip(onward, "zx")))
    far, late = together((far, late))
    early = all_places(early, got, far)
    got, onward = own_step(late)

    left1, left2, row_mask = arrange_left(position, *early, 2)
    fixed = left1, left2, weight, row_mask
    result = pair(*fixed, *early, 0, 0, 1, None, columns)
    onward, result = together((onward, result))
    far = send_on(list(zip(onward, "zx")))
    late = all_places(late, got, far)
    result = pair(*fixed, *early, 0, 1, 1, result, columns)
    return pair(*fixed, *late, 2, 2, chunks - 2, result, columns)


def solution(mesh):
    split = Mesh(mesh.devices.reshape(4, 4, 2, 2, 2), EVERY)
    placed = (P(EVERY, None, None), P(EVERY, None)) + (P(),) * 7
    return jax.shard_map(
        on_device,
        mesh=split,
        in_specs=placed,
        out_specs=P(PLANE, ("yl", "core"), None),
        check_vma=False,
    )
```

time: 205 us -> 170 us (0.83)
  local copies, waits for them, and re-layouts: 35.2 us -> 12.7 us
  Pallas kernels: 55.7 us -> 71.2 us
  between operations: 13.6 us -> 0.42 us
  waiting for transfers between devices: 40 us -> 27.6 us
  blocking collectives: 27.9 us -> 19.9 us
  starting transfers between devices: 30.1 us -> 37.4 us
    all_to_all x1 -> x0, waiting for transfers between devices: 19.9 us -> none  [on_device(): left = lax.all_to_all(left.reshape(32, RD, width), PLANE, 0, 0, tiled=True)]
    unnamed x59 -> x42, local copies, waits for them, and re-layouts: 18 us -> 2.73 us
    ppermute x16 -> x24, starting transfers between devices: 24 us -> 37.4 us  [the longest x6 19.4 us: send_on(): lax.ppermute(high, axis, ring(-1))]
    all_gather x1 -> x0, blocking collectives: 11.7 us -> none  [on_device(): left = lax.all_gather(left, ('yl', 'core'), axis=1)]
    pallas_call x2 -> x5, Pallas kernels: 15 us -> 23.5 us  [the longest x2 12.2 us: interleave(): pl.pallas_call(kernel, grid_spec=pltpu.PrefetchScalarGridSpec(num_scalar_...]
    ppermute x16 -> x24, waiting for transfers between devices: 20.1 us -> 27.6 us  [the longest x6 12.4 us: send_both(): lax.ppermute(block, axis, ring(-1))]
    squeeze x4 -> x0, local copies, waits for them, and re-layouts: 7.1 us -> none  [on_device(): lower, upper = (lambda t: t[0], lambda t: t[1])]
    pallas_call x1 -> x3, Pallas kernels: 40.7 us -> 47.7 us  [pair(): pl.pallas_call(kernel, grid=(chunks,), out_shape=jax.ShapeDtypeStruct((RD...]
  transfers between devices with their start and end apart: 18 -> 24, of which waited for: 8 -> 8; matrix products, arithmetic and copies ran while one was open for 9% -> 6% of each run, Pallas kernels for 3% -> 18%
where the time goes in v2:
time: 170 us
  Pallas kernels  71.2 us (42%)
  starting transfers between devices  37.4 us (22%)
  waiting for transfers between devices  27.6 us (16%)
  blocking collectives  19.9 us (12%)
  local copies, waits for them, and re-layouts  12.7 us (7%)
    pallas_call x3, Pallas kernels, pair(): pl.pallas_call(kernel, grid=(chunks,), out_shape=jax.ShapeDtypeStruct((RD...  47.7 us
    all_to_all x1, blocking collectives, on_device(): lax.all_to_all(right.reshape(8, width, -1), COLUMN, 0, 0, tiled=True)  19.9 us
    ppermute x6, starting transfers between devices, send_on(): lax.ppermute(high, axis, ring(-1))  19.4 us
    ppermute x6, starting transfers between devices, send_both(): lax.ppermute(block, axis, ring(-1))  14.8 us
    ppermute x6, waiting for transfers between devices, send_both(): lax.ppermute(block, axis, ring(-1))  12.4 us
    pallas_call x2, Pallas kernels, interleave(): pl.pallas_call(kernel, grid_spec=pltpu.PrefetchScalarGridSpec(num_scalar_...  12.2 us
    ppermute x6, waiting for transfers between devices, send_on(): lax.ppermute(low, axis, ring(1))  12.1 us
    pallas_call x1, Pallas kernels, project_right(): pl.pallas_call(kernel, grid=(4,), out_shape=jax.ShapeDtypeStruct((2, 4, w...  5.14 us
  transfers between devices with their start and end apart: 24, of which 8 were waited for; matrix products, arithmetic and copies ran while one was open for 6% of the time, Pallas kernels for 18%

profile of v2, /device:TPU:0, one launch (start us, length us, event | category | flops | bytes accessed | tf_op | source)
XLA Modules:
  0.0 169.8 jit_solution(1674366960280497603)
XLA Ops:
  0.0 2.4 %project_left.1 = (bf16[2,32,512]{2,1,0:T(8,128)(2,1)}, f32[2,8,128]{2,1,0:T(8,128)}) custom-call(bf16[5120,256]{1,0:T(8,128)(2,1)} %bitcast.15, f32[1,5120]{1,0:T(1,128)} %m_ref.1, f32[1,256]{1,0:T(1,128)} %bitcast.23, f32[1,256]{1,0:T(1,128)} %bitcast.25, bf16[32,256]{1,0:T(8,128)(2,1)} %bitcast.21, f32[1,32]{1,0:T(1,128)} %bitcast.27), custom_call_target="tpu_custom_call" | custom-call | tf_op jit(solution)/shard_map/project_left/pallas_call | solution.py:76
  2.4 5.1 %project_right.1 = bf16[2,4,32,1920]{3,2,1,0:T(8,128)(2,1)} custom-call(bf16[5120,256]{1,0:T(8,128)(2,1)} %bitcast.16, f32[4,1,1280]{2,1,0:T(1,128)} %bitcast.20, f32[1,256]{1,0:T(1,128)} %bitcast.24, f32[1,256]{1,0:T(1,128)} %bitcast.26, bf16[32,256]{1,0:T(8,128)(2,1)} %bitcast.22, f32[1,32]{1,0:T(1,128)} %bitcast.28, ...), custom_call_target="tpu_custom_call" | custom-call | tf_op jit(solution)/shard_map/project_right/pallas_call | solution.py:119
  7.6 19.9 %all_to_all.5 = bf16[8,32,1920]{2,1,0:T(8,128)(2,1)S(1)} all-to-all(bf16[8,32,1920]{2,1,0:T(8,128)(2,1)} %bitcast.17), channel_id=1, replica_groups=mesh['x'=4,'z'=4,'yh'=2,'yl'=2,'core'=2] {'yh','yl','core'}, dimensions={0} | all-to-all | bytes 1966080 | tf_op jit(solution)/shard_map/all_to_all | solution.py:369
  27.6 4.1 %collective-permute-start.5 = (bf16[8,16,1920]{2,1,0:T(8,128)(2,1)S(1)}, bf16[8,16,1920]{2,1,0:T(8,128)(2,1)S(1)}, u32[]{:S(2)}, u32[]{:S(2)}) collective-permute-start(bf16[8,16,1920]{2,1,0:T(8,128)(2,1)S(1)} %get-tuple-element.57.refs_5_.refs_20_), channel_id=1, source_target_pairs={{0,24},{8,0},{16,8},{24,16},{1,25},{9,1},{17,9},{25,17},{2,26},{10... | collective-permute-start | bytes 1474568 | tf_op jit(solution)/shard_map/ppermute | solution.py:349
  31.7 2.8 %collective-permute-start.1 = (bf16[8,16,1920]{2,1,0:T(8,128)(2,1)S(1)}, bf16[8,16,1920]{2,1,0:T(8,128)(2,1)S(1)}, u32[]{:S(2)}, u32[]{:S(2)}) collective-permute-start(bf16[8,16,1920]{2,1,0:T(8,128)(2,1)S(1)} %get-tuple-element.58.refs_0_.refs_10_.refs_15_), channel_id=1, source_target_pairs={{0,96},{32,0},{64,32},{96,64},{1,97},{33,1},{65,33},{97,65},{2,98}... | collective-permute-start | bytes 1474568 | tf_op jit(solution)/shard_map/ppermute | solution.py:349
  34.5 7.4 %collective-permute-done.5.refs_7_.refs_22_ = bf16[8,16,1920]{2,1,0:T(8,128)(2,1)S(1)} collective-permute-done((bf16[8,16,1920]{2,1,0:T(8,128)(2,1)S(1)}, bf16[8,16,1920]{2,1,0:T(8,128)(2,1)S(1)}, u32[]{:S(2)}, u32[]{:S(2)}) %collective-permute-start.5) | collective-permute-done | bytes 491552 | tf_op jit(solution)/shard_map/ppermute | solution.py:349
  42.7 3.7 %collective-permute-start.7 = (bf16[4,16,1920]{2,1,0:T(8,128)(2,1)}, bf16[4,16,1920]{2,1,0:T(8,128)(2,1)}, u32[]{:S(2)}, u32[]{:S(2)}) collective-permute-start(bf16[4,16,1920]{2,1,0:T(8,128)(2,1)} %slice.61), channel_id=1, source_target_pairs={{0,24},{8,0},{16,8},{24,16},{1,25},{9,1},{17,9},{25,17},{2,26},{10... | collective-permute-start | bytes 737288 | tf_op jit(solution)/shard_map/ppermute | solution.py:355
  47.9 2.8 %collective-permute-start.3 = (bf16[4,16,1920]{2,1,0:T(8,128)(2,1)}, bf16[4,16,1920]{2,1,0:T(8,128)(2,1)S(1)}, u32[]{:S(2)}, u32[]{:S(2)}) collective-permute-start(bf16[4,16,1920]{2,1,0:T(8,128)(2,1)} %slice.58), channel_id=1, source_target_pairs={{0,96},{32,0},{64,32},{96,64},{1,97},{33,1},{65,33},{97,65},{2,98}... | collective-permute-start | bytes 737288 | tf_op jit(solution)/shard_map/ppermute | solution.py:355
  52.1 2.8 %collective-permute-done.6.refs_8_.refs_23_ = bf16[4,16,1920]{2,1,0:T(8,128)(2,1)} collective-permute-done((bf16[4,16,1920]{2,1,0:T(8,128)(2,1)}, bf16[4,16,1920]{2,1,0:T(8,128)(2,1)}, u32[]{:S(2)}, u32[]{:S(2)}) %collective-permute-start.6) | collective-permute-done | bytes 245792 | tf_op jit(solution)/shard_map/ppermute | solution.py:355
  54.9 4.2 %collective-permute-done.2.refs_3_.refs_13_.refs_18_ = bf16[4,16,1920]{2,1,0:T(8,128)(2,1)S(1)} collective-permute-done((bf16[4,16,1920]{2,1,0:T(8,128)(2,1)}, bf16[4,16,1920]{2,1,0:T(8,128)(2,1)S(1)}, u32[]{:S(2)}, u32[]{:S(2)}) %collective-permute-start.2) | collective-permute-done | bytes 245792 | tf_op jit(solution)/shard_map/ppermute | solution.py:355
  59.9 5.9 %interleave.2 = (bf16[1360,256]{1,0:T(8,128)(2,1)}, bf16[1280,256]{1,0:T(8,128)(2,1)}) custom-call(s32[2]{0:T(128)} %pad_add_fusion.pos, bf16[8,16,1920]{2,1,0:T(8,128)(2,1)} %copy-done, bf16[8,16,1920]{2,1,0:T(8,128)(2,1)} %copy-done.2, bf16[8,16,1920]{2,1,0:T(8,128)(2,1)} %copy-done.1, bf16[4,16,1920]{2,1,0:T(8,128)(2,1)} %copy-done.9, ...), custom_call_target="tpu_custom_call" | custom-call | tf_op jit(solution)/shard_map/interleave/pallas_call | solution.py:222
  65.8 3.2 %collective-permute-start.9 = (bf16[1360,256]{1,0:T(8,128)(2,1)}, bf16[1360,256]{1,0:T(8,128)(2,1)S(1)}, u32[]{:S(2)}, u32[]{:S(2)}) collective-permute-start(bf16[1360,256]{1,0:T(8,128)(2,1)} %get-tuple-element.33.refs_0_), channel_id=1, source_target_pairs={{0,24},{8,0},{16,8},{24,16},{1,25},{9,1},{17,9},{25,17},{2,26},{10... | collective-permute-start | bytes 2088968 | tf_op jit(solution)/shard_map/ppermute | solution.py:349
  69.0 2.0 %collective-permute-start.10 = (bf16[1280,256]{1,0:T(8,128)(2,1)}, bf16[1280,256]{1,0:T(8,128)(2,1)S(1)}, u32[]{:S(2)}, u32[]{:S(2)}) collective-permute-start(bf16[1280,256]{1,0:T(8,128)(2,1)} %get-tuple-element.34.refs_5_), channel_id=1, source_target_pairs={{0,32},{32,64},{64,96},{96,0},{1,33},{33,65},{65,97},{97,1},{2,34}... | collective-permute-start | bytes 1966088 | tf_op jit(solution)/shard_map/ppermute | solution.py:349
  71.0 6.2 %interleave.3 = (bf16[1632,256]{1,0:T(8,128)(2,1)}, bf16[1536,256]{1,0:T(8,128)(2,1)}) custom-call(s32[2]{0:T(128)} %pad_add_fusion.pos, bf16[8,16,1920]{2,1,0:T(8,128)(2,1)} %copy-done, bf16[8,16,1920]{2,1,0:T(8,128)(2,1)} %copy-done.2, bf16[8,16,1920]{2,1,0:T(8,128)(2,1)} %copy-done.1, bf16[4,16,1920]{2,1,0:T(8,128)(2,1)} %copy-done.9, ...), custom_call_target="tpu_custom_call" | custom-call | tf_op jit(solution)/shard_map/interleave/pallas_call | solution.py:222
  77.3 4.9 %collective-permute-done.11.refs_7_ = bf16[1280,256]{1,0:T(8,128)(2,1)S(1)} collective-permute-done((bf16[1280,256]{1,0:T(8,128)(2,1)}, bf16[1280,256]{1,0:T(8,128)(2,1)S(1)}, u32[]{:S(2)}, u32[]{:S(2)}) %collective-permute-start.11) | collective-permute-done | bytes 655392 | tf_op jit(solution)/shard_map/ppermute | solution.py:349
  82.3 1.2 collective-permute-done.10.refs_6_
  83.5 1.4 collective-permute-done.8.refs_1_
  85.0 3.2 %collective-permute-start.13 = (bf16[1360,128]{1,0:T(8,128)(2,1)S(1)}, bf16[1360,128]{1,0:T(8,128)(2,1)S(1)}, u32[]{:S(2)}, u32[]{:S(2)}) collective-permute-start(bf16[1360,128]{1,0:T(8,128)(2,1)S(1)} %slice.63), channel_id=1, source_target_pairs={{0,24},{8,0},{16,8},{24,16},{1,25},{9,1},{17,9},{25,17},{2,26},{10... | collective-permute-start | bytes 1044488 | tf_op jit(solution)/shard_map/ppermute | solution.py:355
  88.2 3.2 %collective-permute-start.15 = (bf16[1280,128]{1,0:T(8,128)(2,1)S(1)}, bf16[1280,128]{1,0:T(8,128)(2,1)S(1)}, u32[]{:S(2)}, u32[]{:S(2)}) collective-permute-start(bf16[1280,128]{1,0:T(8,128)(2,1)S(1)} %slice.65), channel_id=1, source_target_pairs={{0,96},{32,0},{64,32},{96,64},{1,97},{33,1},{65,33},{97,65},{2,98}... | collective-permute-start | bytes 983048 | tf_op jit(solution)/shard_map/ppermute | solution.py:355
  91.5 5.0 %collective-permute-done.14.refs_8_ = bf16[1280,128]{1,0:T(8,128)(2,1)S(1)} collective-permute-done((bf16[1280,128]{1,0:T(8,128)(2,1)S(1)}, bf16[1280,128]{1,0:T(8,128)(2,1)S(1)}, u32[]{:S(2)}, u32[]{:S(2)}) %collective-permute-start.14) | collective-permute-done | bytes 327712 | tf_op jit(solution)/shard_map/ppermute | solution.py:355
  98.3 1.1 collective-permute-start.16
  99.4 3.7 %collective-permute-start.19 = (bf16[1536,256]{1,0:T(8,128)(2,1)}, bf16[1536,256]{1,0:T(8,128)(2,1)}, u32[]{:S(2)}, u32[]{:S(2)}) collective-permute-start(bf16[1536,256]{1,0:T(8,128)(2,1)} %get-tuple-element.51.refs_5_), channel_id=1, source_target_pairs={{0,96},{32,0},{64,32},{96,64},{1,97},{33,1},{65,33},{97,65},{2,98}... | collective-permute-start | bytes 2359304 | tf_op jit(solution)/shard_map/ppermute | solution.py:349
  103.9 1.8 %copy.19.w_ref = bf16[128,1024]{1,0:T(8,128)(2,1)} copy(bf16[128,1024]{0,1:T(8,128)(2,1)} %bitcast.18) | data formatting | bytes 524288 | tf_op jit(solution)/shard_map/reshape | solution.py:380
  105.7 3.7 %arrange_left.1 = (bf16[1024,128]{1,0:T(8,128)(2,1)}, bf16[1024,128]{1,0:T(8,128)(2,1)}, bf16[32,128]{1,0:T(8,128)(2,1)}) custom-call(s32[2]{0:T(128)} %pad_add_fusion.pos, bf16[1360,256]{1,0:T(8,128)(2,1)} %get-tuple-element.33.refs_0_, bf16[1360,256]{1,0:T(8,128)(2,1)} %copy-done.4, bf16[1360,256]{1,0:T(8,128)(2,1)} %copy-done.3, ...), custom_call_target="tpu_custom_call" | custom-call | tf_op jit(solution)/shard_map/arrange_left/pallas_call | solution.py:278
  109.4 10.7 %pair.3.refs_10_ = bf16[32,1280,128]{2,1,0:T(8,128)(2,1)} custom-call(bf16[1024,128]{1,0:T(8,128)(2,1)} %get-tuple-element.47.l1, bf16[1024,128]{1,0:T(8,128)(2,1)} %get-tuple-element.48.l2, bf16[128,1024]{1,0:T(8,128)(2,1)} %copy.19.w_ref, bf16[32,128]{1,0:T(8,128)(2,1)} %get-tuple-element.49.n_ref, bf16[1360,256]{1,0:T(8,128)(2,1)} %get-tuple-element.33.refs_0_, ...), custom_call_target="tpu_custom_call" | custom-call | tf_op jit(solution)/shard_map/pair/pallas_call | solution.py:327
  121.1 1.0 slice.68
  122.2 1.0 slice.67
  123.2 1.0 slice.66
  124.3 3.2 %collective-permute-start.21 = (bf16[1632,128]{1,0:T(8,128)(2,1)S(1)}, bf16[1632,128]{1,0:T(8,128)(2,1)S(1)}, u32[]{:S(2)}, u32[]{:S(2)}) collective-permute-start(bf16[1632,128]{1,0:T(8,128)(2,1)S(1)} %slice.67), channel_id=1, source_target_pairs={{0,24},{8,0},{16,8},{24,16},{1,25},{9,1},{17,9},{25,17},{2,26},{10... | collective-permute-start | bytes 1253384 | tf_op jit(solution)/shard_map/ppermute | solution.py:355
  127.6 3.2 %collective-permute-start.23 = (bf16[1536,128]{1,0:T(8,128)(2,1)S(1)}, bf16[1536,128]{1,0:T(8,128)(2,1)S(1)}, u32[]{:S(2)}, u32[]{:S(2)}) collective-permute-start(bf16[1536,128]{1,0:T(8,128)(2,1)S(1)} %slice.69), channel_id=1, source_target_pairs={{0,96},{32,0},{64,32},{96,64},{1,97},{33,1},{65,33},{97,65},{2,98}... | collective-permute-start | bytes 1179656 | tf_op jit(solution)/shard_map/ppermute | solution.py:355
  130.8 10.7 %pair.4.refs_10_ = bf16[32,1280,128]{2,1,0:T(8,128)(2,1)} custom-call(bf16[1024,128]{1,0:T(8,128)(2,1)} %get-tuple-element.47.l1, bf16[1024,128]{1,0:T(8,128)(2,1)} %get-tuple-element.48.l2, bf16[128,1024]{1,0:T(8,128)(2,1)} %copy.19.w_ref, bf16[32,128]{1,0:T(8,128)(2,1)} %get-tuple-element.49.n_ref, ...), custom_call_target="tpu_custom_call", output_to_operand_aliasing={{}: (14, {})} | custom-call | tf_op jit(solution)/shard_map/pair/pallas_call | solution.py:327
  143.3 26.3 %pair.5 = bf16[32,1280,128]{2,1,0:T(8,128)(2,1)} custom-call(bf16[1024,128]{1,0:T(8,128)(2,1)} %get-tuple-element.47.l1, bf16[1024,128]{1,0:T(8,128)(2,1)} %get-tuple-element.48.l2, bf16[128,1024]{1,0:T(8,128)(2,1)} %copy.19.w_ref, bf16[32,128]{1,0:T(8,128)(2,1)} %get-tuple-element.49.n_ref, ...), custom_call_target="tpu_custom_call", output_to_operand_aliasing={{}: (14, {})} | custom-call | tf_op jit(solution)/shard_map/pair/pallas_call | solution.py:327
  (83 shorter events, 10.1 us)
Async XLA Ops:
  27.6 31.5 %copy-start = (bf16[8,16,1920]{2,1,0:T(8,128)(2,1)}, bf16[8,16,1920]{2,1,0:T(8,128)(2,1)S(1)}, u32[]{:S(2)}) copy-start(bf16[8,16,1920]{2,1,0:T(8,128)(2,1)S(1)} %get-tuple-element.58.refs_0_.refs_10_.refs_15_) | copy-start | bytes 1474564
  27.6 31.5 %copy-start.7 = (bf16[8,16,1920]{2,1,0:T(8,128)(2,1)}, bf16[8,16,1920]{2,1,0:T(8,128)(2,1)S(1)}, u32[]{:S(2)}) copy-start(bf16[8,16,1920]{2,1,0:T(8,128)(2,1)S(1)} %get-tuple-element.57.refs_5_.refs_20_) | copy-start | bytes 1474564
  27.6 14.3 %collective-permute-start.5 = (bf16[8,16,1920]{2,1,0:T(8,128)(2,1)S(1)}, bf16[8,16,1920]{2,1,0:T(8,128)(2,1)S(1)}, u32[]{:S(2)}, u32[]{:S(2)}) collective-permute-start(bf16[8,16,1920]{2,1,0:T(8,128)(2,1)S(1)} %get-tuple-element.57.refs_5_.refs_20_), channel_id=1, source_target_pairs={{0,24},{8,0},{16,8},{24,16},{1,25},{9,1},{17,9},{25,17},{2,26},{10... | collective-permute-start | bytes 1474568 | tf_op jit(solution)/shard_map/ppermute | solution.py:349
  31.7 14.7 %collective-permute-start.4 = (bf16[8,16,1920]{2,1,0:T(8,128)(2,1)S(1)}, bf16[8,16,1920]{2,1,0:T(8,128)(2,1)S(1)}, u32[]{:S(2)}, u32[]{:S(2)}) collective-permute-start(bf16[8,16,1920]{2,1,0:T(8,128)(2,1)S(1)} %get-tuple-element.57.refs_5_.refs_20_), channel_id=1, source_target_pairs={{0,8},{8,16},{16,24},{24,0},{1,9},{9,17},{17,25},{25,1},{2,10},{10... | collective-permute-start | bytes 1474568 | tf_op jit(solution)/shard_map/ppermute | solution.py:349
  31.7 15.5 %collective-permute-start.1 = (bf16[8,16,1920]{2,1,0:T(8,128)(2,1)S(1)}, bf16[8,16,1920]{2,1,0:T(8,128)(2,1)S(1)}, u32[]{:S(2)}, u32[]{:S(2)}) collective-permute-start(bf16[8,16,1920]{2,1,0:T(8,128)(2,1)S(1)} %get-tuple-element.58.refs_0_.refs_10_.refs_15_), channel_id=1, source_target_pairs={{0,96},{32,0},{64,32},{96,64},{1,97},{33,1},{65,33},{97,65},{2,98}... | collective-permute-start | bytes 1474568 | tf_op jit(solution)/shard_map/ppermute | solution.py:349
  34.5 16.2 %collective-permute-start = (bf16[8,16,1920]{2,1,0:T(8,128)(2,1)S(1)}, bf16[8,16,1920]{2,1,0:T(8,128)(2,1)S(1)}, u32[]{:S(2)}, u32[]{:S(2)}) collective-permute-start(bf16[8,16,1920]{2,1,0:T(8,128)(2,1)S(1)} %get-tuple-element.58.refs_0_.refs_10_.refs_15_), channel_id=1, source_target_pairs={{0,32},{32,64},{64,96},{96,0},{1,33},{33,65},{65,97},{97,1},{2,34}... | collective-permute-start | bytes 1474568 | tf_op jit(solution)/shard_map/ppermute | solution.py:349
  41.9 17.2 %copy-start.10 = (bf16[8,16,1920]{2,1,0:T(8,128)(2,1)}, bf16[8,16,1920]{2,1,0:T(8,128)(2,1)S(1)}, u32[]{:S(2)}) copy-start(bf16[8,16,1920]{2,1,0:T(8,128)(2,1)S(1)} %collective-permute-done.5.refs_7_.refs_22_) | copy-start | bytes 1474564
  42.7 9.4 %collective-permute-start.7 = (bf16[4,16,1920]{2,1,0:T(8,128)(2,1)}, bf16[4,16,1920]{2,1,0:T(8,128)(2,1)}, u32[]{:S(2)}, u32[]{:S(2)}) collective-permute-start(bf16[4,16,1920]{2,1,0:T(8,128)(2,1)} %slice.61), channel_id=1, source_target_pairs={{0,24},{8,0},{16,8},{24,16},{1,25},{9,1},{17,9},{25,17},{2,26},{10... | collective-permute-start | bytes 737288 | tf_op jit(solution)/shard_map/ppermute | solution.py:355
  47.2 7.8 %collective-permute-start.6 = (bf16[4,16,1920]{2,1,0:T(8,128)(2,1)}, bf16[4,16,1920]{2,1,0:T(8,128)(2,1)}, u32[]{:S(2)}, u32[]{:S(2)}) collective-permute-start(bf16[4,16,1920]{2,1,0:T(8,128)(2,1)} %slice.60), channel_id=1, source_target_pairs={{0,8},{8,16},{16,24},{24,0},{1,9},{9,17},{17,25},{25,1},{2,10},{10... | collective-permute-start | bytes 737288 | tf_op jit(solution)/shard_map/ppermute | solution.py:355
  47.9 7.0 %collective-permute-start.3 = (bf16[4,16,1920]{2,1,0:T(8,128)(2,1)}, bf16[4,16,1920]{2,1,0:T(8,128)(2,1)S(1)}, u32[]{:S(2)}, u32[]{:S(2)}) collective-permute-start(bf16[4,16,1920]{2,1,0:T(8,128)(2,1)} %slice.58), channel_id=1, source_target_pairs={{0,96},{32,0},{64,32},{96,64},{1,97},{33,1},{65,33},{97,65},{2,98}... | collective-permute-start | bytes 737288 | tf_op jit(solution)/shard_map/ppermute | solution.py:355
  51.5 7.6 %collective-permute-start.2 = (bf16[4,16,1920]{2,1,0:T(8,128)(2,1)}, bf16[4,16,1920]{2,1,0:T(8,128)(2,1)S(1)}, u32[]{:S(2)}, u32[]{:S(2)}) collective-permute-start(bf16[4,16,1920]{2,1,0:T(8,128)(2,1)} %slice.57), channel_id=1, source_target_pairs={{0,32},{32,64},{64,96},{96,0},{1,33},{33,65},{65,97},{97,1},{2,34}... | collective-permute-start | bytes 737288 | tf_op jit(solution)/shard_map/ppermute | solution.py:355
  51.5 51.6 %copy-start.20 = (bf16[1024,128]{1,0:T(8,128)(2,1)S(1)}, bf16[1024,128]{1,0:T(8,128)(2,1)}, u32[]{:S(2)}) copy-start(bf16[1024,128]{1,0:T(8,128)(2,1)} %param.17) | copy-start | bytes 786436
  65.8 17.7 %collective-permute-start.9 = (bf16[1360,256]{1,0:T(8,128)(2,1)}, bf16[1360,256]{1,0:T(8,128)(2,1)S(1)}, u32[]{:S(2)}, u32[]{:S(2)}) collective-permute-start(bf16[1360,256]{1,0:T(8,128)(2,1)} %get-tuple-element.33.refs_0_), channel_id=1, source_target_pairs={{0,24},{8,0},{16,8},{24,16},{1,25},{9,1},{17,9},{25,17},{2,26},{10... | collective-permute-start | bytes 2088968 | tf_op jit(solution)/shard_map/ppermute | solution.py:349
  69.0 15.9 %collective-permute-start.8 = (bf16[1360,256]{1,0:T(8,128)(2,1)}, bf16[1360,256]{1,0:T(8,128)(2,1)S(1)}, u32[]{:S(2)}, u32[]{:S(2)}) collective-permute-start(bf16[1360,256]{1,0:T(8,128)(2,1)} %get-tuple-element.33.refs_0_), channel_id=1, source_target_pairs={{0,8},{8,16},{16,24},{24,0},{1,9},{9,17},{17,25},{25,1},{2,10},{10... | collective-permute-start | bytes 2088968 | tf_op jit(solution)/shard_map/ppermute | solution.py:349
  69.0 13.2 %collective-permute-start.11 = (bf16[1280,256]{1,0:T(8,128)(2,1)}, bf16[1280,256]{1,0:T(8,128)(2,1)S(1)}, u32[]{:S(2)}, u32[]{:S(2)}) collective-permute-start(bf16[1280,256]{1,0:T(8,128)(2,1)} %get-tuple-element.34.refs_5_), channel_id=1, source_target_pairs={{0,96},{32,0},{64,32},{96,64},{1,97},{33,1},{65,33},{97,65},{2,98}... | collective-permute-start | bytes 1966088 | tf_op jit(solution)/shard_map/ppermute | solution.py:349
  69.0 14.4 %collective-permute-start.10 = (bf16[1280,256]{1,0:T(8,128)(2,1)}, bf16[1280,256]{1,0:T(8,128)(2,1)S(1)}, u32[]{:S(2)}, u32[]{:S(2)}) collective-permute-start(bf16[1280,256]{1,0:T(8,128)(2,1)} %get-tuple-element.34.refs_5_), channel_id=1, source_target_pairs={{0,32},{32,64},{64,96},{96,0},{1,33},{33,65},{65,97},{97,1},{2,34}... | collective-permute-start | bytes 1966088 | tf_op jit(solution)/shard_map/ppermute | solution.py:349
  82.2 23.4 %copy-start.5 = (bf16[1280,256]{1,0:T(8,128)(2,1)}, bf16[1280,256]{1,0:T(8,128)(2,1)S(1)}, u32[]{:S(2)}) copy-start(bf16[1280,256]{1,0:T(8,128)(2,1)S(1)} %collective-permute-done.11.refs_7_) | copy-start | bytes 1966084
  83.5 22.2 %copy-start.6 = (bf16[1280,256]{1,0:T(8,128)(2,1)}, bf16[1280,256]{1,0:T(8,128)(2,1)S(1)}, u32[]{:S(2)}) copy-start(bf16[1280,256]{1,0:T(8,128)(2,1)S(1)} %collective-permute-done.10.refs_6_) | copy-start | bytes 1966084
  83.5 22.2 %copy-start.3 = (bf16[1360,256]{1,0:T(8,128)(2,1)}, bf16[1360,256]{1,0:T(8,128)(2,1)S(1)}, u32[]{:S(2)}) copy-start(bf16[1360,256]{1,0:T(8,128)(2,1)S(1)} %collective-permute-done.9.refs_2_) | copy-start | bytes 2088964
  84.9 20.8 %copy-start.4 = (bf16[1360,256]{1,0:T(8,128)(2,1)}, bf16[1360,256]{1,0:T(8,128)(2,1)S(1)}, u32[]{:S(2)}) copy-start(bf16[1360,256]{1,0:T(8,128)(2,1)S(1)} %collective-permute-done.8.refs_1_) | copy-start | bytes 2088964
  84.9 12.1 %collective-permute-start.12 = (bf16[1360,128]{1,0:T(8,128)(2,1)S(1)}, bf16[1360,128]{1,0:T(8,128)(2,1)S(1)}, u32[]{:S(2)}, u32[]{:S(2)}) collective-permute-start(bf16[1360,128]{1,0:T(8,128)(2,1)S(1)} %slice.62), channel_id=1, source_target_pairs={{0,8},{8,16},{16,24},{24,0},{1,9},{9,17},{17,25},{25,1},{2,10},{10... | collective-permute-start | bytes 1044488 | tf_op jit(solution)/shard_map/ppermute | solution.py:355
  85.0 12.0 %collective-permute-start.13 = (bf16[1360,128]{1,0:T(8,128)(2,1)S(1)}, bf16[1360,128]{1,0:T(8,128)(2,1)S(1)}, u32[]{:S(2)}, u32[]{:S(2)}) collective-permute-start(bf16[1360,128]{1,0:T(8,128)(2,1)S(1)} %slice.63), channel_id=1, source_target_pairs={{0,24},{8,0},{16,8},{24,16},{1,25},{9,1},{17,9},{25,17},{2,26},{10... | collective-permute-start | bytes 1044488 | tf_op jit(solution)/shard_map/ppermute | solution.py:355
  88.2 8.3 %collective-permute-start.14 = (bf16[1280,128]{1,0:T(8,128)(2,1)S(1)}, bf16[1280,128]{1,0:T(8,128)(2,1)S(1)}, u32[]{:S(2)}, u32[]{:S(2)}) collective-permute-start(bf16[1280,128]{1,0:T(8,128)(2,1)S(1)} %slice.64), channel_id=1, source_target_pairs={{0,32},{32,64},{64,96},{96,0},{1,33},{33,65},{65,97},{97,1},{2,34}... | collective-permute-start | bytes 983048 | tf_op jit(solution)/shard_map/ppermute | solution.py:355
  88.2 8.8 %collective-permute-start.15 = (bf16[1280,128]{1,0:T(8,128)(2,1)S(1)}, bf16[1280,128]{1,0:T(8,128)(2,1)S(1)}, u32[]{:S(2)}, u32[]{:S(2)}) collective-permute-start(bf16[1280,128]{1,0:T(8,128)(2,1)S(1)} %slice.65), channel_id=1, source_target_pairs={{0,96},{32,0},{64,32},{96,64},{1,97},{33,1},{65,33},{97,65},{2,98}... | collective-permute-start | bytes 983048 | tf_op jit(solution)/shard_map/ppermute | solution.py:355
  97.3 24.9 %collective-permute-start.17 = (bf16[1632,256]{1,0:T(8,128)(2,1)}, bf16[1632,256]{1,0:T(8,128)(2,1)}, u32[]{:S(2)}, u32[]{:S(2)}) collective-permute-start(bf16[1632,256]{1,0:T(8,128)(2,1)} %get-tuple-element.50.refs_0_), channel_id=1, source_target_pairs={{0,24},{8,0},{16,8},{24,16},{1,25},{9,1},{17,9},{25,17},{2,26},{10... | collective-permute-start | bytes 2506760 | tf_op jit(solution)/shard_map/ppermute | solution.py:349
  98.3 24.9 %collective-permute-start.16 = (bf16[1632,256]{1,0:T(8,128)(2,1)}, bf16[1632,256]{1,0:T(8,128)(2,1)}, u32[]{:S(2)}, u32[]{:S(2)}) collective-permute-start(bf16[1632,256]{1,0:T(8,128)(2,1)} %get-tuple-element.50.refs_0_), channel_id=1, source_target_pairs={{0,8},{8,16},{16,24},{24,0},{1,9},{9,17},{17,25},{25,1},{2,10},{10... | collective-permute-start | bytes 2506760 | tf_op jit(solution)/shard_map/ppermute | solution.py:349
  99.4 20.7 %collective-permute-start.19 = (bf16[1536,256]{1,0:T(8,128)(2,1)}, bf16[1536,256]{1,0:T(8,128)(2,1)}, u32[]{:S(2)}, u32[]{:S(2)}) collective-permute-start(bf16[1536,256]{1,0:T(8,128)(2,1)} %get-tuple-element.51.refs_5_), channel_id=1, source_target_pairs={{0,96},{32,0},{64,32},{96,64},{1,97},{33,1},{65,33},{97,65},{2,98}... | collective-permute-start | bytes 2359304 | tf_op jit(solution)/shard_map/ppermute | solution.py:349
  103.1 18.1 %collective-permute-start.18 = (bf16[1536,256]{1,0:T(8,128)(2,1)}, bf16[1536,256]{1,0:T(8,128)(2,1)}, u32[]{:S(2)}, u32[]{:S(2)}) collective-permute-start(bf16[1536,256]{1,0:T(8,128)(2,1)} %get-tuple-element.51.refs_5_), channel_id=1, source_target_pairs={{0,32},{32,64},{64,96},{96,0},{1,33},{33,65},{65,97},{97,1},{2,34}... | collective-permute-start | bytes 2359304 | tf_op jit(solution)/shard_map/ppermute | solution.py:349
  124.3 17.3 %collective-permute-start.20 = (bf16[1632,128]{1,0:T(8,128)(2,1)S(1)}, bf16[1632,128]{1,0:T(8,128)(2,1)S(1)}, u32[]{:S(2)}, u32[]{:S(2)}) collective-permute-start(bf16[1632,128]{1,0:T(8,128)(2,1)S(1)} %slice.66), channel_id=1, source_target_pairs={{0,8},{8,16},{16,24},{24,0},{1,9},{9,17},{17,25},{25,1},{2,10},{10... | collective-permute-start | bytes 1253384 | tf_op jit(solution)/shard_map/ppermute | solution.py:355
  124.3 17.2 %collective-permute-start.21 = (bf16[1632,128]{1,0:T(8,128)(2,1)S(1)}, bf16[1632,128]{1,0:T(8,128)(2,1)S(1)}, u32[]{:S(2)}, u32[]{:S(2)}) collective-permute-start(bf16[1632,128]{1,0:T(8,128)(2,1)S(1)} %slice.67), channel_id=1, source_target_pairs={{0,24},{8,0},{16,8},{24,16},{1,25},{9,1},{17,9},{25,17},{2,26},{10... | collective-permute-start | bytes 1253384 | tf_op jit(solution)/shard_map/ppermute | solution.py:355
  127.6 13.9 %collective-permute-start.22 = (bf16[1536,128]{1,0:T(8,128)(2,1)S(1)}, bf16[1536,128]{1,0:T(8,128)(2,1)S(1)}, u32[]{:S(2)}, u32[]{:S(2)}) collective-permute-start(bf16[1536,128]{1,0:T(8,128)(2,1)S(1)} %slice.68), channel_id=1, source_target_pairs={{0,32},{32,64},{64,96},{96,0},{1,33},{33,65},{65,97},{97,1},{2,34}... | collective-permute-start | bytes 1179656 | tf_op jit(solution)/shard_map/ppermute | solution.py:355
  127.6 13.9 %collective-permute-start.23 = (bf16[1536,128]{1,0:T(8,128)(2,1)S(1)}, bf16[1536,128]{1,0:T(8,128)(2,1)S(1)}, u32[]{:S(2)}, u32[]{:S(2)}) collective-permute-start(bf16[1536,128]{1,0:T(8,128)(2,1)S(1)} %slice.69), channel_id=1, source_target_pairs={{0,96},{32,0},{64,32},{96,64},{1,97},{33,1},{65,33},{97,65},{2,98}... | collective-permute-start | bytes 1179656 | tf_op jit(solution)/shard_map/ppermute | solution.py:355
  (13 other events, 60.4 us)

commit v3 on v2

--- a/solution.py
+++ b/solution.py
@@ -8,7 +8,7 @@
 
 RD = 32
 CHUNK = 256
-GROUP = 8
+GROUP = 32
 TILE = 128
 COLUMN = ("yh", "yl", "core")
 PLANE = ("x", "z", "yh")
@@ -17,7 +17,7 @@
 bf16 = jnp.bfloat16
 
 
-def vmem(mib=60):
+def vmem(mib=63):
     return pltpu.CompilerParams(vmem_limit_bytes=mib * 2**20)
 
 
@@ -147,59 +147,38 @@
     heights = (544, 512)
     extra = (272, 256) if with_left else (0, 0)
 
-    def place_rows(ins, put):
+    def by_row(ins, lane):
         own, before, after, low, high = ins
-        for place in range(4):
-            for m in range(8):
-                if place < 3:
-                    part = (own, before, after)[place][m]
-                else:
-                    part = low[m] if m < 4 else high[m - 4]
-                put(pl.ds(place * 8 + m, 16, stride=32), part.astype(f32))
+        at = slice(lane * TILE, (lane + 1) * TILE)
+        parts = [own[:, :, at], before[:, :, at], after[:, :, at], low[:, :, at], high[:, :, at]]
+        near = jnp.swapaxes(jnp.concatenate(parts[:2], axis=0), 0, 1)
+        away = jnp.swapaxes(jnp.concatenate(parts[2:], axis=0), 0, 1)
+        return jnp.concatenate([near, away], axis=1).reshape(512, TILE)
 
     def kernel(pos, *refs):
-        main, masks, lefts = refs[:10], refs[10:15], refs[15:-4]
-        outs, (scratch, mask_rows) = refs[-4:-2], refs[-2:]
-
-        def put_mask(at, part):
-            mask_rows[at, :] = part
-
-        place_rows(masks, put_mask)
-
-        def masks_at(row):
-            return mask_rows[pl.ds(pl.multiple_of(row * 32, 32), 32), :].astype(bf16)
-
+        main, masks, lefts = refs[:10], refs[10:15], refs[15 : 15 + 10 * with_left]
+        outs, mask_rows = refs[15 + 10 * with_left : -1], refs[-1]
+
+        def put(half, lane, base, rows):
+            outs[half][base : base + rows.shape[0], lane * TILE : (lane + 1) * TILE] = rows
+
+        mask_rows[...] = by_row(masks, 0)
         for chunk in range(chunks):
             for half in range(2):
                 base = chunk * heights[half]
-
-                def put(at, part):
-                    for lane in range(tiles):
-                        scratch[chunk, half, lane, at, :] = part[:, lane * TILE : (lane + 1) * TILE]
-
-                ins = [r.at[:, :, chunk * CHUNK : (chunk + 1) * CHUNK] for r in main[5 * half : 5 * half + 5]]
-                place_rows(ins, put)
                 for lane in range(tiles):
-                    at = slice(lane * TILE, (lane + 1) * TILE)
-                    outs[half][base : base + 512, at] = scratch[chunk, half, lane].astype(bf16)
+                    put(half, lane, base, by_row(main[5 * half : 5 * half + 5], chunk * tiles + lane))
                     if half == 0:
-                        outs[0][base + 512 : base + 544, at] = masks_at((start + chunk) * tiles + lane)
+                        row = ((start + chunk) * tiles + lane) * 32
+                        put(0, lane, base + 512, mask_rows[row : row + 32, :])
         if with_left:
             for half in range(2):
-                base = chunks * heights[half]
-
-                def put_left(at, part):
-                    scratch[chunks, half, 0, at, :] = part
-
-                place_rows(lefts[5 * half : 5 * half + 5], put_left)
+                rows = by_row(lefts[5 * half : 5 * half + 5], 0)
                 for lane in range(2):
-                    at = slice(lane * TILE, (lane + 1) * TILE)
-                    rows = scratch[chunks, half, 0, lane * 256 : (lane + 1) * 256, :]
-                    outs[half][base : base + 256, at] = rows.astype(bf16)
-            rows = masks_at(mask_tile + pos[0])
-            base = chunks * heights[0] + 256
-            outs[0][base : base + 16, :TILE] = rows[:16]
-            outs[0][base : base + 16, TILE:] = rows[16:]
+                    put(half, lane, chunks * heights[half], rows[lane * 256 : (lane + 1) * 256])
+            rows = mask_rows[pl.ds(pl.multiple_of((mask_tile + pos[0]) * 32, 32), 32), :]
+            for lane in range(2):
+                put(0, lane, chunks * heights[0] + 256, rows[lane * 16 : (lane + 1) * 16])
 
     def blocks(m):
         span = chunks * CHUNK
@@ -226,10 +205,7 @@
             grid=(1,),
             in_specs=specs,
             out_specs=tuple(whole(*shape) for shape in shapes),
-            scratch_shapes=[
-                pltpu.VMEM((chunks + with_left, 2, tiles, 512, TILE), f32),
-                pltpu.VMEM((512, TILE), f32),
-            ],
+            scratch_shapes=[pltpu.VMEM((512, TILE), bf16)],
         ),
         out_shape=tuple(jax.ShapeDtypeStruct(shape, bf16) for shape in shapes),
         compiler_params=vmem(),
@@ -237,14 +213,18 @@
     )(position, *args)
 
 
-def arrange_left(position, first, second, chunks):
+def arrange_left(position, first, second, chunks, w_out):
+    width = 32
+    features, out_width = w_out.shape
+
     def kernel(pos, *refs):
-        ins, (one_ref, two_ref, mask_ref, scratch) = refs[:10], refs[10:]
+        ins, (w_ref, one_ref, two_ref, mask_ref, weight_ref, scratch) = refs[:8], refs[8:]
+        w = jnp.swapaxes(w_ref[...].reshape(width, width, out_width), 0, 1).reshape(features, out_width)
+        weight_ref[...] = w.T
 
         def sequences(half, rows, lane):
             at = slice(lane * TILE, (lane + 1) * TILE)
-            own, before, after, low, high = ins[5 * half : 5 * half + 5]
-            return [r[rows, at] for r in (own, before, after)] + [(low, high)[lane][rows, :]]
+            return [r[rows, at] for r in ins[4 * half : 4 * half + 4]]
 
         def mine(half, values):
             wanted = lax.broadcasted_iota(jnp.int32, (RD, TILE), 0) + RD * pos[1 - half]
@@ -274,35 +254,32 @@
         rows = (272, 256)[half]
         return pl.BlockSpec((rows, t.shape[1]), lambda _, pos: (2 * chunks, 0))
 
-    shapes = [(RD * 32, 128), (RD * 32, 128), (RD, 128)]
+    shapes = [(RD * 32, 128), (RD * 32, 128), (RD, 128), (out_width, features)]
     return pl.pallas_call(
         kernel,
         grid_spec=pltpu.PrefetchScalarGridSpec(
             num_scalar_prefetch=1,
             grid=(1,),
-            in_specs=[block(0, t) for t in first] + [block(1, t) for t in second],
+            in_specs=[block(0, t) for t in first] + [block(1, t) for t in second] + [whole(*w_out.shape)],
             out_specs=tuple(whole(*shape) for shape in shapes),
             scratch_shapes=[pltpu.VMEM((RD * 32, 128), f32)],
         ),
         out_shape=tuple(jax.ShapeDtypeStruct(shape, bf16) for shape in shapes),
         compiler_params=vmem(),
         name="arrange_left",
-    )(position, *first, *second)
-
-
-def pair(left1, left2, weight, row_mask, first, second, base, start, chunks, result, columns):
+    )(position, *first, *second, w_out)
+
+
+def pair(left1, left2, weight, row_mask, first, second, start, chunks, result, columns):
     out_width = weight.shape[0]
-    skip = start - base
     earlier = () if result is None else (result,)
 
     def kernel(l1, l2, w_ref, n_ref, *refs):
-        ins, (out_ref, outer, scale) = refs[:10], refs[-3:]
+        ins, (out_ref, outer, scale) = refs[:8], refs[-3:]
 
         def sequences(half, row):
-            own, before, after, low, high = ins[5 * half : 5 * half + 5]
             at = slice(row * 32, row * 32 + 32)
-            far = jnp.concatenate([low[at, :], high[at, :]], axis=1)
-            return jnp.concatenate([own[at, :], before[at, :], after[at, :], far], axis=0)
+            return jnp.concatenate([r[at, :] for r in ins[4 * half : 4 * half + 4]], axis=0)
 
         count = jnp.dot(n_ref[...], sequences(0, 16), preferred_element_type=f32)
         scale[...] = 1.0 / (0.001 + count)
@@ -322,8 +299,8 @@
 
         lax.fori_loop(0, RD // GROUP, rows_of, 0)
 
-    blocks = [pl.BlockSpec((544, t.shape[1]), lambda j: (skip + j, 0)) for t in first]
-    blocks += [pl.BlockSpec((512, t.shape[1]), lambda j: (skip + j, 0)) for t in second]
+    blocks = [pl.BlockSpec((544, t.shape[1]), lambda j: (j, 0)) for t in first]
+    blocks += [pl.BlockSpec((512, t.shape[1]), lambda j: (j, 0)) for t in second]
     return pl.pallas_call(
         kernel,
         grid=(chunks,),
@@ -338,7 +315,7 @@
         + [pl.BlockSpec(memory_space=pl.ANY)] * len(earlier),
         out_specs=pl.BlockSpec((RD, CHUNK, out_width), lambda j: (0, start + j, 0)),
         scratch_shapes=[pltpu.VMEM((GROUP, 1024, CHUNK), bf16), pltpu.VMEM((RD, CHUNK), f32)],
-        input_output_aliases={14: 0} if earlier else {},
+        input_output_aliases={12: 0} if earlier else {},
         compiler_params=vmem(),
         name="pair",
     )(left1, left2, weight, row_mask, *first, *second, *earlier)
@@ -377,31 +354,22 @@
         interleave(position, *held, columns, 0, 2, True),
         interleave(position, *held, columns, 2, chunks - 2, False),
     ]
-    weight = w_out.reshape(width, width, -1).transpose(2, 1, 0).reshape(-1, width * width)
-
-    def own_step(blocks):
-        got = send_both(((blocks[0], "z"), (blocks[1], "x")))
-        return got, [(before[:, :TILE], after[:, TILE:]) for before, after in got]
-
-    def all_places(blocks, got, far):
-        return [(blocks[h], *got[h], *far[h]) for h in range(2)]
-
     early, late = mixed
-    got, onward = own_step(early)
-    onward, late = together((onward, late))
-    far = send_on(list(zip(onward, "zx")))
+    got = send_both(((early[0], "z"), (early[1], "x")))
+    got, late = together((got, late))
+    far = [lax.ppermute(before, axis, ring(1)) for (before, _), axis in zip(got, "zx")]
+    after = [lax.ppermute(block, axis, ring(-1)) for block, axis in zip(late, "zx")]
     far, late = together((far, late))
-    early = all_places(early, got, far)
-    got, onward = own_step(late)
-
-    left1, left2, row_mask = arrange_left(position, *early, 2)
+    early = [(early[h], *got[h], far[h]) for h in range(2)]
+    before = [lax.ppermute(block, axis, ring(1)) for block, axis in zip(late, "zx")]
+    early, after = together((early, after))
+    far = [lax.ppermute(block, axis, ring(-1)) for block, axis in zip(after, "zx")]
+    late = [(late[h], before[h], after[h], far[h]) for h in range(2)]
+
+    left1, left2, row_mask, weight = arrange_left(position, *early, 2, w_out)
     fixed = left1, left2, weight, row_mask
-    result = pair(*fixed, *early, 0, 0, 1, None, columns)
-    onward, result = together((onward, result))
-    far = send_on(list(zip(onward, "zx")))
-    late = all_places(late, got, far)
-    result = pair(*fixed, *early, 0, 1, 1, result, columns)
-    return pair(*fixed, *late, 2, 2, chunks - 2, result, columns)
+    result = pair(*fixed, *early, 0, 2, None, columns)
+    return pair(*fixed, *late, 2, chunks - 2, result, columns)
 
 
 def solution(mesh):

time: 170 us -> 150 us (0.88)
  local copies, waits for them, and re-layouts: 12.7 us -> 1 us
  Pallas kernels: 71.2 us -> 60 us
  waiting for transfers between devices: 27.6 us -> 38.3 us
  starting transfers between devices: 37.4 us -> 29.2 us
    ppermute x0 -> x8, waiting for transfers between devices: none -> 14.6 us  [the longest x2 14.2 us: on_device(): lax.ppermute(before, axis, ring(1))]
    ppermute x6 -> x2, starting transfers between devices: 19.4 us -> 6.59 us  [send_on(): lax.ppermute(high, axis, ring(-1))]
    ppermute x0 -> x8, starting transfers between devices: none -> 10.3 us  [the longest x4 7.22 us: on_device(): lax.ppermute(block, axis, ring(-1))]
    pallas_call x3 -> x2, Pallas kernels: 47.7 us -> 40.9 us  [pair(): pl.pallas_call(kernel, grid=(chunks,), out_shape=jax.ShapeDtypeStruct((RD...]
    ppermute x6 -> x2, waiting for transfers between devices: 12.1 us -> 6.86 us  [send_on(): lax.ppermute(low, axis, ring(1))]
    ppermute x6 -> x4, starting transfers between devices: 14.8 us -> 10.1 us  [send_both(): lax.ppermute(block, axis, ring(-1))]
    pallas_call x2, Pallas kernels: 12.2 us -> 7.6 us  [interleave(): pl.pallas_call(kernel, grid_spec=pltpu.PrefetchScalarGridSpec(num_scalar_...]
    slice x8 -> x0, local copies, waits for them, and re-layouts: 4.2 us -> none  [own_step(): return (got, [(before[:, :TILE], after[:, TILE:]) for before, after in got])]
  transfers between devices with their start and end apart: 24 -> 20, of which waited for: 8 -> 9; matrix products, arithmetic and copies ran while one was open for 6% -> 0% of each run, Pallas kernels for 18% -> 16%
where the time goes in v3:
time: 150 us; the launch traced here: 149 us
  Pallas kernels  60 us (40%)
  waiting for transfers between devices  38.3 us (26%)
  starting transfers between devices  29.2 us (19%)
  blocking collectives  19.9 us (13%)
    pallas_call x2, Pallas kernels, pair(): pl.pallas_call(kernel, grid=(chunks,), out_shape=jax.ShapeDtypeStruct((RD...  40.9 us
    all_to_all x1, blocking collectives, on_device(): lax.all_to_all(right.reshape(8, width, -1), COLUMN, 0, 0, tiled=True)  19.9 us
    ppermute x4, waiting for transfers between devices, send_both(): lax.ppermute(block, axis, ring(-1))  14.8 us
    ppermute x2, waiting for transfers between devices, on_device(): lax.ppermute(before, axis, ring(1))  14.2 us
    ppermute x4, starting transfers between devices, send_both(): lax.ppermute(block, axis, ring(-1))  10.1 us
    pallas_call x2, Pallas kernels, interleave(): pl.pallas_call(kernel, grid_spec=pltpu.PrefetchScalarGridSpec(num_scalar_...  7.6 us
    ppermute x4, starting transfers between devices, on_device(): lax.ppermute(block, axis, ring(-1))  7.22 us
    ppermute x2, waiting for transfers between devices, send_on(): lax.ppermute(low, axis, ring(1))  6.86 us
  transfers between devices with their start and end apart: 20, of which 9 were waited for; matrix products, arithmetic and copies ran while one was open for 0% of the time, Pallas kernels for 16%

profile of v3, /device:TPU:0, one launch (start us, length us, event | category | flops | bytes accessed | tf_op | source)
XLA Modules:
  0.0 149.2 jit_solution(18202156687899636879)
XLA Ops:
  0.0 2.4 %project_left.1 = (bf16[2,32,512]{2,1,0:T(8,128)(2,1)}, f32[2,8,128]{2,1,0:T(8,128)}) custom-call(bf16[5120,256]{1,0:T(8,128)(2,1)} %bitcast.11, f32[1,5120]{1,0:T(1,128)} %m_ref.1, f32[1,256]{1,0:T(1,128)} %bitcast.17, f32[1,256]{1,0:T(1,128)} %bitcast.19, bf16[32,256]{1,0:T(8,128)(2,1)} %bitcast.15, f32[1,32]{1,0:T(1,128)} %bitcast.21), custom_call_target="tpu_custom_call" | custom-call | tf_op jit(solution)/shard_map/project_left/pallas_call | solution.py:76
  2.4 5.1 %project_right.1 = bf16[2,4,32,1920]{3,2,1,0:T(8,128)(2,1)} custom-call(bf16[5120,256]{1,0:T(8,128)(2,1)} %bitcast.12, f32[4,1,1280]{2,1,0:T(1,128)} %bitcast.14, f32[1,256]{1,0:T(1,128)} %bitcast.18, f32[1,256]{1,0:T(1,128)} %bitcast.20, bf16[32,256]{1,0:T(8,128)(2,1)} %bitcast.16, f32[1,32]{1,0:T(1,128)} %bitcast.22, ...), custom_call_target="tpu_custom_call" | custom-call | tf_op jit(solution)/shard_map/project_right/pallas_call | solution.py:119
  7.6 19.9 %all_to_all.5 = bf16[8,32,1920]{2,1,0:T(8,128)(2,1)S(1)} all-to-all(bf16[8,32,1920]{2,1,0:T(8,128)(2,1)} %bitcast.13), channel_id=1, replica_groups=mesh['x'=4,'z'=4,'yh'=2,'yl'=2,'core'=2] {'yh','yl','core'}, dimensions={0} | all-to-all | bytes 1966080 | tf_op jit(solution)/shard_map/all_to_all | solution.py:346
  27.6 4.1 %collective-permute-start.5 = (bf16[8,16,1920]{2,1,0:T(8,128)(2,1)S(1)}, bf16[8,16,1920]{2,1,0:T(8,128)(2,1)S(1)}, u32[]{:S(2)}, u32[]{:S(2)}) collective-permute-start(bf16[8,16,1920]{2,1,0:T(8,128)(2,1)S(1)} %get-tuple-element.65.refs_5_.refs_20_), channel_id=1, source_target_pairs={{0,24},{8,0},{16,8},{24,16},{1,25},{9,1},{17,9},{25,17},{2,26},{10... | collective-permute-start | bytes 1474568 | tf_op jit(solution)/shard_map/ppermute | solution.py:326
  31.7 2.8 %collective-permute-start.1 = (bf16[8,16,1920]{2,1,0:T(8,128)(2,1)S(1)}, bf16[8,16,1920]{2,1,0:T(8,128)(2,1)S(1)}, u32[]{:S(2)}, u32[]{:S(2)}) collective-permute-start(bf16[8,16,1920]{2,1,0:T(8,128)(2,1)S(1)} %get-tuple-element.66.refs_0_.refs_10_.refs_15_), channel_id=1, source_target_pairs={{0,96},{32,0},{64,32},{96,64},{1,97},{33,1},{65,33},{97,65},{2,98}... | collective-permute-start | bytes 1474568 | tf_op jit(solution)/shard_map/ppermute | solution.py:326
  34.5 7.4 %collective-permute-done.5.refs_7_.refs_22_ = bf16[8,16,1920]{2,1,0:T(8,128)(2,1)S(1)} collective-permute-done((bf16[8,16,1920]{2,1,0:T(8,128)(2,1)S(1)}, bf16[8,16,1920]{2,1,0:T(8,128)(2,1)S(1)}, u32[]{:S(2)}, u32[]{:S(2)}) %collective-permute-start.5) | collective-permute-done | bytes 491552 | tf_op jit(solution)/shard_map/ppermute | solution.py:326
  42.0 3.8 %collective-permute-start.7 = (bf16[4,16,1920]{2,1,0:T(8,128)(2,1)S(1)}, bf16[4,16,1920]{2,1,0:T(8,128)(2,1)}, u32[]{:S(2)}, u32[]{:S(2)}) collective-permute-start(bf16[4,16,1920]{2,1,0:T(8,128)(2,1)S(1)} %slice.29), channel_id=1, source_target_pairs={{0,24},{8,0},{16,8},{24,16},{1,25},{9,1},{17,9},{25,17},{2,26},{10... | collective-permute-start | bytes 737288 | tf_op jit(solution)/shard_map/ppermute | solution.py:332
  45.7 0.1 collective-permute-start.6
  45.9 2.8 %collective-permute-start.3 = (bf16[4,16,1920]{2,1,0:T(8,128)(2,1)S(1)}, bf16[4,16,1920]{2,1,0:T(8,128)(2,1)}, u32[]{:S(2)}, u32[]{:S(2)}) collective-permute-start(bf16[4,16,1920]{2,1,0:T(8,128)(2,1)S(1)} %slice.26), channel_id=1, source_target_pairs={{0,96},{32,0},{64,32},{96,64},{1,97},{33,1},{65,33},{97,65},{2,98}... | collective-permute-start | bytes 737288 | tf_op jit(solution)/shard_map/ppermute | solution.py:332
  48.7 0.8 copy-done.2
  49.7 0.6 pad_add_fusion.pos
  50.3 3.1 %collective-permute-done.6.refs_8_.refs_23_ = bf16[4,16,1920]{2,1,0:T(8,128)(2,1)} collective-permute-done((bf16[4,16,1920]{2,1,0:T(8,128)(2,1)S(1)}, bf16[4,16,1920]{2,1,0:T(8,128)(2,1)}, u32[]{:S(2)}, u32[]{:S(2)}) %collective-permute-start.6) | collective-permute-done | bytes 245792 | tf_op jit(solution)/shard_map/ppermute | solution.py:332
  53.4 3.8 %collective-permute-done.2.refs_3_.refs_13_.refs_18_ = bf16[4,16,1920]{2,1,0:T(8,128)(2,1)} collective-permute-done((bf16[4,16,1920]{2,1,0:T(8,128)(2,1)S(1)}, bf16[4,16,1920]{2,1,0:T(8,128)(2,1)}, u32[]{:S(2)}, u32[]{:S(2)}) %collective-permute-start.2) | collective-permute-done | bytes 245792 | tf_op jit(solution)/shard_map/ppermute | solution.py:332
  57.2 3.7 %interleave.2 = (bf16[1360,256]{1,0:T(8,128)(2,1)}, bf16[1280,256]{1,0:T(8,128)(2,1)}) custom-call(s32[2]{0:T(128)} %pad_add_fusion.pos, bf16[8,16,1920]{2,1,0:T(8,128)(2,1)} %copy-done, bf16[8,16,1920]{2,1,0:T(8,128)(2,1)} %copy-done.2, bf16[8,16,1920]{2,1,0:T(8,128)(2,1)} %copy-done.1, ...), custom_call_target="tpu_custom_call" | custom-call | tf_op jit(solution)/shard_map/interleave/pallas_call | solution.py:201
  60.8 3.2 %collective-permute-start.9 = (bf16[1360,256]{1,0:T(8,128)(2,1)}, bf16[1360,256]{1,0:T(8,128)(2,1)S(1)}, u32[]{:S(2)}, u32[]{:S(2)}) collective-permute-start(bf16[1360,256]{1,0:T(8,128)(2,1)} %get-tuple-element.49.refs_0_), channel_id=1, source_target_pairs={{0,24},{8,0},{16,8},{24,16},{1,25},{9,1},{17,9},{25,17},{2,26},{10... | collective-permute-start | bytes 2088968 | tf_op jit(solution)/shard_map/ppermute | solution.py:326
  64.1 2.0 %collective-permute-start.10 = (bf16[1280,256]{1,0:T(8,128)(2,1)}, bf16[1280,256]{1,0:T(8,128)(2,1)}, u32[]{:S(2)}, u32[]{:S(2)}) collective-permute-start(bf16[1280,256]{1,0:T(8,128)(2,1)} %get-tuple-element.53.refs_4_), channel_id=1, source_target_pairs={{0,32},{32,64},{64,96},{96,0},{1,33},{33,65},{65,97},{97,1},{2,34}... | collective-permute-start | bytes 1966088 | tf_op jit(solution)/shard_map/ppermute | solution.py:326
  66.1 3.9 %interleave.3 = (bf16[1632,256]{1,0:T(8,128)(2,1)}, bf16[1536,256]{1,0:T(8,128)(2,1)}) custom-call(s32[2]{0:T(128)} %pad_add_fusion.pos, bf16[8,16,1920]{2,1,0:T(8,128)(2,1)} %copy-done, bf16[8,16,1920]{2,1,0:T(8,128)(2,1)} %copy-done.2, bf16[8,16,1920]{2,1,0:T(8,128)(2,1)} %copy-done.1, ...), custom_call_target="tpu_custom_call" | custom-call | tf_op jit(solution)/shard_map/interleave/pallas_call | solution.py:201
  70.0 7.4 %collective-permute-done.11.refs_6_ = bf16[1280,256]{1,0:T(8,128)(2,1)} collective-permute-done((bf16[1280,256]{1,0:T(8,128)(2,1)}, bf16[1280,256]{1,0:T(8,128)(2,1)}, u32[]{:S(2)}, u32[]{:S(2)}) %collective-permute-start.11) | collective-permute-done | bytes 655392 | tf_op jit(solution)/shard_map/ppermute | solution.py:326
  77.4 1.2 collective-permute-done.10.refs_5_
  78.6 0.9 collective-permute-done.8.refs_1_
  79.5 2.2 %collective-permute-start.14 = (bf16[1632,256]{1,0:T(8,128)(2,1)}, bf16[1632,256]{1,0:T(8,128)(2,1)}, u32[]{:S(2)}, u32[]{:S(2)}) collective-permute-start(bf16[1632,256]{1,0:T(8,128)(2,1)} %get-tuple-element.61.refs_0_), channel_id=1, source_target_pairs={{0,24},{8,0},{16,8},{24,16},{1,25},{9,1},{17,9},{25,17},{2,26},{10... | collective-permute-start | bytes 2506760 | tf_op jit(solution)/shard_map/ppermute | solution.py:361
  81.6 0.5 collective-permute-start.15
  82.1 1.5 %collective-permute-start.13 = (bf16[1280,256]{1,0:T(8,128)(2,1)}, bf16[1280,256]{1,0:T(8,128)(2,1)}, u32[]{:S(2)}, u32[]{:S(2)}) collective-permute-start(bf16[1280,256]{1,0:T(8,128)(2,1)} %collective-permute-done.10.refs_5_), channel_id=1, source_target_pairs={{0,32},{32,64},{64,96},{96,0},{1,33},{33,65},{65,97},{97,1},{2,34}... | collective-permute-start | bytes 1966088 | tf_op jit(solution)/shard_map/ppermute | solution.py:360
  83.7 11.3 %collective-permute-done.13.refs_7_ = bf16[1280,256]{1,0:T(8,128)(2,1)} collective-permute-done((bf16[1280,256]{1,0:T(8,128)(2,1)}, bf16[1280,256]{1,0:T(8,128)(2,1)}, u32[]{:S(2)}, u32[]{:S(2)}) %collective-permute-start.13) | collective-permute-done | bytes 655392 | tf_op jit(solution)/shard_map/ppermute | solution.py:360
  95.0 2.9 %collective-permute-done.12.refs_3_ = bf16[1360,256]{1,0:T(8,128)(2,1)} collective-permute-done((bf16[1360,256]{1,0:T(8,128)(2,1)}, bf16[1360,256]{1,0:T(8,128)(2,1)}, u32[]{:S(2)}, u32[]{:S(2)}) %collective-permute-start.12) | collective-permute-done | bytes 696352 | tf_op jit(solution)/shard_map/ppermute | solution.py:360
  97.9 0.3 collective-permute-done.14.refs_2_
  98.2 2.9 %collective-permute-start.17 = (bf16[1632,256]{1,0:T(8,128)(2,1)}, bf16[1632,256]{1,0:T(8,128)(2,1)}, u32[]{:S(2)}, u32[]{:S(2)}) collective-permute-start(bf16[1632,256]{1,0:T(8,128)(2,1)} %collective-permute-done.14.refs_2_), channel_id=1, source_target_pairs={{0,24},{8,0},{16,8},{24,16},{1,25},{9,1},{17,9},{25,17},{2,26},{10... | collective-permute-start | bytes 2506760 | tf_op jit(solution)/shard_map/ppermute | solution.py:366
  101.1 1.5 %collective-permute-start.18 = (bf16[1536,256]{1,0:T(8,128)(2,1)}, bf16[1536,256]{1,0:T(8,128)(2,1)}, u32[]{:S(2)}, u32[]{:S(2)}) collective-permute-start(bf16[1536,256]{1,0:T(8,128)(2,1)} %get-tuple-element.63.refs_4_), channel_id=1, source_target_pairs={{0,32},{32,64},{64,96},{96,0},{1,33},{33,65},{65,97},{97,1},{2,34}... | collective-permute-start | bytes 2359304 | tf_op jit(solution)/shard_map/ppermute | solution.py:364
  102.7 1.7 %collective-permute-start.19 = (bf16[1536,256]{1,0:T(8,128)(2,1)}, bf16[1536,256]{1,0:T(8,128)(2,1)}, u32[]{:S(2)}, u32[]{:S(2)}) collective-permute-start(bf16[1536,256]{1,0:T(8,128)(2,1)} %collective-permute-done.15.refs_6_), channel_id=1, source_target_pairs={{0,96},{32,0},{64,32},{96,64},{1,97},{33,1},{65,33},{97,65},{2,98}... | collective-permute-start | bytes 2359304 | tf_op jit(solution)/shard_map/ppermute | solution.py:366
  104.4 3.9 %arrange_left.1 = (bf16[1024,128]{1,0:T(8,128)(2,1)}, bf16[1024,128]{1,0:T(8,128)(2,1)}, bf16[32,128]{1,0:T(8,128)(2,1)}, bf16[128,1024]{1,0:T(8,128)(2,1)}) custom-call(s32[2]{0:T(128)} %pad_add_fusion.pos, bf16[1360,256]{1,0:T(8,128)(2,1)} %get-tuple-element.49.refs_0_, bf16[1360,256]{1,0:T(8,128)(2,1)} %collective-permute-done.8.refs_1_, ...), custom_call_target="tpu_custom_call" | custom-call | tf_op jit(solution)/shard_map/arrange_left/pallas_call | solution.py:258
  108.3 16.8 %pair.2.refs_8_ = bf16[32,1280,128]{2,1,0:T(8,128)(2,1)} custom-call(bf16[1024,128]{1,0:T(8,128)(2,1)} %get-tuple-element.57.l1, bf16[1024,128]{1,0:T(8,128)(2,1)} %get-tuple-element.58.l2, bf16[128,1024]{1,0:T(8,128)(2,1)} %get-tuple-element.59.w_ref, bf16[32,128]{1,0:T(8,128)(2,1)} %get-tuple-element.60.n_ref, ...), custom_call_target="tpu_custom_call" | custom-call | tf_op jit(solution)/shard_map/pair/pallas_call | solution.py:304
  125.1 24.1 %pair.3 = bf16[32,1280,128]{2,1,0:T(8,128)(2,1)} custom-call(bf16[1024,128]{1,0:T(8,128)(2,1)} %get-tuple-element.57.l1, bf16[1024,128]{1,0:T(8,128)(2,1)} %get-tuple-element.58.l2, bf16[128,1024]{1,0:T(8,128)(2,1)} %get-tuple-element.59.w_ref, bf16[32,128]{1,0:T(8,128)(2,1)} %get-tuple-element.60.n_ref, ...), custom_call_target="tpu_custom_call", output_to_operand_aliasing={{}: (12, {})} | custom-call | tf_op jit(solution)/shard_map/pair/pallas_call | solution.py:304
  (36 shorter events, 0.3 us)
Async XLA Ops:
  27.6 22.0 %copy-start.3 = (bf16[8,16,1920]{2,1,0:T(8,128)(2,1)}, bf16[8,16,1920]{2,1,0:T(8,128)(2,1)S(1)}, u32[]{:S(2)}) copy-start(bf16[8,16,1920]{2,1,0:T(8,128)(2,1)S(1)} %get-tuple-element.65.refs_5_.refs_20_) | copy-start | bytes 1474564
  27.6 29.5 %copy-start = (bf16[8,16,1920]{2,1,0:T(8,128)(2,1)}, bf16[8,16,1920]{2,1,0:T(8,128)(2,1)S(1)}, u32[]{:S(2)}) copy-start(bf16[8,16,1920]{2,1,0:T(8,128)(2,1)S(1)} %get-tuple-element.66.refs_0_.refs_10_.refs_15_) | copy-start | bytes 1474564
  27.6 14.3 %collective-permute-start.5 = (bf16[8,16,1920]{2,1,0:T(8,128)(2,1)S(1)}, bf16[8,16,1920]{2,1,0:T(8,128)(2,1)S(1)}, u32[]{:S(2)}, u32[]{:S(2)}) collective-permute-start(bf16[8,16,1920]{2,1,0:T(8,128)(2,1)S(1)} %get-tuple-element.65.refs_5_.refs_20_), channel_id=1, source_target_pairs={{0,24},{8,0},{16,8},{24,16},{1,25},{9,1},{17,9},{25,17},{2,26},{10... | collective-permute-start | bytes 1474568 | tf_op jit(solution)/shard_map/ppermute | solution.py:326
  31.7 14.0 %collective-permute-start.4 = (bf16[8,16,1920]{2,1,0:T(8,128)(2,1)S(1)}, bf16[8,16,1920]{2,1,0:T(8,128)(2,1)S(1)}, u32[]{:S(2)}, u32[]{:S(2)}) collective-permute-start(bf16[8,16,1920]{2,1,0:T(8,128)(2,1)S(1)} %get-tuple-element.65.refs_5_.refs_20_), channel_id=1, source_target_pairs={{0,8},{8,16},{16,24},{24,0},{1,9},{9,17},{17,25},{25,1},{2,10},{10... | collective-permute-start | bytes 1474568 | tf_op jit(solution)/shard_map/ppermute | solution.py:326
  31.7 14.1 %collective-permute-start.1 = (bf16[8,16,1920]{2,1,0:T(8,128)(2,1)S(1)}, bf16[8,16,1920]{2,1,0:T(8,128)(2,1)S(1)}, u32[]{:S(2)}, u32[]{:S(2)}) collective-permute-start(bf16[8,16,1920]{2,1,0:T(8,128)(2,1)S(1)} %get-tuple-element.66.refs_0_.refs_10_.refs_15_), channel_id=1, source_target_pairs={{0,96},{32,0},{64,32},{96,64},{1,97},{33,1},{65,33},{97,65},{2,98}... | collective-permute-start | bytes 1474568 | tf_op jit(solution)/shard_map/ppermute | solution.py:326
  34.5 14.2 %collective-permute-start = (bf16[8,16,1920]{2,1,0:T(8,128)(2,1)S(1)}, bf16[8,16,1920]{2,1,0:T(8,128)(2,1)S(1)}, u32[]{:S(2)}, u32[]{:S(2)}) collective-permute-start(bf16[8,16,1920]{2,1,0:T(8,128)(2,1)S(1)} %get-tuple-element.66.refs_0_.refs_10_.refs_15_), channel_id=1, source_target_pairs={{0,32},{32,64},{64,96},{96,0},{1,33},{33,65},{65,97},{97,1},{2,34}... | collective-permute-start | bytes 1474568 | tf_op jit(solution)/shard_map/ppermute | solution.py:326
  41.9 7.7 %copy-start.4 = (bf16[8,16,1920]{2,1,0:T(8,128)(2,1)}, bf16[8,16,1920]{2,1,0:T(8,128)(2,1)S(1)}, u32[]{:S(2)}) copy-start(bf16[8,16,1920]{2,1,0:T(8,128)(2,1)S(1)} %collective-permute-done.5.refs_7_.refs_22_) | copy-start | bytes 1474564
  42.0 8.3 %collective-permute-start.7 = (bf16[4,16,1920]{2,1,0:T(8,128)(2,1)S(1)}, bf16[4,16,1920]{2,1,0:T(8,128)(2,1)}, u32[]{:S(2)}, u32[]{:S(2)}) collective-permute-start(bf16[4,16,1920]{2,1,0:T(8,128)(2,1)S(1)} %slice.29), channel_id=1, source_target_pairs={{0,24},{8,0},{16,8},{24,16},{1,25},{9,1},{17,9},{25,17},{2,26},{10... | collective-permute-start | bytes 737288 | tf_op jit(solution)/shard_map/ppermute | solution.py:332
  45.7 3.9 %copy-start.5 = (bf16[8,16,1920]{2,1,0:T(8,128)(2,1)}, bf16[8,16,1920]{2,1,0:T(8,128)(2,1)S(1)}, u32[]{:S(2)}) copy-start(bf16[8,16,1920]{2,1,0:T(8,128)(2,1)S(1)} %collective-permute-done.4.refs_6_.refs_21_) | copy-start | bytes 1474564
  45.7 7.6 %collective-permute-start.6 = (bf16[4,16,1920]{2,1,0:T(8,128)(2,1)S(1)}, bf16[4,16,1920]{2,1,0:T(8,128)(2,1)}, u32[]{:S(2)}, u32[]{:S(2)}) collective-permute-start(bf16[4,16,1920]{2,1,0:T(8,128)(2,1)S(1)} %slice.28), channel_id=1, source_target_pairs={{0,8},{8,16},{16,24},{24,0},{1,9},{9,17},{17,25},{25,1},{2,10},{10... | collective-permute-start | bytes 737288 | tf_op jit(solution)/shard_map/ppermute | solution.py:332
  45.8 11.3 %copy-start.1 = (bf16[8,16,1920]{2,1,0:T(8,128)(2,1)}, bf16[8,16,1920]{2,1,0:T(8,128)(2,1)S(1)}, u32[]{:S(2)}) copy-start(bf16[8,16,1920]{2,1,0:T(8,128)(2,1)S(1)} %collective-permute-done.1.refs_2_.refs_12_.refs_17_) | copy-start | bytes 1474564
  45.9 7.5 %collective-permute-start.3 = (bf16[4,16,1920]{2,1,0:T(8,128)(2,1)S(1)}, bf16[4,16,1920]{2,1,0:T(8,128)(2,1)}, u32[]{:S(2)}, u32[]{:S(2)}) collective-permute-start(bf16[4,16,1920]{2,1,0:T(8,128)(2,1)S(1)} %slice.26), channel_id=1, source_target_pairs={{0,96},{32,0},{64,32},{96,64},{1,97},{33,1},{65,33},{97,65},{2,98}... | collective-permute-start | bytes 737288 | tf_op jit(solution)/shard_map/ppermute | solution.py:332
  48.7 0.8 copy-start.2
  49.6 7.6 %collective-permute-start.2 = (bf16[4,16,1920]{2,1,0:T(8,128)(2,1)S(1)}, bf16[4,16,1920]{2,1,0:T(8,128)(2,1)}, u32[]{:S(2)}, u32[]{:S(2)}) collective-permute-start(bf16[4,16,1920]{2,1,0:T(8,128)(2,1)S(1)} %slice.25), channel_id=1, source_target_pairs={{0,32},{32,64},{64,96},{96,0},{1,33},{33,65},{65,97},{97,1},{2,34}... | collective-permute-start | bytes 737288 | tf_op jit(solution)/shard_map/ppermute | solution.py:332
  60.8 17.8 %collective-permute-start.9 = (bf16[1360,256]{1,0:T(8,128)(2,1)}, bf16[1360,256]{1,0:T(8,128)(2,1)S(1)}, u32[]{:S(2)}, u32[]{:S(2)}) collective-permute-start(bf16[1360,256]{1,0:T(8,128)(2,1)} %get-tuple-element.49.refs_0_), channel_id=1, source_target_pairs={{0,24},{8,0},{16,8},{24,16},{1,25},{9,1},{17,9},{25,17},{2,26},{10... | collective-permute-start | bytes 2088968 | tf_op jit(solution)/shard_map/ppermute | solution.py:326
  64.1 15.4 %collective-permute-start.8 = (bf16[1360,256]{1,0:T(8,128)(2,1)}, bf16[1360,256]{1,0:T(8,128)(2,1)}, u32[]{:S(2)}, u32[]{:S(2)}) collective-permute-start(bf16[1360,256]{1,0:T(8,128)(2,1)} %get-tuple-element.49.refs_0_), channel_id=1, source_target_pairs={{0,8},{8,16},{16,24},{24,0},{1,9},{9,17},{17,25},{25,1},{2,10},{10... | collective-permute-start | bytes 2088968 | tf_op jit(solution)/shard_map/ppermute | solution.py:326
  64.1 13.3 %collective-permute-start.11 = (bf16[1280,256]{1,0:T(8,128)(2,1)}, bf16[1280,256]{1,0:T(8,128)(2,1)}, u32[]{:S(2)}, u32[]{:S(2)}) collective-permute-start(bf16[1280,256]{1,0:T(8,128)(2,1)} %get-tuple-element.53.refs_4_), channel_id=1, source_target_pairs={{0,96},{32,0},{64,32},{96,64},{1,97},{33,1},{65,33},{97,65},{2,98}... | collective-permute-start | bytes 1966088 | tf_op jit(solution)/shard_map/ppermute | solution.py:326
  64.1 14.5 %collective-permute-start.10 = (bf16[1280,256]{1,0:T(8,128)(2,1)}, bf16[1280,256]{1,0:T(8,128)(2,1)}, u32[]{:S(2)}, u32[]{:S(2)}) collective-permute-start(bf16[1280,256]{1,0:T(8,128)(2,1)} %get-tuple-element.53.refs_4_), channel_id=1, source_target_pairs={{0,32},{32,64},{64,96},{96,0},{1,33},{33,65},{65,97},{97,1},{2,34}... | collective-permute-start | bytes 1966088 | tf_op jit(solution)/shard_map/ppermute | solution.py:326
  78.6 25.8 %copy-start.6 = (bf16[1360,256]{1,0:T(8,128)(2,1)}, bf16[1360,256]{1,0:T(8,128)(2,1)S(1)}, u32[]{:S(2)}) copy-start(bf16[1360,256]{1,0:T(8,128)(2,1)S(1)} %collective-permute-done.9.refs_2_) | copy-start | bytes 2088964
  79.5 18.8 %collective-permute-start.14 = (bf16[1632,256]{1,0:T(8,128)(2,1)}, bf16[1632,256]{1,0:T(8,128)(2,1)}, u32[]{:S(2)}, u32[]{:S(2)}) collective-permute-start(bf16[1632,256]{1,0:T(8,128)(2,1)} %get-tuple-element.61.refs_0_), channel_id=1, source_target_pairs={{0,24},{8,0},{16,8},{24,16},{1,25},{9,1},{17,9},{25,17},{2,26},{10... | collective-permute-start | bytes 2506760 | tf_op jit(solution)/shard_map/ppermute | solution.py:361
  81.6 16.3 %collective-permute-start.15 = (bf16[1536,256]{1,0:T(8,128)(2,1)}, bf16[1536,256]{1,0:T(8,128)(2,1)}, u32[]{:S(2)}, u32[]{:S(2)}) collective-permute-start(bf16[1536,256]{1,0:T(8,128)(2,1)} %get-tuple-element.63.refs_4_), channel_id=1, source_target_pairs={{0,96},{32,0},{64,32},{96,64},{1,97},{33,1},{65,33},{97,65},{2,98}... | collective-permute-start | bytes 2359304 | tf_op jit(solution)/shard_map/ppermute | solution.py:361
  82.1 15.8 %collective-permute-start.12 = (bf16[1360,256]{1,0:T(8,128)(2,1)}, bf16[1360,256]{1,0:T(8,128)(2,1)}, u32[]{:S(2)}, u32[]{:S(2)}) collective-permute-start(bf16[1360,256]{1,0:T(8,128)(2,1)} %collective-permute-done.8.refs_1_), channel_id=1, source_target_pairs={{0,8},{8,16},{16,24},{24,0},{1,9},{9,17},{17,25},{25,1},{2,10},{10... | collective-permute-start | bytes 2088968 | tf_op jit(solution)/shard_map/ppermute | solution.py:360
  82.1 12.9 %collective-permute-start.13 = (bf16[1280,256]{1,0:T(8,128)(2,1)}, bf16[1280,256]{1,0:T(8,128)(2,1)}, u32[]{:S(2)}, u32[]{:S(2)}) collective-permute-start(bf16[1280,256]{1,0:T(8,128)(2,1)} %collective-permute-done.10.refs_5_), channel_id=1, source_target_pairs={{0,32},{32,64},{64,96},{96,0},{1,33},{33,65},{65,97},{97,1},{2,34}... | collective-permute-start | bytes 1966088 | tf_op jit(solution)/shard_map/ppermute | solution.py:360
  97.9 27.2 %collective-permute-start.16 = (bf16[1632,256]{1,0:T(8,128)(2,1)}, bf16[1632,256]{1,0:T(8,128)(2,1)}, u32[]{:S(2)}, u32[]{:S(2)}) collective-permute-start(bf16[1632,256]{1,0:T(8,128)(2,1)} %get-tuple-element.61.refs_0_), channel_id=1, source_target_pairs={{0,8},{8,16},{16,24},{24,0},{1,9},{9,17},{17,25},{25,1},{2,10},{10... | collective-permute-start | bytes 2506760 | tf_op jit(solution)/shard_map/ppermute | solution.py:364
  98.2 26.9 %collective-permute-start.17 = (bf16[1632,256]{1,0:T(8,128)(2,1)}, bf16[1632,256]{1,0:T(8,128)(2,1)}, u32[]{:S(2)}, u32[]{:S(2)}) collective-permute-start(bf16[1632,256]{1,0:T(8,128)(2,1)} %collective-permute-done.14.refs_2_), channel_id=1, source_target_pairs={{0,24},{8,0},{16,8},{24,16},{1,25},{9,1},{17,9},{25,17},{2,26},{10... | collective-permute-start | bytes 2506760 | tf_op jit(solution)/shard_map/ppermute | solution.py:366
  101.1 23.9 %collective-permute-start.18 = (bf16[1536,256]{1,0:T(8,128)(2,1)}, bf16[1536,256]{1,0:T(8,128)(2,1)}, u32[]{:S(2)}, u32[]{:S(2)}) collective-permute-start(bf16[1536,256]{1,0:T(8,128)(2,1)} %get-tuple-element.63.refs_4_), channel_id=1, source_target_pairs={{0,32},{32,64},{64,96},{96,0},{1,33},{33,65},{65,97},{97,1},{2,34}... | collective-permute-start | bytes 2359304 | tf_op jit(solution)/shard_map/ppermute | solution.py:364
  102.7 22.4 %collective-permute-start.19 = (bf16[1536,256]{1,0:T(8,128)(2,1)}, bf16[1536,256]{1,0:T(8,128)(2,1)}, u32[]{:S(2)}, u32[]{:S(2)}) collective-permute-start(bf16[1536,256]{1,0:T(8,128)(2,1)} %collective-permute-done.15.refs_6_), channel_id=1, source_target_pairs={{0,96},{32,0},{64,32},{96,64},{1,97},{33,1},{65,33},{97,65},{2,98}... | collective-permute-start | bytes 2359304 | tf_op jit(solution)/shard_map/ppermute | solution.py:366

commit v4 on v3

v4 whole, which is shorter than its diff:
```python
import jax
import jax.numpy as jnp
from jax import lax
from jax.experimental import pallas as pl
from jax.experimental.pallas import tpu as pltpu
from jax.sharding import Mesh
from jax.sharding import PartitionSpec as P

RD = 32
CHUNK = 256
GROUP = 32
TILE = 128
COLUMN = ("yh", "yl", "core")
PLANE = ("x", "z", "yh")
EVERY = ("x", "z", "yh", "yl", "core")
f32 = jnp.float32
bf16 = jnp.bfloat16


def vmem(mib=63):
    return pltpu.CompilerParams(vmem_limit_bytes=mib * 2**20)


def whole(*shape):
    return pl.BlockSpec(shape, lambda *_: (0,) * len(shape))


def turned(bias_ref):
    return jnp.broadcast_to(bias_ref[...], (8, bias_ref.shape[1])).T[:, :1]


def standardize(v, gain, bias):
    v = v.astype(f32)
    v = v - jnp.mean(v, axis=-1, keepdims=True)
    spread = jnp.mean(v * v, axis=-1, keepdims=True)
    return (v * lax.rsqrt(spread + 1e-05) * gain + bias).astype(bf16)


def affine(w_ref, bias, normed, mask):
    y = lax.dot_general(w_ref[...], normed, (((1,), (1,)), ((), ())), preferred_element_type=f32)
    return (y + bias) * mask


def one_hot(rows, columns, where):
    row = lax.broadcasted_iota(jnp.int32, (rows, columns), 0)
    column = lax.broadcasted_iota(jnp.int32, (rows, columns), 1)
    return jnp.where(where(row, column), 1.0, 0.0).astype(bf16)


def move(values, choose):
    return jnp.dot(values, choose, preferred_element_type=f32).astype(bf16)


def project_left(x, mask, gain, bias, weight, shift):
    features = x.shape[1]
    width = weight.shape[0]
    rows = RD * 32
    sub = 512

    def kernel(x_ref, m_ref, g_ref, s_ref, w_ref, b_ref, out_ref, mask_ref):
        b = turned(b_ref)
        y = []
        for part in range(rows // sub):
            at = slice(part * sub, (part + 1) * sub)
            normed = standardize(x_ref[at, :], g_ref[...], s_ref[...])
            y.append(affine(w_ref, b, normed, m_ref[:, at]))
        y = jnp.concatenate(y, axis=1)
        y = jnp.concatenate([y, jnp.broadcast_to(m_ref[...], (16, rows))], axis=0).astype(bf16)

        def regroup(src, dst):
            return src == ((dst >> 3) & 3) * 64 + (dst >> 5) * 8 + (dst & 7)

        choose = one_hot(256, 256, regroup)
        y = [move(y[:, k * 256 : (k + 1) * 256], choose) for k in range(4)]
        for device in range(8):
            tile = jnp.concatenate([t[:, device * 32 : (device + 1) * 32] for t in y], axis=1)
            out_ref[device] = tile[:32]
            mask_ref[device] = tile[32:]

    return pl.pallas_call(
        kernel,
        grid=(1,),
        out_shape=(
            jax.ShapeDtypeStruct((8, 32, TILE), bf16),
            jax.ShapeDtypeStruct((8, 16, TILE), bf16),
        ),
        in_specs=[
            pl.BlockSpec((rows, features), lambda _: (0, 0)),
            pl.BlockSpec((1, rows), lambda _: (0, 0)),
            whole(1, features),
            whole(1, features),
            whole(width, features),
            whole(1, width),
        ],
        out_specs=(whole(8, 32, TILE), whole(8, 16, TILE)),
        compiler_params=vmem(),
        name="project_left",
    )(x, mask, gain, bias, weight, shift)


def project_right(x, mask, gain, bias, weight, shift, left, left_mask):
    rows, features = x.shape
    quarter = rows // 4
    width = weight.shape[0]
    sub = 640
    total = quarter + 2 * TILE

    def kernel(x_ref, m_ref, g_ref, s_ref, w_ref, b_ref, l_ref, n_ref, out_ref):
        b = turned(b_ref)
        for part in range(quarter // sub):
            at = slice(part * sub, (part + 1) * sub)
            normed = standardize(x_ref[at, :], g_ref[...], s_ref[...])
            y = affine(w_ref, b, normed, m_ref[0, :, at]).astype(bf16)
            out_ref[0, 0, :, at] = y
            out_ref[1, 0, :, at] = y
        m = [m_ref[0, :, k * TILE : (k + 1) * TILE] for k in range(quarter // TILE)]
        for yh in range(2):
            device = yh * 4 + pl.program_id(0)
            tile = jnp.concatenate(m + [jnp.zeros((16 - len(m), TILE), f32)], axis=0)
            out_ref[yh, 0, :16, quarter : quarter + TILE] = tile.astype(bf16)
            out_ref[yh, 0, 16:, quarter : quarter + TILE] = n_ref[device]
            out_ref[yh, 0, :, quarter + TILE :] = l_ref[device]

    return pl.pallas_call(
        kernel,
        grid=(4,),
        out_shape=jax.ShapeDtypeStruct((2, 4, width, total), bf16),
        in_specs=[
            pl.BlockSpec((quarter, features), lambda q: (q, 0)),
            pl.BlockSpec((1, 1, quarter), lambda q: (q, 0, 0)),
            whole(1, features),
            whole(1, features),
            whole(width, features),
            whole(1, width),
            whole(*left.shape),
            whole(*left_mask.shape),
        ],
        out_specs=pl.BlockSpec((2, 1, width, total), lambda q: (0, q, 0, 0)),
        compiler_params=vmem(),
        name="project_right",
    )(x, mask.reshape(4, 1, quarter), gain, bias, weight, shift, left, left_mask)


def ring(step):
    return [(i, (i + step) % 4) for i in range(4)]


def interleave(position, first, second, columns, start, chunks, w_out=None):
    tiles = CHUNK // TILE
    sizes = (8, 8, 8, 4, 4)
    heights = (544, 512)
    extra = 0 if w_out is not None else 144
    width = 32
    mask_tile = columns // TILE

    def by_row(ins, lane):
        own, before, after, low, high = ins
        at = slice(lane * TILE, (lane + 1) * TILE)
        parts = [own[:, :, at], before[:, :, at], after[:, :, at], low[:, :, at], high[:, :, at]]
        near = jnp.swapaxes(jnp.concatenate(parts[:2], axis=0), 0, 1)
        away = jnp.swapaxes(jnp.concatenate(parts[2:], axis=0), 0, 1)
        return jnp.concatenate([near, away], axis=1).reshape(512, TILE)

    def kernel(pos, *refs):
        main, masks, rest, outs = refs[:10], refs[10:15], refs[15:-3], refs[-3:]
        mask_rows = by_row(masks, 0)
        for chunk in range(chunks):
            for half in range(2):
                base = chunk * heights[half]
                for lane in range(tiles):
                    at = slice(lane * TILE, (lane + 1) * TILE)
                    rows = by_row(main[5 * half : 5 * half + 5], chunk * tiles + lane)
                    outs[half][base : base + 512, at] = rows
                    if half == 0:
                        row = ((start + chunk) * tiles + lane) * 32
                        outs[0][base + 512 : base + 544, at] = mask_rows[row : row + 32, :]
        if w_out is not None:
            w = rest[0][...].reshape(width, width, TILE)
            outs[2][...] = jnp.swapaxes(w, 0, 1).reshape(width * width, TILE).T
            return

        def mine(group):
            def pick(src, dst):
                place = ((dst >> 3) & 3) * 32 + pos[1] * 8 + (dst & 7)
                return (src == place) & ((dst >> 5) == group)

            return one_hot(TILE, TILE, pick)

        choose = [mine(group) for group in range(4)]
        left_masks, *lefts = [by_row(rest[5 * k : 5 * k + 5], 0) for k in range(3)]
        for lane, rows in enumerate(lefts):
            at = slice(lane * TILE, (lane + 1) * TILE)
            parts = [rows[g * 128 : (g + 1) * 128] for g in range(4)]
            parts = [jnp.dot(v, c, preferred_element_type=f32) for v, c in zip(parts, choose)]
            outs[2][:128, at] = sum(parts[1:], parts[0]).astype(bf16)
            outs[2][128:, at] = move(left_masks[lane * 16 : (lane + 1) * 16], choose[0])
        outs[1][chunks * 512 :, :] = outs[2][...]

    def blocks(m):
        span = chunks * CHUNK
        if start * CHUNK % span == 0:
            return pl.BlockSpec((m, 16, span), lambda _, pos: (0, 0, start * CHUNK // span))
        return pl.BlockSpec((pl.Element(m), pl.Element(16), pl.Element(span)), lambda _, pos: (0, 0, start * CHUNK))

    def tile_blocks(m, tile):
        return pl.BlockSpec((m, 16, TILE), lambda _, pos: (0, 0, tile))

    specs = [blocks(m) for m in sizes] * 2 + [tile_blocks(m, mask_tile) for m in sizes]
    args = (*first, *second, *first)
    shapes = [(chunks * heights[0], CHUNK), (chunks * heights[1] + extra, CHUNK)]
    if w_out is None:
        specs += [tile_blocks(m, mask_tile + k) for k in (0, 2, 1) for m in sizes]
        args += (*second, *second, *second)
        shapes.append((extra, CHUNK))
    else:
        specs.append(whole(*w_out.shape))
        args += (w_out,)
        shapes.append((w_out.shape[1], width * width))
    return pl.pallas_call(
        kernel,
        grid_spec=pltpu.PrefetchScalarGridSpec(
            num_scalar_prefetch=1,
            grid=(1,),
            in_specs=specs,
            out_specs=tuple(whole(*shape) for shape in shapes),
        ),
        out_shape=tuple(jax.ShapeDtypeStruct(shape, bf16) for shape in shapes),
        compiler_params=vmem(),
        name="interleave",
    )(position, *args)


def arrange_left(position, own, before, after, far, base):
    height = own.shape[0]

    def kernel(pos, *refs):
        ins, out_ref = refs[:4], refs[4]

        def sequences(rows, lane):
            return [r[rows, lane * TILE : (lane + 1) * TILE] for r in ins]

        def turn(choose, values):
            over = (((1,), (1,)), ((), ()))
            return lax.dot_general(choose, values, over, preferred_element_type=f32).astype(bf16)

        choose = one_hot(32, TILE, lambda row, lane: lane == (row & 3) * 32 + pos[0] * 8 + (row >> 2))
        held = []
        for lane in range(2):
            for c in range(4):
                values = jnp.concatenate(sequences(slice(c * 32, c * 32 + 32), lane), axis=0)
                held.append(turn(choose, values))

        def regroup(dst, src):
            c = dst & 31
            return src == (c >> 4) * 128 + (c & 3) * 32 + (dst >> 5) * 4 + ((c >> 2) & 3)

        held = move(one_hot(256, 256, regroup), jnp.concatenate(held, axis=0))
        swap = one_hot(128, 128, lambda k, to: to == ((k >> 3) & 3) * 32 + (k >> 5) * 8 + (k & 7))
        out_ref[:256, :] = move(held, swap)
        out_ref[256:512, :] = held
        masks = [sequences(slice(128, 144), lane) for lane in range(2)]
        masks = [masks[lane][place] for place in range(4) for lane in range(2)]
        choose = one_hot(16, TILE, lambda row, lane: lane == pos[0] * 8 + row)
        out_ref[512:, :] = move(turn(choose, jnp.concatenate(masks, axis=0)), swap)

    part = pl.BlockSpec((pl.Element(height), pl.Element(CHUNK)), lambda _, pos: (base, 0))
    return pl.pallas_call(
        kernel,
        grid_spec=pltpu.PrefetchScalarGridSpec(
            num_scalar_prefetch=1,
            grid=(1,),
            in_specs=[whole(*own.shape), part, part, whole(*far.shape)],
            out_specs=whole(528, 128),
        ),
        out_shape=jax.ShapeDtypeStruct((528, 128), bf16),
        compiler_params=vmem(),
        name="arrange_left",
    )(position, own, before, after, far)


def pair(left, weight, first, second, start, chunks, result, columns):
    out_width = weight.shape[0]
    earlier = () if result is None else (result,)

    def kernel(left_ref, w_ref, *refs):
        ins = refs[:8]
        out_ref, outer, scale, l1, l2, row_mask = refs[-6:]

        @pl.when(pl.program_id(0) == 0)
        def _():
            for device in range(4):
                at = slice(device * 256, (device + 1) * 256)
                l1[at, :] = left_ref[device, :256, :]
                l2[at, :] = left_ref[device, 256:512, :]
                row_mask[device * 8 : (device + 1) * 8, :] = left_ref[device, 512:, :].astype(f32)[:8]

        def sequences(half, row):
            at = slice(row * 32, row * 32 + 32)
            return jnp.concatenate([r[at, :] for r in ins[4 * half : 4 * half + 4]], axis=0)

        count = jnp.dot(row_mask[...].astype(bf16), sequences(0, 16), preferred_element_type=f32)
        scale[...] = 1.0 / (0.001 + count)

        def rows_of(group, _):
            at = pl.ds(pl.multiple_of(group * (GROUP * 32), GROUP * 32), GROUP * 32)
            for e in range(32):
                left = (l1, l2)[e // 16][at, :]
                prod = jnp.dot(left, sequences(e // 16, e % 16), preferred_element_type=f32).astype(bf16)
                for i in range(GROUP):
                    outer[i, e * 32 : (e + 1) * 32, :] = prod[i * 32 : (i + 1) * 32, :]
            part = scale[pl.ds(pl.multiple_of(group * GROUP, GROUP), GROUP), :]
            for i in range(GROUP):
                mixed = jnp.dot(w_ref[...], outer[i], preferred_element_type=f32)
                out_ref[group * GROUP + i] = (mixed * part[i : i + 1, :]).T.astype(bf16)
            return 0

        lax.fori_loop(0, RD // GROUP, rows_of, 0)

    blocks = [pl.BlockSpec((544, t.shape[1]), lambda j: (j, 0)) for t in first]
    blocks += [pl.BlockSpec((512, t.shape[1]), lambda j: (j, 0)) for t in second]
    return pl.pallas_call(
        kernel,
        grid=(chunks,),
        out_shape=jax.ShapeDtypeStruct((RD, columns, out_width), bf16),
        in_specs=[whole(*left.shape), whole(*weight.shape)]
        + blocks
        + [pl.BlockSpec(memory_space=pl.ANY)] * len(earlier),
        out_specs=pl.BlockSpec((RD, CHUNK, out_width), lambda j: (0, start + j, 0)),
        scratch_shapes=[
            pltpu.VMEM((GROUP, 1024, CHUNK), bf16),
            pltpu.VMEM((RD, CHUNK), f32),
            pltpu.VMEM((1024, 128), bf16),
            pltpu.VMEM((1024, 128), bf16),
            pltpu.VMEM((RD, 128), f32),
        ],
        input_output_aliases={10: 0} if earlier else {},
        compiler_params=vmem(),
        name="pair",
    )(left, weight, *first, *second, *earlier)


def send_both(blocks):
    return [
        (lax.ppermute(block, axis, ring(1)), lax.ppermute(block, axis, ring(-1))) for block, axis in blocks
    ]


def send_on(parts):
    return [
        (lax.ppermute(low, axis, ring(1)), lax.ppermute(high, axis, ring(-1))) for (low, high), axis in parts
    ]


def on_device(x, mask, gain, bias, w_left, b_left, w_right, b_right, w_out):
    columns = x.shape[1] // 4
    width = w_left.shape[1]
    chunks = columns // CHUNK
    together = lax.optimization_barrier

    narrow = ("yl", "core")
    position = jnp.stack([lax.axis_index(axis) for axis in ("x", "z")]).astype(jnp.int32)
    norm = gain[None], bias[None]
    left = project_left(x[0], mask, *norm, w_left.T, b_left[None])
    right = project_right(x[0], mask, *norm, w_right.T, b_right[None], *left)
    right = lax.all_to_all(right.reshape(8, width, -1), COLUMN, 0, 0, tiled=True)

    halves = (
        right[:, :16, : columns + TILE],
        jnp.concatenate([right[:, 16:], right[:, :16, columns + TILE :]], axis=2),
    )
    got = send_both(((halves[0], "x"), (halves[1], "z")))
    far = send_on([((before[:4], after[4:]), axis) for (before, after), axis in zip(got, "xz")])
    held = [(halves[h], *got[h], *far[h]) for h in range(2)]

    *early, left = interleave(position, *held, columns, 0, 2)
    *late, weight = interleave(position, *held, columns, 2, chunks - 2, w_out)
    left_far = lax.ppermute(left, "x", ring(2))
    got = send_both(((early[0], "z"), (early[1], "x")))
    got, late, left_far = together((got, late, left_far))
    far = [lax.ppermute(before, axis, ring(1)) for (before, _), axis in zip(got, "zx")]
    after = [lax.ppermute(block, axis, ring(-1)) for block, axis in zip(late, "zx")]
    left = arrange_left(position, left, *got[1], left_far, 2 * 512)
    left = lax.all_gather(left, narrow, axis=0)
    far, late, left = together((far, late, left))
    early = [(early[h], *got[h], far[h]) for h in range(2)]
    before = [lax.ppermute(block, axis, ring(1)) for block, axis in zip(late, "zx")]
    left, after = together((left, after))
    far = [lax.ppermute(block, axis, ring(-1)) for block, axis in zip(after, "zx")]
    late = [(late[h], before[h], after[h], far[h]) for h in range(2)]

    result = pair(left, weight, *early, 0, 2, None, columns)
    return pair(left, weight, *late, 2, chunks - 2, result, columns)


def solution(mesh):
    split = Mesh(mesh.devices.reshape(4, 4, 2, 2, 2), EVERY)
    placed = (P(EVERY, None, None), P(EVERY, None)) + (P(),) * 7
    return jax.shard_map(
        on_device,
        mesh=split,
        in_specs=placed,
        out_specs=P(PLANE, ("yl", "core"), None),
        check_vma=False,
    )
```

time: 150 us -> 138 us (0.920)
  waiting for transfers between devices: 38.3 us -> 21.3 us
  blocking collectives: 19.9 us -> 25.1 us
  local copies, waits for them, and re-layouts: 1 us -> 2.57 us
    ppermute x2, waiting for transfers between devices: 14.2 us -> 0.69 us  [on_device(): lax.ppermute(before, axis, ring(1))]
    ppermute x4, waiting for transfers between devices: 14.8 us -> 5.84 us  [send_both(): lax.ppermute(block, axis, ring(-1))]
    all_gather x0 -> x1, blocking collectives: none -> 7.3 us  [on_device(): left = lax.all_gather(left, narrow, axis=0)]
    ppermute x0 -> x1, waiting for transfers between devices: none -> 4.92 us  [on_device(): left_far = lax.ppermute(left, 'x', ring(2))]
    ppermute x2, waiting for transfers between devices: 6.86 us -> 4.57 us  [send_on(): lax.ppermute(low, axis, ring(1))]
    ppermute x4, starting transfers between devices: 7.22 us -> 9.42 us  [on_device(): lax.ppermute(block, axis, ring(-1))]
    all_to_all x1, blocking collectives: 19.9 us -> 17.8 us  [on_device(): lax.all_to_all(right.reshape(8, width, -1), COLUMN, 0, 0, tiled=True)]
    ppermute x2, waiting for transfers between devices: 0.01 us -> 1.63 us  [send_on(): lax.ppermute(high, axis, ring(-1))]
  transfers between devices with their start and end apart: 20 -> 21, of which waited for: 9 -> 9; matrix products, arithmetic and copies ran while one was open for 0% -> 1% of each run, Pallas kernels for 16% -> 17%
where the time goes in v4:
time: 138 us
  Pallas kernels  58.9 us (43%)
  starting transfers between devices  29 us (21%)
  blocking collectives  25.1 us (18%)
  waiting for transfers between devices  21.3 us (15%)
  local copies, waits for them, and re-layouts  2.57 us (2%)
    pallas_call x2, Pallas kernels, pair(): pl.pallas_call(kernel, grid=(chunks,), out_shape=jax.ShapeDtypeStruct((RD...  40.8 us
    all_to_all x1, blocking collectives, on_device(): lax.all_to_all(right.reshape(8, width, -1), COLUMN, 0, 0, tiled=True)  17.8 us
    ppermute x4, starting transfers between devices, send_both(): lax.ppermute(block, axis, ring(-1))  10.2 us
    ppermute x4, starting transfers between devices, on_device(): lax.ppermute(block, axis, ring(-1))  9.42 us
    pallas_call x2, Pallas kernels, interleave(): pl.pallas_call(kernel, grid_spec=pltpu.PrefetchScalarGridSpec(num_scalar_...  7.56 us
    all_gather x1, blocking collectives, on_device(): left = lax.all_gather(left, narrow, axis=0)  7.3 us
    ppermute x2, starting transfers between devices, send_on(): lax.ppermute(high, axis, ring(-1))  6.59 us
    ppermute x4, waiting for transfers between devices, send_both(): lax.ppermute(block, axis, ring(-1))  5.84 us
  transfers between devices with their start and end apart: 21, of which 9 were waited for; matrix products, arithmetic and copies ran while one was open for 1% of the time, Pallas kernels for 17%

profile of v4, /device:TPU:0, one launch (start us, length us, event | category | flops | bytes accessed | tf_op | source)
XLA Modules:
  0.0 137.7 jit_solution(2756446429352446527)
XLA Ops:
  0.0 2.5 %project_left.1 = (bf16[8,32,128]{2,1,0:T(8,128)(2,1)}, bf16[8,16,128]{2,1,0:T(8,128)(2,1)}) custom-call(bf16[5120,256]{1,0:T(8,128)(2,1)} %bitcast.12, f32[1,5120]{1,0:T(1,128)} %m_ref.1, f32[1,256]{1,0:T(1,128)} %bitcast.20, f32[1,256]{1,0:T(1,128)} %bitcast.22, bf16[32,256]{1,0:T(8,128)(2,1)} %bitcast.18, f32[1,32]{1,0:T(1,128)} %bitcast.24), custom_call_target="tpu_custom_call" | custom-call | tf_op jit(solution)/shard_map/project_left/pallas_call | solution.py:80
  2.5 5.1 %project_right.1 = bf16[2,4,32,1536]{3,2,1,0:T(8,128)(2,1)} custom-call(bf16[5120,256]{1,0:T(8,128)(2,1)} %bitcast.13, f32[4,1,1280]{2,1,0:T(1,128)} %bitcast.17, f32[1,256]{1,0:T(1,128)} %bitcast.21, f32[1,256]{1,0:T(1,128)} %bitcast.23, bf16[32,256]{1,0:T(8,128)(2,1)} %bitcast.19, f32[1,32]{1,0:T(1,128)} %bitcast.25, ...), custom_call_target="tpu_custom_call" | custom-call | tf_op jit(solution)/shard_map/project_right/pallas_call | solution.py:124
  7.6 17.8 %all_to_all.5 = bf16[8,32,1536]{2,1,0:T(8,128)(2,1)S(1)} all-to-all(bf16[8,32,1536]{2,1,0:T(8,128)(2,1)} %bitcast.16), channel_id=1, replica_groups=mesh['x'=4,'z'=4,'yh'=2,'yl'=2,'core'=2] {'yh','yl','core'}, dimensions={0} | all-to-all | bytes 1572864 | tf_op jit(solution)/shard_map/all_to_all | solution.py:365
  25.5 4.1 %collective-permute-start.5 = (bf16[8,16,1664]{2,1,0:T(8,128)(2,1)S(1)}, bf16[8,16,1664]{2,1,0:T(8,128)(2,1)S(1)}, u32[]{:S(2)}, u32[]{:S(2)}) collective-permute-start(bf16[8,16,1664]{2,1,0:T(8,128)(2,1)S(1)} %pad_maximum_fusion.refs_5_.refs_15_.refs_20_.refs_25_), channel_id=1, source_target_pairs={{0,24},{8,0},{16,8},{24,16},{1,25},{9,1},{17,9},{25,17},{2,26},{10... | collective-permute-start | bytes 1277960 | tf_op jit(solution)/shard_map/ppermute | solution.py:344
  29.7 2.8 %collective-permute-start.1 = (bf16[8,16,1408]{2,1,0:T(8,128)(2,1)S(1)}, bf16[8,16,1408]{2,1,0:T(8,128)(2,1)S(1)}, u32[]{:S(2)}, u32[]{:S(2)}) collective-permute-start(bf16[8,16,1408]{2,1,0:T(8,128)(2,1)S(1)} %slice.28.refs_0_.refs_10_), channel_id=1, source_target_pairs={{0,96},{32,0},{64,32},{96,64},{1,97},{33,1},{65,33},{97,65},{2,98}... | collective-permute-start | bytes 1081352 | tf_op jit(solution)/shard_map/ppermute | solution.py:344
  32.5 5.8 %collective-permute-done.5.refs_7_.refs_17_.refs_22_.refs_27_ = bf16[8,16,1664]{2,1,0:T(8,128)(2,1)S(1)} collective-permute-done((bf16[8,16,1664]{2,1,0:T(8,128)(2,1)S(1)}, bf16[8,16,1664]{2,1,0:T(8,128)(2,1)S(1)}, u32[]{:S(2)}, u32[]{:S(2)}) %collective-permute-start.5) | collective-permute-done | bytes 426016 | tf_op jit(solution)/shard_map/ppermute | solution.py:344
  38.4 3.8 %collective-permute-start.7 = (bf16[4,16,1664]{2,1,0:T(8,128)(2,1)S(1)}, bf16[4,16,1664]{2,1,0:T(8,128)(2,1)}, u32[]{:S(2)}, u32[]{:S(2)}) collective-permute-start(bf16[4,16,1664]{2,1,0:T(8,128)(2,1)S(1)} %slice.34), channel_id=1, source_target_pairs={{0,24},{8,0},{16,8},{24,16},{1,25},{9,1},{17,9},{25,17},{2,26},{10... | collective-permute-start | bytes 638984 | tf_op jit(solution)/shard_map/ppermute | solution.py:350
  42.1 0.8 copy-done.2
  43.1 2.8 %collective-permute-start.3 = (bf16[4,16,1408]{2,1,0:T(8,128)(2,1)S(1)}, bf16[4,16,1408]{2,1,0:T(8,128)(2,1)}, u32[]{:S(2)}, u32[]{:S(2)}) collective-permute-start(bf16[4,16,1408]{2,1,0:T(8,128)(2,1)S(1)} %slice.30), channel_id=1, source_target_pairs={{0,96},{32,0},{64,32},{96,64},{1,97},{33,1},{65,33},{97,65},{2,98}... | collective-permute-start | bytes 540680 | tf_op jit(solution)/shard_map/ppermute | solution.py:350
  45.9 0.7 copy-done.5
  46.7 0.6 pad_add_fusion.pos
  47.3 1.6 %collective-permute-done.3.refs_4_.refs_14_ = bf16[4,16,1408]{2,1,0:T(8,128)(2,1)} collective-permute-done((bf16[4,16,1408]{2,1,0:T(8,128)(2,1)S(1)}, bf16[4,16,1408]{2,1,0:T(8,128)(2,1)}, u32[]{:S(2)}, u32[]{:S(2)}) %collective-permute-start.3) | collective-permute-done | bytes 180256 | tf_op jit(solution)/shard_map/ppermute | solution.py:350
  48.9 4.6 %collective-permute-done.2.refs_3_.refs_13_ = bf16[4,16,1408]{2,1,0:T(8,128)(2,1)} collective-permute-done((bf16[4,16,1408]{2,1,0:T(8,128)(2,1)S(1)}, bf16[4,16,1408]{2,1,0:T(8,128)(2,1)}, u32[]{:S(2)}, u32[]{:S(2)}) %collective-permute-start.2) | collective-permute-done | bytes 180256 | tf_op jit(solution)/shard_map/ppermute | solution.py:350
  53.5 3.6 %interleave.2 = (bf16[1088,256]{1,0:T(8,128)(2,1)}, bf16[1168,256]{1,0:T(8,128)(2,1)}, bf16[144,256]{1,0:T(8,128)(2,1)}) custom-call(s32[2]{0:T(128)} %pad_add_fusion.pos, bf16[8,16,1408]{2,1,0:T(8,128)(2,1)} %copy-done.3, bf16[8,16,1408]{2,1,0:T(8,128)(2,1)} %copy-done.5, bf16[8,16,1408]{2,1,0:T(8,128)(2,1)} %copy-done.4, ...), custom_call_target="tpu_custom_call" | custom-call | tf_op jit(solution)/shard_map/interleave/pallas_call | solution.py:219
  57.2 2.0 %collective-permute-start.10 = (bf16[1168,256]{1,0:T(8,128)(2,1)}, bf16[1168,256]{1,0:T(8,128)(2,1)}, u32[]{:S(2)}, u32[]{:S(2)}) collective-permute-start(bf16[1168,256]{1,0:T(8,128)(2,1)} %get-tuple-element.31.refs_4_), channel_id=1, source_target_pairs={{0,32},{32,64},{64,96},{96,0},{1,33},{33,65},{65,97},{97,1},{2,34}... | collective-permute-start | bytes 1794056 | tf_op jit(solution)/shard_map/ppermute | solution.py:344
  59.2 3.2 %collective-permute-start.9 = (bf16[1088,256]{1,0:T(8,128)(2,1)}, bf16[1088,256]{1,0:T(8,128)(2,1)}, u32[]{:S(2)}, u32[]{:S(2)}) collective-permute-start(bf16[1088,256]{1,0:T(8,128)(2,1)} %get-tuple-element.30.refs_0_), channel_id=1, source_target_pairs={{0,24},{8,0},{16,8},{24,16},{1,25},{9,1},{17,9},{25,17},{2,26},{10... | collective-permute-start | bytes 1671176 | tf_op jit(solution)/shard_map/ppermute | solution.py:344
  62.4 4.0 %interleave.3 = (bf16[1632,256]{1,0:T(8,128)(2,1)}, bf16[1536,256]{1,0:T(8,128)(2,1)}, bf16[128,1024]{1,0:T(8,128)(2,1)}) custom-call(s32[2]{0:T(128)} %pad_add_fusion.pos, bf16[8,16,1408]{2,1,0:T(8,128)(2,1)} %copy-done.3, bf16[8,16,1408]{2,1,0:T(8,128)(2,1)} %copy-done.5, bf16[8,16,1408]{2,1,0:T(8,128)(2,1)} %copy-done.4, ...), custom_call_target="tpu_custom_call" | custom-call | tf_op jit(solution)/shard_map/interleave/pallas_call | solution.py:219
  66.4 4.9 %collective-permute-done.12.refs_3_ = bf16[144,256]{1,0:T(8,128)(2,1)S(1)} collective-permute-done((bf16[144,256]{1,0:T(8,128)(2,1)}, bf16[144,256]{1,0:T(8,128)(2,1)S(1)}, u32[]{:S(2)}, u32[]{:S(2)}) %collective-permute-start.12) | collective-permute-done | bytes 73760 | tf_op jit(solution)/shard_map/ppermute | solution.py:377
  71.3 2.9 %collective-permute-done.8.refs_1_ = bf16[1088,256]{1,0:T(8,128)(2,1)} collective-permute-done((bf16[1088,256]{1,0:T(8,128)(2,1)}, bf16[1088,256]{1,0:T(8,128)(2,1)}, u32[]{:S(2)}, u32[]{:S(2)}) %collective-permute-start.8) | collective-permute-done | bytes 557088 | tf_op jit(solution)/shard_map/ppermute | solution.py:344
  74.2 1.3 collective-permute-start.15
  75.5 2.3 %collective-permute-start.16 = (bf16[1536,256]{1,0:T(8,128)(2,1)}, bf16[1536,256]{1,0:T(8,128)(2,1)}, u32[]{:S(2)}, u32[]{:S(2)}) collective-permute-start(bf16[1536,256]{1,0:T(8,128)(2,1)} %get-tuple-element.46.refs_4_), channel_id=1, source_target_pairs={{0,96},{32,0},{64,32},{96,64},{1,97},{33,1},{65,33},{97,65},{2,98}... | collective-permute-start | bytes 2359304 | tf_op jit(solution)/shard_map/ppermute | solution.py:381
  77.8 0.5 collective-permute-start.13
  78.3 3.0 %arrange_left.1 = bf16[528,128]{1,0:T(8,128)(2,1)} custom-call(s32[2]{0:T(128)} %pad_add_fusion.pos, bf16[144,256]{1,0:T(8,128)(2,1)} %get-tuple-element.34.refs_0_, bf16[1168,256]{1,0:T(8,128)(2,1)} %collective-permute-done.10.refs_1_.refs_5_, bf16[1168,256]{1,0:T(8,128)(2,1)} %copy-done.6, bf16[144,256]{1,0:T(8,128)(2,1)} %copy-done.8), custom_call_target="tpu_custom_call" | custom-call | tf_op jit(solution)/shard_map/arrange_left/pallas_call | solution.py:267
  81.3 7.3 %all-gather = bf16[2112,128]{1,0:T(8,128)(2,1)} all-gather(bf16[528,128]{1,0:T(8,128)(2,1)} %arrange_left.1), channel_id=2, replica_groups=mesh['x'=4,'z'=4,'yh'=2,'yl'=2,'core'=2] {'yl','core'}, dimensions={0}, use_global_device_ids=true | all-gather | bytes 675840 | tf_op jit(solution)/shard_map/all_gather | solution.py:383
  88.6 0.3 collective-permute-done.13.refs_3_
  88.8 0.4 collective-permute-done.14.refs_7_
  89.3 0.5 collective-permute-done.16.refs_6_
  89.9 2.7 %collective-permute-start.18 = (bf16[1632,256]{1,0:T(8,128)(2,1)}, bf16[1632,256]{1,0:T(8,128)(2,1)}, u32[]{:S(2)}, u32[]{:S(2)}) collective-permute-start(bf16[1632,256]{1,0:T(8,128)(2,1)} %collective-permute-done.15.refs_2_), channel_id=1, source_target_pairs={{0,24},{8,0},{16,8},{24,16},{1,25},{9,1},{17,9},{25,17},{2,26},{10... | collective-permute-start | bytes 2506760 | tf_op jit(solution)/shard_map/ppermute | solution.py:388
  92.6 3.1 %collective-permute-start.20 = (bf16[1536,256]{1,0:T(8,128)(2,1)}, bf16[1536,256]{1,0:T(8,128)(2,1)}, u32[]{:S(2)}, u32[]{:S(2)}) collective-permute-start(bf16[1536,256]{1,0:T(8,128)(2,1)} %collective-permute-done.16.refs_6_), channel_id=1, source_target_pairs={{0,96},{32,0},{64,32},{96,64},{1,97},{33,1},{65,33},{97,65},{2,98}... | collective-permute-start | bytes 2359304 | tf_op jit(solution)/shard_map/ppermute | solution.py:388
  95.8 16.8 %pair.2.refs_8_ = bf16[32,1280,128]{2,1,0:T(8,128)(2,1)} custom-call(bf16[4,528,128]{2,1,0:T(8,128)(2,1)} %bitcast.14, bf16[128,1024]{1,0:T(8,128)(2,1)} %get-tuple-element.43.w_ref, bf16[1088,256]{1,0:T(8,128)(2,1)} %get-tuple-element.30.refs_0_, bf16[1088,256]{1,0:T(8,128)(2,1)} %collective-permute-done.8.refs_1_, ...), custom_call_target="tpu_custom_call" | custom-call | tf_op jit(solution)/shard_map/pair/pallas_call | solution.py:321
  112.8 0.9 copy-done.7
  113.7 24.0 %pair.3 = bf16[32,1280,128]{2,1,0:T(8,128)(2,1)} custom-call(bf16[4,528,128]{2,1,0:T(8,128)(2,1)} %bitcast.15, bf16[128,1024]{1,0:T(8,128)(2,1)} %get-tuple-element.43.w_ref, bf16[1632,256]{1,0:T(8,128)(2,1)} %get-tuple-element.44.refs_0_, bf16[1632,256]{1,0:T(8,128)(2,1)} %copy-done.7, ...), custom_call_target="tpu_custom_call", output_to_operand_aliasing={{}: (10, {})} | custom-call | tf_op jit(solution)/shard_map/pair/pallas_call | solution.py:321
  (46 shorter events, 0.8 us)
Async XLA Ops:
  25.5 28.0 %copy-start = (bf16[8,16,1664]{2,1,0:T(8,128)(2,1)}, bf16[8,16,1664]{2,1,0:T(8,128)(2,1)S(1)}, u32[]{:S(2)}) copy-start(bf16[8,16,1664]{2,1,0:T(8,128)(2,1)S(1)} %pad_maximum_fusion.refs_5_.refs_15_.refs_20_.refs_25_) | copy-start | bytes 1277956
  25.5 12.8 %collective-permute-start.5 = (bf16[8,16,1664]{2,1,0:T(8,128)(2,1)S(1)}, bf16[8,16,1664]{2,1,0:T(8,128)(2,1)S(1)}, u32[]{:S(2)}, u32[]{:S(2)}) collective-permute-start(bf16[8,16,1664]{2,1,0:T(8,128)(2,1)S(1)} %pad_maximum_fusion.refs_5_.refs_15_.refs_20_.refs_25_), channel_id=1, source_target_pairs={{0,24},{8,0},{16,8},{24,16},{1,25},{9,1},{17,9},{25,17},{2,26},{10... | collective-permute-start | bytes 1277960 | tf_op jit(solution)/shard_map/ppermute | solution.py:344
  29.6 12.5 %collective-permute-start.4 = (bf16[8,16,1664]{2,1,0:T(8,128)(2,1)S(1)}, bf16[8,16,1664]{2,1,0:T(8,128)(2,1)S(1)}, u32[]{:S(2)}, u32[]{:S(2)}) collective-permute-start(bf16[8,16,1664]{2,1,0:T(8,128)(2,1)S(1)} %pad_maximum_fusion.refs_5_.refs_15_.refs_20_.refs_25_), channel_id=1, source_target_pairs={{0,8},{8,16},{16,24},{24,0},{1,9},{9,17},{17,25},{25,1},{2,10},{10... | collective-permute-start | bytes 1277960 | tf_op jit(solution)/shard_map/ppermute | solution.py:344
  29.7 13.3 %copy-start.3 = (bf16[8,16,1408]{2,1,0:T(8,128)(2,1)}, bf16[8,16,1408]{2,1,0:T(8,128)(2,1)S(1)}, u32[]{:S(2)}) copy-start(bf16[8,16,1408]{2,1,0:T(8,128)(2,1)S(1)} %slice.28.refs_0_.refs_10_) | copy-start | bytes 1081348
  29.7 13.4 %collective-permute-start.1 = (bf16[8,16,1408]{2,1,0:T(8,128)(2,1)S(1)}, bf16[8,16,1408]{2,1,0:T(8,128)(2,1)S(1)}, u32[]{:S(2)}, u32[]{:S(2)}) collective-permute-start(bf16[8,16,1408]{2,1,0:T(8,128)(2,1)S(1)} %slice.28.refs_0_.refs_10_), channel_id=1, source_target_pairs={{0,96},{32,0},{64,32},{96,64},{1,97},{33,1},{65,33},{97,65},{2,98}... | collective-permute-start | bytes 1081352 | tf_op jit(solution)/shard_map/ppermute | solution.py:344
  32.5 13.4 %collective-permute-start = (bf16[8,16,1408]{2,1,0:T(8,128)(2,1)S(1)}, bf16[8,16,1408]{2,1,0:T(8,128)(2,1)S(1)}, u32[]{:S(2)}, u32[]{:S(2)}) collective-permute-start(bf16[8,16,1408]{2,1,0:T(8,128)(2,1)S(1)} %slice.28.refs_0_.refs_10_), channel_id=1, source_target_pairs={{0,32},{32,64},{64,96},{96,0},{1,33},{33,65},{65,97},{97,1},{2,34}... | collective-permute-start | bytes 1081352 | tf_op jit(solution)/shard_map/ppermute | solution.py:344
  38.4 15.2 %copy-start.1 = (bf16[8,16,1664]{2,1,0:T(8,128)(2,1)}, bf16[8,16,1664]{2,1,0:T(8,128)(2,1)S(1)}, u32[]{:S(2)}) copy-start(bf16[8,16,1664]{2,1,0:T(8,128)(2,1)S(1)} %collective-permute-done.5.refs_7_.refs_17_.refs_22_.refs_27_) | copy-start | bytes 1277956
  38.4 15.1 %collective-permute-start.7 = (bf16[4,16,1664]{2,1,0:T(8,128)(2,1)S(1)}, bf16[4,16,1664]{2,1,0:T(8,128)(2,1)}, u32[]{:S(2)}, u32[]{:S(2)}) collective-permute-start(bf16[4,16,1664]{2,1,0:T(8,128)(2,1)S(1)} %slice.34), channel_id=1, source_target_pairs={{0,24},{8,0},{16,8},{24,16},{1,25},{9,1},{17,9},{25,17},{2,26},{10... | collective-permute-start | bytes 638984 | tf_op jit(solution)/shard_map/ppermute | solution.py:350
  42.1 0.8 copy-start.2
  43.0 10.5 %collective-permute-start.6 = (bf16[4,16,1664]{2,1,0:T(8,128)(2,1)S(1)}, bf16[4,16,1664]{2,1,0:T(8,128)(2,1)}, u32[]{:S(2)}, u32[]{:S(2)}) collective-permute-start(bf16[4,16,1664]{2,1,0:T(8,128)(2,1)S(1)} %slice.33), channel_id=1, source_target_pairs={{0,8},{8,16},{16,24},{24,0},{1,9},{9,17},{17,25},{25,1},{2,10},{10... | collective-permute-start | bytes 638984 | tf_op jit(solution)/shard_map/ppermute | solution.py:350
  43.1 2.9 %copy-start.4 = (bf16[8,16,1408]{2,1,0:T(8,128)(2,1)}, bf16[8,16,1408]{2,1,0:T(8,128)(2,1)S(1)}, u32[]{:S(2)}) copy-start(bf16[8,16,1408]{2,1,0:T(8,128)(2,1)S(1)} %collective-permute-done.1.refs_2_.refs_12_) | copy-start | bytes 1081348
  43.1 5.8 %collective-permute-start.3 = (bf16[4,16,1408]{2,1,0:T(8,128)(2,1)S(1)}, bf16[4,16,1408]{2,1,0:T(8,128)(2,1)}, u32[]{:S(2)}, u32[]{:S(2)}) collective-permute-start(bf16[4,16,1408]{2,1,0:T(8,128)(2,1)S(1)} %slice.30), channel_id=1, source_target_pairs={{0,96},{32,0},{64,32},{96,64},{1,97},{33,1},{65,33},{97,65},{2,98}... | collective-permute-start | bytes 540680 | tf_op jit(solution)/shard_map/ppermute | solution.py:350
  45.9 0.8 copy-start.5
  46.7 6.8 %collective-permute-start.2 = (bf16[4,16,1408]{2,1,0:T(8,128)(2,1)S(1)}, bf16[4,16,1408]{2,1,0:T(8,128)(2,1)}, u32[]{:S(2)}, u32[]{:S(2)}) collective-permute-start(bf16[4,16,1408]{2,1,0:T(8,128)(2,1)S(1)} %slice.29), channel_id=1, source_target_pairs={{0,32},{32,64},{64,96},{96,0},{1,33},{33,65},{65,97},{97,1},{2,34}... | collective-permute-start | bytes 540680 | tf_op jit(solution)/shard_map/ppermute | solution.py:350
  57.1 17.1 %collective-permute-start.11 = (bf16[1168,256]{1,0:T(8,128)(2,1)}, bf16[1168,256]{1,0:T(8,128)(2,1)S(1)}, u32[]{:S(2)}, u32[]{:S(2)}) collective-permute-start(bf16[1168,256]{1,0:T(8,128)(2,1)} %get-tuple-element.31.refs_4_), channel_id=1, source_target_pairs={{0,96},{32,0},{64,32},{96,64},{1,97},{33,1},{65,33},{97,65},{2,98}... | collective-permute-start | bytes 1794056 | tf_op jit(solution)/shard_map/ppermute | solution.py:344
  57.2 17.0 %collective-permute-start.10 = (bf16[1168,256]{1,0:T(8,128)(2,1)}, bf16[1168,256]{1,0:T(8,128)(2,1)}, u32[]{:S(2)}, u32[]{:S(2)}) collective-permute-start(bf16[1168,256]{1,0:T(8,128)(2,1)} %get-tuple-element.31.refs_4_), channel_id=1, source_target_pairs={{0,32},{32,64},{64,96},{96,0},{1,33},{33,65},{65,97},{97,1},{2,34}... | collective-permute-start | bytes 1794056 | tf_op jit(solution)/shard_map/ppermute | solution.py:344
  59.2 12.1 %collective-permute-start.9 = (bf16[1088,256]{1,0:T(8,128)(2,1)}, bf16[1088,256]{1,0:T(8,128)(2,1)}, u32[]{:S(2)}, u32[]{:S(2)}) collective-permute-start(bf16[1088,256]{1,0:T(8,128)(2,1)} %get-tuple-element.30.refs_0_), channel_id=1, source_target_pairs={{0,24},{8,0},{16,8},{24,16},{1,25},{9,1},{17,9},{25,17},{2,26},{10... | collective-permute-start | bytes 1671176 | tf_op jit(solution)/shard_map/ppermute | solution.py:344
  62.4 11.8 %collective-permute-start.8 = (bf16[1088,256]{1,0:T(8,128)(2,1)}, bf16[1088,256]{1,0:T(8,128)(2,1)}, u32[]{:S(2)}, u32[]{:S(2)}) collective-permute-start(bf16[1088,256]{1,0:T(8,128)(2,1)} %get-tuple-element.30.refs_0_), channel_id=1, source_target_pairs={{0,8},{8,16},{16,24},{24,0},{1,9},{9,17},{17,25},{25,1},{2,10},{10... | collective-permute-start | bytes 1671176 | tf_op jit(solution)/shard_map/ppermute | solution.py:344
  62.4 8.9 %collective-permute-start.12 = (bf16[144,256]{1,0:T(8,128)(2,1)}, bf16[144,256]{1,0:T(8,128)(2,1)S(1)}, u32[]{:S(2)}, u32[]{:S(2)}) collective-permute-start(bf16[144,256]{1,0:T(8,128)(2,1)} %get-tuple-element.34.refs_0_), channel_id=1, source_target_pairs={{0,64},{32,96},{64,0},{96,32},{1,65},{33,97},{65,1},{97,33},{2,66}... | collective-permute-start | bytes 221192 | tf_op jit(solution)/shard_map/ppermute | solution.py:377
  71.3 7.0 %copy-start.8 = (bf16[144,256]{1,0:T(8,128)(2,1)}, bf16[144,256]{1,0:T(8,128)(2,1)S(1)}, u32[]{:S(2)}) copy-start(bf16[144,256]{1,0:T(8,128)(2,1)S(1)} %collective-permute-done.12.refs_3_) | copy-start | bytes 221188
  74.2 4.1 %copy-start.6 = (bf16[1168,256]{1,0:T(8,128)(2,1)}, bf16[1168,256]{1,0:T(8,128)(2,1)S(1)}, u32[]{:S(2)}) copy-start(bf16[1168,256]{1,0:T(8,128)(2,1)S(1)} %collective-permute-done.11.refs_2_.refs_6_) | copy-start | bytes 1794052
  74.2 15.7 %collective-permute-start.15 = (bf16[1632,256]{1,0:T(8,128)(2,1)}, bf16[1632,256]{1,0:T(8,128)(2,1)}, u32[]{:S(2)}, u32[]{:S(2)}) collective-permute-start(bf16[1632,256]{1,0:T(8,128)(2,1)} %get-tuple-element.44.refs_0_), channel_id=1, source_target_pairs={{0,24},{8,0},{16,8},{24,16},{1,25},{9,1},{17,9},{25,17},{2,26},{10... | collective-permute-start | bytes 2506760 | tf_op jit(solution)/shard_map/ppermute | solution.py:381
  75.5 14.3 %collective-permute-start.16 = (bf16[1536,256]{1,0:T(8,128)(2,1)}, bf16[1536,256]{1,0:T(8,128)(2,1)}, u32[]{:S(2)}, u32[]{:S(2)}) collective-permute-start(bf16[1536,256]{1,0:T(8,128)(2,1)} %get-tuple-element.46.refs_4_), channel_id=1, source_target_pairs={{0,96},{32,0},{64,32},{96,64},{1,97},{33,1},{65,33},{97,65},{2,98}... | collective-permute-start | bytes 2359304 | tf_op jit(solution)/shard_map/ppermute | solution.py:381
  77.8 11.5 %collective-permute-start.14 = (bf16[1168,256]{1,0:T(8,128)(2,1)}, bf16[1168,256]{1,0:T(8,128)(2,1)}, u32[]{:S(2)}, u32[]{:S(2)}) collective-permute-start(bf16[1168,256]{1,0:T(8,128)(2,1)} %collective-permute-done.10.refs_1_.refs_5_), channel_id=1, source_target_pairs={{0,32},{32,64},{64,96},{96,0},{1,33},{33,65},{65,97},{97,1},{2,34}... | collective-permute-start | bytes 1794056 | tf_op jit(solution)/shard_map/ppermute | solution.py:380
  77.8 11.1 %collective-permute-start.13 = (bf16[1088,256]{1,0:T(8,128)(2,1)}, bf16[1088,256]{1,0:T(8,128)(2,1)}, u32[]{:S(2)}, u32[]{:S(2)}) collective-permute-start(bf16[1088,256]{1,0:T(8,128)(2,1)} %collective-permute-done.8.refs_1_), channel_id=1, source_target_pairs={{0,8},{8,16},{16,24},{24,0},{1,9},{9,17},{17,25},{25,1},{2,10},{10... | collective-permute-start | bytes 1671176 | tf_op jit(solution)/shard_map/ppermute | solution.py:380
  89.3 23.5 %collective-permute-start.17 = (bf16[1632,256]{1,0:T(8,128)(2,1)}, bf16[1632,256]{1,0:T(8,128)(2,1)S(1)}, u32[]{:S(2)}, u32[]{:S(2)}) collective-permute-start(bf16[1632,256]{1,0:T(8,128)(2,1)} %get-tuple-element.44.refs_0_), channel_id=1, source_target_pairs={{0,8},{8,16},{16,24},{24,0},{1,9},{9,17},{17,25},{25,1},{2,10},{10... | collective-permute-start | bytes 2506760 | tf_op jit(solution)/shard_map/ppermute | solution.py:386
  89.9 23.0 %collective-permute-start.18 = (bf16[1632,256]{1,0:T(8,128)(2,1)}, bf16[1632,256]{1,0:T(8,128)(2,1)}, u32[]{:S(2)}, u32[]{:S(2)}) collective-permute-start(bf16[1632,256]{1,0:T(8,128)(2,1)} %collective-permute-done.15.refs_2_), channel_id=1, source_target_pairs={{0,24},{8,0},{16,8},{24,16},{1,25},{9,1},{17,9},{25,17},{2,26},{10... | collective-permute-start | bytes 2506760 | tf_op jit(solution)/shard_map/ppermute | solution.py:388
  92.5 20.3 %collective-permute-start.19 = (bf16[1536,256]{1,0:T(8,128)(2,1)}, bf16[1536,256]{1,0:T(8,128)(2,1)}, u32[]{:S(2)}, u32[]{:S(2)}) collective-permute-start(bf16[1536,256]{1,0:T(8,128)(2,1)} %get-tuple-element.46.refs_4_), channel_id=1, source_target_pairs={{0,32},{32,64},{64,96},{96,0},{1,33},{33,65},{65,97},{97,1},{2,34}... | collective-permute-start | bytes 2359304 | tf_op jit(solution)/shard_map/ppermute | solution.py:386
  92.6 20.2 %collective-permute-start.20 = (bf16[1536,256]{1,0:T(8,128)(2,1)}, bf16[1536,256]{1,0:T(8,128)(2,1)}, u32[]{:S(2)}, u32[]{:S(2)}) collective-permute-start(bf16[1536,256]{1,0:T(8,128)(2,1)} %collective-permute-done.16.refs_6_), channel_id=1, source_target_pairs={{0,96},{32,0},{64,32},{96,64},{1,97},{33,1},{65,33},{97,65},{2,98}... | collective-permute-start | bytes 2359304 | tf_op jit(solution)/shard_map/ppermute | solution.py:388
  112.8 0.9 copy-start.7

commit v5 on v4

--- a/solution.py
+++ b/solution.py
@@ -51,75 +51,48 @@
     return jnp.dot(values, choose, preferred_element_type=f32).astype(bf16)
 
 
-def project_left(x, mask, gain, bias, weight, shift):
-    features = x.shape[1]
-    width = weight.shape[0]
-    rows = RD * 32
-    sub = 512
-
-    def kernel(x_ref, m_ref, g_ref, s_ref, w_ref, b_ref, out_ref, mask_ref):
-        b = turned(b_ref)
-        y = []
-        for part in range(rows // sub):
-            at = slice(part * sub, (part + 1) * sub)
-            normed = standardize(x_ref[at, :], g_ref[...], s_ref[...])
-            y.append(affine(w_ref, b, normed, m_ref[:, at]))
-        y = jnp.concatenate(y, axis=1)
-        y = jnp.concatenate([y, jnp.broadcast_to(m_ref[...], (16, rows))], axis=0).astype(bf16)
-
-        def regroup(src, dst):
-            return src == ((dst >> 3) & 3) * 64 + (dst >> 5) * 8 + (dst & 7)
-
-        choose = one_hot(256, 256, regroup)
-        y = [move(y[:, k * 256 : (k + 1) * 256], choose) for k in range(4)]
-        for device in range(8):
-            tile = jnp.concatenate([t[:, device * 32 : (device + 1) * 32] for t in y], axis=1)
-            out_ref[device] = tile[:32]
-            mask_ref[device] = tile[32:]
-
-    return pl.pallas_call(
-        kernel,
-        grid=(1,),
-        out_shape=(
-            jax.ShapeDtypeStruct((8, 32, TILE), bf16),
-            jax.ShapeDtypeStruct((8, 16, TILE), bf16),
-        ),
-        in_specs=[
-            pl.BlockSpec((rows, features), lambda _: (0, 0)),
-            pl.BlockSpec((1, rows), lambda _: (0, 0)),
-            whole(1, features),
-            whole(1, features),
-            whole(width, features),
-            whole(1, width),
-        ],
-        out_specs=(whole(8, 32, TILE), whole(8, 16, TILE)),
-        compiler_params=vmem(),
-        name="project_left",
-    )(x, mask, gain, bias, weight, shift)
-
-
-def project_right(x, mask, gain, bias, weight, shift, left, left_mask):
+def project(x, mask, gain, bias, w_left, b_left, w_right, b_right):
     rows, features = x.shape
     quarter = rows // 4
-    width = weight.shape[0]
+    width = w_right.shape[0]
+    total = quarter + 2 * TILE
+    left_rows = RD * 32
     sub = 640
-    total = quarter + 2 * TILE
-
-    def kernel(x_ref, m_ref, g_ref, s_ref, w_ref, b_ref, l_ref, n_ref, out_ref):
-        b = turned(b_ref)
+
+    def kernel(x_ref, m_ref, g_ref, s_ref, wl_ref, bl_ref, wr_ref, br_ref, out_ref, normed, left, left_mask):
+        step = pl.program_id(0)
+        b = turned(br_ref)
         for part in range(quarter // sub):
             at = slice(part * sub, (part + 1) * sub)
-            normed = standardize(x_ref[at, :], g_ref[...], s_ref[...])
-            y = affine(w_ref, b, normed, m_ref[0, :, at]).astype(bf16)
+            values = standardize(x_ref[at, :], g_ref[...], s_ref[...])
+            normed[at, :] = values
+            y = affine(wr_ref, b, values, m_ref[0, :, at]).astype(bf16)
             out_ref[0, 0, :, at] = y
             out_ref[1, 0, :, at] = y
+
+        @pl.when(step == 0)
+        def _():
+            m = m_ref[0, :, :left_rows]
+            y = affine(wl_ref, turned(bl_ref), normed[:left_rows, :], m)
+            y = jnp.concatenate([y, jnp.broadcast_to(m, (16, left_rows))], axis=0).astype(bf16)
+
+            def regroup(src, dst):
+                return src == ((dst >> 3) & 3) * 64 + (dst >> 5) * 8 + (dst & 7)
+
+            choose = one_hot(256, 256, regroup)
+            y = [move(y[:, k * 256 : (k + 1) * 256], choose) for k in range(4)]
+            for device in range(8):
+                tile = jnp.concatenate([t[:, device * 32 : (device + 1) * 32] for t in y], axis=1)
+                left[device] = tile[:width]
+                left_mask[device] = tile[width:]
+
         m = [m_ref[0, :, k * TILE : (k + 1) * TILE] for k in range(quarter // TILE)]
+        m = jnp.concatenate(m + [jnp.zeros((16 - len(m), TILE), f32)], axis=0).astype(bf16)
         for yh in range(2):
-            device = yh * 4 + pl.program_id(0)
-            tile = jnp.concatenate(m + [jnp.zeros((16 - len(m), TILE), f32)], axis=0)
-            out_ref[yh, 0, :16, quarter : quarter + TILE] = tile.astype(bf16)
-            out_ref[yh, 0, 16:, quarter : quarter + TILE] = n_ref[device]
-            out_ref[yh, 0, :, quarter + TILE :] = l_ref[device]
+            device = yh * 4 + step
+            out_ref[yh, 0, :16, quarter : quarter + TILE] = m
+            out_ref[yh, 0, 16:, quarter : quarter + TILE] = left_mask[device]
+            out_ref[yh, 0, :, quarter + TILE :] = left[device]
 
     return pl.pallas_call(
         kernel,
@@ -132,13 +105,18 @@
             whole(1, features),
             whole(width, features),
             whole(1, width),
-            whole(*left.shape),
-            whole(*left_mask.shape),
+            whole(width, features),
+            whole(1, width),
         ],
         out_specs=pl.BlockSpec((2, 1, width, total), lambda q: (0, q, 0, 0)),
+        scratch_shapes=[
+            pltpu.VMEM((quarter, features), bf16),
+            pltpu.VMEM((8, width, TILE), bf16),
+            pltpu.VMEM((8, 16, TILE), bf16),
+        ],
         compiler_params=vmem(),
-        name="project_right",
-    )(x, mask.reshape(4, 1, quarter), gain, bias, weight, shift, left, left_mask)
+        name="project",
+    )(x, mask.reshape(4, 1, quarter), gain, bias, w_left, b_left, w_right, b_right)
 
 
 def ring(step):
@@ -360,8 +338,7 @@
     narrow = ("yl", "core")
     position = jnp.stack([lax.axis_index(axis) for axis in ("x", "z")]).astype(jnp.int32)
     norm = gain[None], bias[None]
-    left = project_left(x[0], mask, *norm, w_left.T, b_left[None])
-    right = project_right(x[0], mask, *norm, w_right.T, b_right[None], *left)
+    right = project(x[0], mask, *norm, w_left.T, b_left[None], w_right.T, b_right[None])
     right = lax.all_to_all(right.reshape(8, width, -1), COLUMN, 0, 0, tiled=True)
 
     halves = (

time: 138 us -> 136 us (0.986)
  Pallas kernels: 58.9 us -> 56.9 us
    pallas_call x2 -> x1, Pallas kernels: 7.64 us -> 5.62 us  [project(): pl.pallas_call(kernel, grid=(4,), out_shape=jax.ShapeDtypeStruct((2, 4, w...]
  transfers between devices with their start and end apart: 21 -> 21, of which waited for: 9 -> 9; matrix products, arithmetic and copies ran while one was open for 1% -> 0% of each run, Pallas kernels for 17% -> 18%
where the time goes in v5:
time: 136 us
  Pallas kernels  56.9 us (42%)
  starting transfers between devices  29 us (21%)
  blocking collectives  25.1 us (18%)
  waiting for transfers between devices  21.3 us (16%)
  local copies, waits for them, and re-layouts  2.56 us (2%)
    pallas_call x2, Pallas kernels, pair(): pl.pallas_call(kernel, grid=(chunks,), out_shape=jax.ShapeDtypeStruct((RD...  40.8 us
    all_to_all x1, blocking collectives, on_device(): lax.all_to_all(right.reshape(8, width, -1), COLUMN, 0, 0, tiled=True)  17.8 us
    ppermute x4, starting transfers between devices, send_both(): lax.ppermute(block, axis, ring(-1))  10.2 us
    ppermute x4, starting transfers between devices, on_device(): lax.ppermute(block, axis, ring(-1))  9.42 us
    pallas_call x2, Pallas kernels, interleave(): pl.pallas_call(kernel, grid_spec=pltpu.PrefetchScalarGridSpec(num_scalar_...  7.56 us
    all_gather x1, blocking collectives, on_device(): left = lax.all_gather(left, narrow, axis=0)  7.28 us
    ppermute x2, starting transfers between devices, send_on(): lax.ppermute(high, axis, ring(-1))  6.59 us
    ppermute x4, waiting for transfers between devices, send_both(): lax.ppermute(block, axis, ring(-1))  5.84 us
  transfers between devices with their start and end apart: 21, of which 9 were waited for; matrix products, arithmetic and copies ran while one was open for 0% of the time, Pallas kernels for 18%

profile of v5, /device:TPU:0, one launch (start us, length us, event | category | flops | bytes accessed | tf_op | source)
XLA Modules:
  0.0 135.6 jit_solution(17903383455613223825)
XLA Ops:
  0.0 5.6 %project.1 = bf16[2,4,32,1536]{3,2,1,0:T(8,128)(2,1)} custom-call(bf16[5120,256]{1,0:T(8,128)(2,1)} %bitcast.15, f32[4,1,1280]{2,1,0:T(1,128)} %bitcast.16, f32[1,256]{1,0:T(1,128)} %bitcast.19, f32[1,256]{1,0:T(1,128)} %bitcast.20, bf16[32,256]{1,0:T(8,128)(2,1)} %bitcast.17, f32[1,32]{1,0:T(1,128)} %bitcast.21, bf16[32,256]{1,0:T(8,128)(2,1)} %bitcast.18, ...), custom_call_target="tpu_custom_call" | custom-call | tf_op jit(solution)/shard_map/project/pallas_call | solution.py:97
  5.6 17.8 %all_to_all.5 = bf16[8,32,1536]{2,1,0:T(8,128)(2,1)S(1)} all-to-all(bf16[8,32,1536]{2,1,0:T(8,128)(2,1)} %bitcast.14), channel_id=1, replica_groups=mesh['x'=4,'z'=4,'yh'=2,'yl'=2,'core'=2] {'yh','yl','core'}, dimensions={0} | all-to-all | bytes 1572864 | tf_op jit(solution)/shard_map/all_to_all | solution.py:342
  23.5 4.1 %collective-permute-start.5 = (bf16[8,16,1664]{2,1,0:T(8,128)(2,1)S(1)}, bf16[8,16,1664]{2,1,0:T(8,128)(2,1)S(1)}, u32[]{:S(2)}, u32[]{:S(2)}) collective-permute-start(bf16[8,16,1664]{2,1,0:T(8,128)(2,1)S(1)} %pad_maximum_fusion.refs_5_.refs_15_.refs_20_.refs_25_), channel_id=1, source_target_pairs={{0,24},{8,0},{16,8},{24,16},{1,25},{9,1},{17,9},{25,17},{2,26},{10... | collective-permute-start | bytes 1277960 | tf_op jit(solution)/shard_map/ppermute | solution.py:322
  27.7 2.8 %collective-permute-start.1 = (bf16[8,16,1408]{2,1,0:T(8,128)(2,1)S(1)}, bf16[8,16,1408]{2,1,0:T(8,128)(2,1)S(1)}, u32[]{:S(2)}, u32[]{:S(2)}) collective-permute-start(bf16[8,16,1408]{2,1,0:T(8,128)(2,1)S(1)} %slice.28.refs_0_.refs_10_), channel_id=1, source_target_pairs={{0,96},{32,0},{64,32},{96,64},{1,97},{33,1},{65,33},{97,65},{2,98}... | collective-permute-start | bytes 1081352 | tf_op jit(solution)/shard_map/ppermute | solution.py:322
  30.5 5.8 %collective-permute-done.5.refs_7_.refs_17_.refs_22_.refs_27_ = bf16[8,16,1664]{2,1,0:T(8,128)(2,1)S(1)} collective-permute-done((bf16[8,16,1664]{2,1,0:T(8,128)(2,1)S(1)}, bf16[8,16,1664]{2,1,0:T(8,128)(2,1)S(1)}, u32[]{:S(2)}, u32[]{:S(2)}) %collective-permute-start.5) | collective-permute-done | bytes 426016 | tf_op jit(solution)/shard_map/ppermute | solution.py:322
  36.4 3.8 %collective-permute-start.7 = (bf16[4,16,1664]{2,1,0:T(8,128)(2,1)S(1)}, bf16[4,16,1664]{2,1,0:T(8,128)(2,1)}, u32[]{:S(2)}, u32[]{:S(2)}) collective-permute-start(bf16[4,16,1664]{2,1,0:T(8,128)(2,1)S(1)} %slice.34), channel_id=1, source_target_pairs={{0,24},{8,0},{16,8},{24,16},{1,25},{9,1},{17,9},{25,17},{2,26},{10... | collective-permute-start | bytes 638984 | tf_op jit(solution)/shard_map/ppermute | solution.py:328
  40.1 0.8 copy-done.2
  41.1 2.8 %collective-permute-start.3 = (bf16[4,16,1408]{2,1,0:T(8,128)(2,1)S(1)}, bf16[4,16,1408]{2,1,0:T(8,128)(2,1)}, u32[]{:S(2)}, u32[]{:S(2)}) collective-permute-start(bf16[4,16,1408]{2,1,0:T(8,128)(2,1)S(1)} %slice.30), channel_id=1, source_target_pairs={{0,96},{32,0},{64,32},{96,64},{1,97},{33,1},{65,33},{97,65},{2,98}... | collective-permute-start | bytes 540680 | tf_op jit(solution)/shard_map/ppermute | solution.py:328
  43.9 0.7 copy-done.5
  44.7 0.6 pad_add_fusion.pos
  45.2 1.7 %collective-permute-done.3.refs_4_.refs_14_ = bf16[4,16,1408]{2,1,0:T(8,128)(2,1)} collective-permute-done((bf16[4,16,1408]{2,1,0:T(8,128)(2,1)S(1)}, bf16[4,16,1408]{2,1,0:T(8,128)(2,1)}, u32[]{:S(2)}, u32[]{:S(2)}) %collective-permute-start.3) | collective-permute-done | bytes 180256 | tf_op jit(solution)/shard_map/ppermute | solution.py:328
  46.9 4.6 %collective-permute-done.2.refs_3_.refs_13_ = bf16[4,16,1408]{2,1,0:T(8,128)(2,1)} collective-permute-done((bf16[4,16,1408]{2,1,0:T(8,128)(2,1)S(1)}, bf16[4,16,1408]{2,1,0:T(8,128)(2,1)}, u32[]{:S(2)}, u32[]{:S(2)}) %collective-permute-start.2) | collective-permute-done | bytes 180256 | tf_op jit(solution)/shard_map/ppermute | solution.py:328
  51.5 3.6 %interleave.2 = (bf16[1088,256]{1,0:T(8,128)(2,1)}, bf16[1168,256]{1,0:T(8,128)(2,1)}, bf16[144,256]{1,0:T(8,128)(2,1)}) custom-call(s32[2]{0:T(128)} %pad_add_fusion.pos, bf16[8,16,1408]{2,1,0:T(8,128)(2,1)} %copy-done.3, bf16[8,16,1408]{2,1,0:T(8,128)(2,1)} %copy-done.5, bf16[8,16,1408]{2,1,0:T(8,128)(2,1)} %copy-done.4, ...), custom_call_target="tpu_custom_call" | custom-call | tf_op jit(solution)/shard_map/interleave/pallas_call | solution.py:197
  55.2 2.0 %collective-permute-start.10 = (bf16[1168,256]{1,0:T(8,128)(2,1)}, bf16[1168,256]{1,0:T(8,128)(2,1)}, u32[]{:S(2)}, u32[]{:S(2)}) collective-permute-start(bf16[1168,256]{1,0:T(8,128)(2,1)} %get-tuple-element.27.refs_4_), channel_id=1, source_target_pairs={{0,32},{32,64},{64,96},{96,0},{1,33},{33,65},{65,97},{97,1},{2,34}... | collective-permute-start | bytes 1794056 | tf_op jit(solution)/shard_map/ppermute | solution.py:322
  57.2 3.2 %collective-permute-start.9 = (bf16[1088,256]{1,0:T(8,128)(2,1)}, bf16[1088,256]{1,0:T(8,128)(2,1)}, u32[]{:S(2)}, u32[]{:S(2)}) collective-permute-start(bf16[1088,256]{1,0:T(8,128)(2,1)} %get-tuple-element.26.refs_0_), channel_id=1, source_target_pairs={{0,24},{8,0},{16,8},{24,16},{1,25},{9,1},{17,9},{25,17},{2,26},{10... | collective-permute-start | bytes 1671176 | tf_op jit(solution)/shard_map/ppermute | solution.py:322
  60.4 4.0 %interleave.3 = (bf16[1632,256]{1,0:T(8,128)(2,1)}, bf16[1536,256]{1,0:T(8,128)(2,1)}, bf16[128,1024]{1,0:T(8,128)(2,1)}) custom-call(s32[2]{0:T(128)} %pad_add_fusion.pos, bf16[8,16,1408]{2,1,0:T(8,128)(2,1)} %copy-done.3, bf16[8,16,1408]{2,1,0:T(8,128)(2,1)} %copy-done.5, bf16[8,16,1408]{2,1,0:T(8,128)(2,1)} %copy-done.4, ...), custom_call_target="tpu_custom_call" | custom-call | tf_op jit(solution)/shard_map/interleave/pallas_call | solution.py:197
  64.4 4.9 %collective-permute-done.12.refs_3_ = bf16[144,256]{1,0:T(8,128)(2,1)S(1)} collective-permute-done((bf16[144,256]{1,0:T(8,128)(2,1)}, bf16[144,256]{1,0:T(8,128)(2,1)S(1)}, u32[]{:S(2)}, u32[]{:S(2)}) %collective-permute-start.12) | collective-permute-done | bytes 73760 | tf_op jit(solution)/shard_map/ppermute | solution.py:354
  69.3 2.9 %collective-permute-done.8.refs_1_ = bf16[1088,256]{1,0:T(8,128)(2,1)} collective-permute-done((bf16[1088,256]{1,0:T(8,128)(2,1)}, bf16[1088,256]{1,0:T(8,128)(2,1)}, u32[]{:S(2)}, u32[]{:S(2)}) %collective-permute-start.8) | collective-permute-done | bytes 557088 | tf_op jit(solution)/shard_map/ppermute | solution.py:322
  72.2 1.3 collective-permute-start.15
  73.5 2.3 %collective-permute-start.16 = (bf16[1536,256]{1,0:T(8,128)(2,1)}, bf16[1536,256]{1,0:T(8,128)(2,1)}, u32[]{:S(2)}, u32[]{:S(2)}) collective-permute-start(bf16[1536,256]{1,0:T(8,128)(2,1)} %get-tuple-element.42.refs_4_), channel_id=1, source_target_pairs={{0,96},{32,0},{64,32},{96,64},{1,97},{33,1},{65,33},{97,65},{2,98}... | collective-permute-start | bytes 2359304 | tf_op jit(solution)/shard_map/ppermute | solution.py:358
  75.8 0.5 collective-permute-start.13
  76.3 3.0 %arrange_left.1 = bf16[528,128]{1,0:T(8,128)(2,1)} custom-call(s32[2]{0:T(128)} %pad_add_fusion.pos, bf16[144,256]{1,0:T(8,128)(2,1)} %get-tuple-element.30.refs_0_, bf16[1168,256]{1,0:T(8,128)(2,1)} %collective-permute-done.10.refs_1_.refs_5_, bf16[1168,256]{1,0:T(8,128)(2,1)} %copy-done.6, bf16[144,256]{1,0:T(8,128)(2,1)} %copy-done.8), custom_call_target="tpu_custom_call" | custom-call | tf_op jit(solution)/shard_map/arrange_left/pallas_call | solution.py:245
  79.3 7.3 %all-gather = bf16[2112,128]{1,0:T(8,128)(2,1)} all-gather(bf16[528,128]{1,0:T(8,128)(2,1)} %arrange_left.1), channel_id=2, replica_groups=mesh['x'=4,'z'=4,'yh'=2,'yl'=2,'core'=2] {'yl','core'}, dimensions={0}, use_global_device_ids=true | all-gather | bytes 675840 | tf_op jit(solution)/shard_map/all_gather | solution.py:360
  86.6 0.3 collective-permute-done.13.refs_3_
  86.8 0.4 collective-permute-done.14.refs_7_
  87.3 0.5 collective-permute-done.16.refs_6_
  87.8 2.7 %collective-permute-start.18 = (bf16[1632,256]{1,0:T(8,128)(2,1)}, bf16[1632,256]{1,0:T(8,128)(2,1)}, u32[]{:S(2)}, u32[]{:S(2)}) collective-permute-start(bf16[1632,256]{1,0:T(8,128)(2,1)} %collective-permute-done.15.refs_2_), channel_id=1, source_target_pairs={{0,24},{8,0},{16,8},{24,16},{1,25},{9,1},{17,9},{25,17},{2,26},{10... | collective-permute-start | bytes 2506760 | tf_op jit(solution)/shard_map/ppermute | solution.py:365
  90.6 3.1 %collective-permute-start.20 = (bf16[1536,256]{1,0:T(8,128)(2,1)}, bf16[1536,256]{1,0:T(8,128)(2,1)}, u32[]{:S(2)}, u32[]{:S(2)}) collective-permute-start(bf16[1536,256]{1,0:T(8,128)(2,1)} %collective-permute-done.16.refs_6_), channel_id=1, source_target_pairs={{0,96},{32,0},{64,32},{96,64},{1,97},{33,1},{65,33},{97,65},{2,98}... | collective-permute-start | bytes 2359304 | tf_op jit(solution)/shard_map/ppermute | solution.py:365
  93.8 16.8 %pair.2.refs_8_ = bf16[32,1280,128]{2,1,0:T(8,128)(2,1)} custom-call(bf16[4,528,128]{2,1,0:T(8,128)(2,1)} %bitcast.12, bf16[128,1024]{1,0:T(8,128)(2,1)} %get-tuple-element.39.w_ref, bf16[1088,256]{1,0:T(8,128)(2,1)} %get-tuple-element.26.refs_0_, bf16[1088,256]{1,0:T(8,128)(2,1)} %collective-permute-done.8.refs_1_, ...), custom_call_target="tpu_custom_call" | custom-call | tf_op jit(solution)/shard_map/pair/pallas_call | solution.py:299
  110.6 0.2 collective-permute-done.19.refs_5_
  110.8 0.9 copy-done.7
  111.7 24.0 %pair.3 = bf16[32,1280,128]{2,1,0:T(8,128)(2,1)} custom-call(bf16[4,528,128]{2,1,0:T(8,128)(2,1)} %bitcast.13, bf16[128,1024]{1,0:T(8,128)(2,1)} %get-tuple-element.39.w_ref, bf16[1632,256]{1,0:T(8,128)(2,1)} %get-tuple-element.40.refs_0_, bf16[1632,256]{1,0:T(8,128)(2,1)} %copy-done.7, ...), custom_call_target="tpu_custom_call", output_to_operand_aliasing={{}: (10, {})} | custom-call | tf_op jit(solution)/shard_map/pair/pallas_call | solution.py:299
  (45 shorter events, 0.6 us)
Async XLA Ops:
  23.5 28.0 %copy-start = (bf16[8,16,1664]{2,1,0:T(8,128)(2,1)}, bf16[8,16,1664]{2,1,0:T(8,128)(2,1)S(1)}, u32[]{:S(2)}) copy-start(bf16[8,16,1664]{2,1,0:T(8,128)(2,1)S(1)} %pad_maximum_fusion.refs_5_.refs_15_.refs_20_.refs_25_) | copy-start | bytes 1277956
  23.5 12.8 %collective-permute-start.5 = (bf16[8,16,1664]{2,1,0:T(8,128)(2,1)S(1)}, bf16[8,16,1664]{2,1,0:T(8,128)(2,1)S(1)}, u32[]{:S(2)}, u32[]{:S(2)}) collective-permute-start(bf16[8,16,1664]{2,1,0:T(8,128)(2,1)S(1)} %pad_maximum_fusion.refs_5_.refs_15_.refs_20_.refs_25_), channel_id=1, source_target_pairs={{0,24},{8,0},{16,8},{24,16},{1,25},{9,1},{17,9},{25,17},{2,26},{10... | collective-permute-start | bytes 1277960 | tf_op jit(solution)/shard_map/ppermute | solution.py:322
  27.6 12.5 %collective-permute-start.4 = (bf16[8,16,1664]{2,1,0:T(8,128)(2,1)S(1)}, bf16[8,16,1664]{2,1,0:T(8,128)(2,1)S(1)}, u32[]{:S(2)}, u32[]{:S(2)}) collective-permute-start(bf16[8,16,1664]{2,1,0:T(8,128)(2,1)S(1)} %pad_maximum_fusion.refs_5_.refs_15_.refs_20_.refs_25_), channel_id=1, source_target_pairs={{0,8},{8,16},{16,24},{24,0},{1,9},{9,17},{17,25},{25,1},{2,10},{10... | collective-permute-start | bytes 1277960 | tf_op jit(solution)/shard_map/ppermute | solution.py:322
  27.7 13.3 %copy-start.3 = (bf16[8,16,1408]{2,1,0:T(8,128)(2,1)}, bf16[8,16,1408]{2,1,0:T(8,128)(2,1)S(1)}, u32[]{:S(2)}) copy-start(bf16[8,16,1408]{2,1,0:T(8,128)(2,1)S(1)} %slice.28.refs_0_.refs_10_) | copy-start | bytes 1081348
  27.7 13.4 %collective-permute-start.1 = (bf16[8,16,1408]{2,1,0:T(8,128)(2,1)S(1)}, bf16[8,16,1408]{2,1,0:T(8,128)(2,1)S(1)}, u32[]{:S(2)}, u32[]{:S(2)}) collective-permute-start(bf16[8,16,1408]{2,1,0:T(8,128)(2,1)S(1)} %slice.28.refs_0_.refs_10_), channel_id=1, source_target_pairs={{0,96},{32,0},{64,32},{96,64},{1,97},{33,1},{65,33},{97,65},{2,98}... | collective-permute-start | bytes 1081352 | tf_op jit(solution)/shard_map/ppermute | solution.py:322
  30.5 13.4 %collective-permute-start = (bf16[8,16,1408]{2,1,0:T(8,128)(2,1)S(1)}, bf16[8,16,1408]{2,1,0:T(8,128)(2,1)S(1)}, u32[]{:S(2)}, u32[]{:S(2)}) collective-permute-start(bf16[8,16,1408]{2,1,0:T(8,128)(2,1)S(1)} %slice.28.refs_0_.refs_10_), channel_id=1, source_target_pairs={{0,32},{32,64},{64,96},{96,0},{1,33},{33,65},{65,97},{97,1},{2,34}... | collective-permute-start | bytes 1081352 | tf_op jit(solution)/shard_map/ppermute | solution.py:322
  36.3 15.1 %copy-start.1 = (bf16[8,16,1664]{2,1,0:T(8,128)(2,1)}, bf16[8,16,1664]{2,1,0:T(8,128)(2,1)S(1)}, u32[]{:S(2)}) copy-start(bf16[8,16,1664]{2,1,0:T(8,128)(2,1)S(1)} %collective-permute-done.5.refs_7_.refs_17_.refs_22_.refs_27_) | copy-start | bytes 1277956
  36.4 15.1 %collective-permute-start.7 = (bf16[4,16,1664]{2,1,0:T(8,128)(2,1)S(1)}, bf16[4,16,1664]{2,1,0:T(8,128)(2,1)}, u32[]{:S(2)}, u32[]{:S(2)}) collective-permute-start(bf16[4,16,1664]{2,1,0:T(8,128)(2,1)S(1)} %slice.34), channel_id=1, source_target_pairs={{0,24},{8,0},{16,8},{24,16},{1,25},{9,1},{17,9},{25,17},{2,26},{10... | collective-permute-start | bytes 638984 | tf_op jit(solution)/shard_map/ppermute | solution.py:328
  40.1 0.8 copy-start.2
  41.0 10.5 %collective-permute-start.6 = (bf16[4,16,1664]{2,1,0:T(8,128)(2,1)S(1)}, bf16[4,16,1664]{2,1,0:T(8,128)(2,1)}, u32[]{:S(2)}, u32[]{:S(2)}) collective-permute-start(bf16[4,16,1664]{2,1,0:T(8,128)(2,1)S(1)} %slice.33), channel_id=1, source_target_pairs={{0,8},{8,16},{16,24},{24,0},{1,9},{9,17},{17,25},{25,1},{2,10},{10... | collective-permute-start | bytes 638984 | tf_op jit(solution)/shard_map/ppermute | solution.py:328
  41.1 2.9 %copy-start.4 = (bf16[8,16,1408]{2,1,0:T(8,128)(2,1)}, bf16[8,16,1408]{2,1,0:T(8,128)(2,1)S(1)}, u32[]{:S(2)}) copy-start(bf16[8,16,1408]{2,1,0:T(8,128)(2,1)S(1)} %collective-permute-done.1.refs_2_.refs_12_) | copy-start | bytes 1081348
  41.1 5.8 %collective-permute-start.3 = (bf16[4,16,1408]{2,1,0:T(8,128)(2,1)S(1)}, bf16[4,16,1408]{2,1,0:T(8,128)(2,1)}, u32[]{:S(2)}, u32[]{:S(2)}) collective-permute-start(bf16[4,16,1408]{2,1,0:T(8,128)(2,1)S(1)} %slice.30), channel_id=1, source_target_pairs={{0,96},{32,0},{64,32},{96,64},{1,97},{33,1},{65,33},{97,65},{2,98}... | collective-permute-start | bytes 540680 | tf_op jit(solution)/shard_map/ppermute | solution.py:328
  43.9 0.7 copy-start.5
  44.7 6.8 %collective-permute-start.2 = (bf16[4,16,1408]{2,1,0:T(8,128)(2,1)S(1)}, bf16[4,16,1408]{2,1,0:T(8,128)(2,1)}, u32[]{:S(2)}, u32[]{:S(2)}) collective-permute-start(bf16[4,16,1408]{2,1,0:T(8,128)(2,1)S(1)} %slice.29), channel_id=1, source_target_pairs={{0,32},{32,64},{64,96},{96,0},{1,33},{33,65},{65,97},{97,1},{2,34}... | collective-permute-start | bytes 540680 | tf_op jit(solution)/shard_map/ppermute | solution.py:328
  55.1 17.1 %collective-permute-start.11 = (bf16[1168,256]{1,0:T(8,128)(2,1)}, bf16[1168,256]{1,0:T(8,128)(2,1)S(1)}, u32[]{:S(2)}, u32[]{:S(2)}) collective-permute-start(bf16[1168,256]{1,0:T(8,128)(2,1)} %get-tuple-element.27.refs_4_), channel_id=1, source_target_pairs={{0,96},{32,0},{64,32},{96,64},{1,97},{33,1},{65,33},{97,65},{2,98}... | collective-permute-start | bytes 1794056 | tf_op jit(solution)/shard_map/ppermute | solution.py:322
  55.2 17.0 %collective-permute-start.10 = (bf16[1168,256]{1,0:T(8,128)(2,1)}, bf16[1168,256]{1,0:T(8,128)(2,1)}, u32[]{:S(2)}, u32[]{:S(2)}) collective-permute-start(bf16[1168,256]{1,0:T(8,128)(2,1)} %get-tuple-element.27.refs_4_), channel_id=1, source_target_pairs={{0,32},{32,64},{64,96},{96,0},{1,33},{33,65},{65,97},{97,1},{2,34}... | collective-permute-start | bytes 1794056 | tf_op jit(solution)/shard_map/ppermute | solution.py:322
  57.2 12.1 %collective-permute-start.9 = (bf16[1088,256]{1,0:T(8,128)(2,1)}, bf16[1088,256]{1,0:T(8,128)(2,1)}, u32[]{:S(2)}, u32[]{:S(2)}) collective-permute-start(bf16[1088,256]{1,0:T(8,128)(2,1)} %get-tuple-element.26.refs_0_), channel_id=1, source_target_pairs={{0,24},{8,0},{16,8},{24,16},{1,25},{9,1},{17,9},{25,17},{2,26},{10... | collective-permute-start | bytes 1671176 | tf_op jit(solution)/shard_map/ppermute | solution.py:322
  60.4 11.8 %collective-permute-start.8 = (bf16[1088,256]{1,0:T(8,128)(2,1)}, bf16[1088,256]{1,0:T(8,128)(2,1)}, u32[]{:S(2)}, u32[]{:S(2)}) collective-permute-start(bf16[1088,256]{1,0:T(8,128)(2,1)} %get-tuple-element.26.refs_0_), channel_id=1, source_target_pairs={{0,8},{8,16},{16,24},{24,0},{1,9},{9,17},{17,25},{25,1},{2,10},{10... | collective-permute-start | bytes 1671176 | tf_op jit(solution)/shard_map/ppermute | solution.py:322
  60.4 8.9 %collective-permute-start.12 = (bf16[144,256]{1,0:T(8,128)(2,1)}, bf16[144,256]{1,0:T(8,128)(2,1)S(1)}, u32[]{:S(2)}, u32[]{:S(2)}) collective-permute-start(bf16[144,256]{1,0:T(8,128)(2,1)} %get-tuple-element.30.refs_0_), channel_id=1, source_target_pairs={{0,64},{32,96},{64,0},{96,32},{1,65},{33,97},{65,1},{97,33},{2,66}... | collective-permute-start | bytes 221192 | tf_op jit(solution)/shard_map/ppermute | solution.py:354
  69.3 7.0 %copy-start.8 = (bf16[144,256]{1,0:T(8,128)(2,1)}, bf16[144,256]{1,0:T(8,128)(2,1)S(1)}, u32[]{:S(2)}) copy-start(bf16[144,256]{1,0:T(8,128)(2,1)S(1)} %collective-permute-done.12.refs_3_) | copy-start | bytes 221188
  72.2 4.1 %copy-start.6 = (bf16[1168,256]{1,0:T(8,128)(2,1)}, bf16[1168,256]{1,0:T(8,128)(2,1)S(1)}, u32[]{:S(2)}) copy-start(bf16[1168,256]{1,0:T(8,128)(2,1)S(1)} %collective-permute-done.11.refs_2_.refs_6_) | copy-start | bytes 1794052
  72.2 15.7 %collective-permute-start.15 = (bf16[1632,256]{1,0:T(8,128)(2,1)}, bf16[1632,256]{1,0:T(8,128)(2,1)}, u32[]{:S(2)}, u32[]{:S(2)}) collective-permute-start(bf16[1632,256]{1,0:T(8,128)(2,1)} %get-tuple-element.40.refs_0_), channel_id=1, source_target_pairs={{0,24},{8,0},{16,8},{24,16},{1,25},{9,1},{17,9},{25,17},{2,26},{10... | collective-permute-start | bytes 2506760 | tf_op jit(solution)/shard_map/ppermute | solution.py:358
  73.5 14.3 %collective-permute-start.16 = (bf16[1536,256]{1,0:T(8,128)(2,1)}, bf16[1536,256]{1,0:T(8,128)(2,1)}, u32[]{:S(2)}, u32[]{:S(2)}) collective-permute-start(bf16[1536,256]{1,0:T(8,128)(2,1)} %get-tuple-element.42.refs_4_), channel_id=1, source_target_pairs={{0,96},{32,0},{64,32},{96,64},{1,97},{33,1},{65,33},{97,65},{2,98}... | collective-permute-start | bytes 2359304 | tf_op jit(solution)/shard_map/ppermute | solution.py:358
  75.8 11.5 %collective-permute-start.14 = (bf16[1168,256]{1,0:T(8,128)(2,1)}, bf16[1168,256]{1,0:T(8,128)(2,1)}, u32[]{:S(2)}, u32[]{:S(2)}) collective-permute-start(bf16[1168,256]{1,0:T(8,128)(2,1)} %collective-permute-done.10.refs_1_.refs_5_), channel_id=1, source_target_pairs={{0,32},{32,64},{64,96},{96,0},{1,33},{33,65},{65,97},{97,1},{2,34}... | collective-permute-start | bytes 1794056 | tf_op jit(solution)/shard_map/ppermute | solution.py:357
  75.8 11.1 %collective-permute-start.13 = (bf16[1088,256]{1,0:T(8,128)(2,1)}, bf16[1088,256]{1,0:T(8,128)(2,1)}, u32[]{:S(2)}, u32[]{:S(2)}) collective-permute-start(bf16[1088,256]{1,0:T(8,128)(2,1)} %collective-permute-done.8.refs_1_), channel_id=1, source_target_pairs={{0,8},{8,16},{16,24},{24,0},{1,9},{9,17},{17,25},{25,1},{2,10},{10... | collective-permute-start | bytes 1671176 | tf_op jit(solution)/shard_map/ppermute | solution.py:357
  87.3 23.5 %collective-permute-start.17 = (bf16[1632,256]{1,0:T(8,128)(2,1)}, bf16[1632,256]{1,0:T(8,128)(2,1)S(1)}, u32[]{:S(2)}, u32[]{:S(2)}) collective-permute-start(bf16[1632,256]{1,0:T(8,128)(2,1)} %get-tuple-element.40.refs_0_), channel_id=1, source_target_pairs={{0,8},{8,16},{16,24},{24,0},{1,9},{9,17},{17,25},{25,1},{2,10},{10... | collective-permute-start | bytes 2506760 | tf_op jit(solution)/shard_map/ppermute | solution.py:363
  87.8 22.9 %collective-permute-start.18 = (bf16[1632,256]{1,0:T(8,128)(2,1)}, bf16[1632,256]{1,0:T(8,128)(2,1)}, u32[]{:S(2)}, u32[]{:S(2)}) collective-permute-start(bf16[1632,256]{1,0:T(8,128)(2,1)} %collective-permute-done.15.refs_2_), channel_id=1, source_target_pairs={{0,24},{8,0},{16,8},{24,16},{1,25},{9,1},{17,9},{25,17},{2,26},{10... | collective-permute-start | bytes 2506760 | tf_op jit(solution)/shard_map/ppermute | solution.py:365
  90.5 20.2 %collective-permute-start.19 = (bf16[1536,256]{1,0:T(8,128)(2,1)}, bf16[1536,256]{1,0:T(8,128)(2,1)}, u32[]{:S(2)}, u32[]{:S(2)}) collective-permute-start(bf16[1536,256]{1,0:T(8,128)(2,1)} %get-tuple-element.42.refs_4_), channel_id=1, source_target_pairs={{0,32},{32,64},{64,96},{96,0},{1,33},{33,65},{65,97},{97,1},{2,34}... | collective-permute-start | bytes 2359304 | tf_op jit(solution)/shard_map/ppermute | solution.py:363
  90.6 20.2 %collective-permute-start.20 = (bf16[1536,256]{1,0:T(8,128)(2,1)}, bf16[1536,256]{1,0:T(8,128)(2,1)}, u32[]{:S(2)}, u32[]{:S(2)}) collective-permute-start(bf16[1536,256]{1,0:T(8,128)(2,1)} %collective-permute-done.16.refs_6_), channel_id=1, source_target_pairs={{0,96},{32,0},{64,32},{96,64},{1,97},{33,1},{65,33},{97,65},{2,98}... | collective-permute-start | bytes 2359304 | tf_op jit(solution)/shard_map/ppermute | solution.py:365
  110.8 0.9 copy-start.7

commit v6 on v5

--- a/solution.py
+++ b/solution.py
@@ -73,8 +73,12 @@
         @pl.when(step == 0)
         def _():
             m = m_ref[0, :, :left_rows]
-            y = affine(wl_ref, turned(bl_ref), normed[:left_rows, :], m)
-            y = jnp.concatenate([y, jnp.broadcast_to(m, (16, left_rows))], axis=0).astype(bf16)
+            y = affine(wl_ref, turned(bl_ref), normed[:left_rows, :], m).astype(bf16)
+            for yh in range(2):
+                first = [(x * 8 + z * 2 + yh) * RD for x in range(4) for z in range(4)]
+                pieces = [m[:, at : at + RD] for at in first]
+                lines = [jnp.concatenate(pieces[4 * x : 4 * x + 4], axis=1) for x in range(4)]
+                left_mask[yh] = jnp.concatenate(lines + [jnp.zeros((4, TILE), f32)], axis=0)
 
             def regroup(src, dst):
                 return src == ((dst >> 3) & 3) * 64 + (dst >> 5) * 8 + (dst & 7)
@@ -83,16 +87,14 @@
             y = [move(y[:, k * 256 : (k + 1) * 256], choose) for k in range(4)]
             for device in range(8):
                 tile = jnp.concatenate([t[:, device * 32 : (device + 1) * 32] for t in y], axis=1)
-                left[device] = tile[:width]
-                left_mask[device] = tile[width:]
+                left[device] = tile
 
         m = [m_ref[0, :, k * TILE : (k + 1) * TILE] for k in range(quarter // TILE)]
-        m = jnp.concatenate(m + [jnp.zeros((16 - len(m), TILE), f32)], axis=0).astype(bf16)
+        zeros = jnp.zeros((width - 4 - len(m), TILE), f32)
         for yh in range(2):
-            device = yh * 4 + step
-            out_ref[yh, 0, :16, quarter : quarter + TILE] = m
-            out_ref[yh, 0, 16:, quarter : quarter + TILE] = left_mask[device]
-            out_ref[yh, 0, :, quarter + TILE :] = left[device]
+            tile = jnp.concatenate(m + [left_mask[yh, :4, :], zeros], axis=0)
+            out_ref[yh, 0, :, quarter : quarter + TILE] = tile.astype(bf16)
+            out_ref[yh, 0, :, quarter + TILE :] = left[yh * 4 + step]
 
     return pl.pallas_call(
         kernel,
@@ -112,7 +114,7 @@
         scratch_shapes=[
             pltpu.VMEM((quarter, features), bf16),
             pltpu.VMEM((8, width, TILE), bf16),
-            pltpu.VMEM((8, 16, TILE), bf16),
+            pltpu.VMEM((2, 8, TILE), f32),
         ],
         compiler_params=vmem(),
         name="project",
@@ -125,29 +127,32 @@
 
 def interleave(position, first, second, columns, start, chunks, w_out=None):
     tiles = CHUNK // TILE
-    sizes = (8, 8, 8, 4, 4)
+    sizes = [[t.shape[0] for t in held] for held in (first, second)]
+    cut = len(first)
     heights = (544, 512)
-    extra = 0 if w_out is not None else 144
+    extra = (16, 128) if w_out is None else (0, 0)
     width = 32
     mask_tile = columns // TILE
 
     def by_row(ins, lane):
-        own, before, after, low, high = ins
         at = slice(lane * TILE, (lane + 1) * TILE)
-        parts = [own[:, :, at], before[:, :, at], after[:, :, at], low[:, :, at], high[:, :, at]]
+        parts = [r[:, :, at] for r in ins]
         near = jnp.swapaxes(jnp.concatenate(parts[:2], axis=0), 0, 1)
         away = jnp.swapaxes(jnp.concatenate(parts[2:], axis=0), 0, 1)
         return jnp.concatenate([near, away], axis=1).reshape(512, TILE)
 
     def kernel(pos, *refs):
-        main, masks, rest, outs = refs[:10], refs[10:15], refs[15:-3], refs[-3:]
-        mask_rows = by_row(masks, 0)
+        n = cut + len(second)
+        halves, masks = (refs[:cut], refs[cut:n]), refs[n : n + cut]
+        rest, outs = refs[n + cut : -1 - len(shapes)], refs[-1 - len(shapes) : -1]
+        mask_rows = refs[-1]
+        mask_rows[...] = by_row(masks, 0)
         for chunk in range(chunks):
             for half in range(2):
                 base = chunk * heights[half]
                 for lane in range(tiles):
                     at = slice(lane * TILE, (lane + 1) * TILE)
-                    rows = by_row(main[5 * half : 5 * half + 5], chunk * tiles + lane)
+                    rows = by_row(halves[half], chunk * tiles + lane)
                     outs[half][base : base + 512, at] = rows
                     if half == 0:
                         row = ((start + chunk) * tiles + lane) * 32
@@ -165,14 +170,17 @@
             return one_hot(TILE, TILE, pick)
 
         choose = [mine(group) for group in range(4)]
-        left_masks, *lefts = [by_row(rest[5 * k : 5 * k + 5], 0) for k in range(3)]
-        for lane, rows in enumerate(lefts):
+        n = len(second)
+        for lane in range(2):
             at = slice(lane * TILE, (lane + 1) * TILE)
+            rows = by_row(rest[n * lane : n * lane + n], 0)
             parts = [rows[g * 128 : (g + 1) * 128] for g in range(4)]
             parts = [jnp.dot(v, c, preferred_element_type=f32) for v, c in zip(parts, choose)]
-            outs[2][:128, at] = sum(parts[1:], parts[0]).astype(bf16)
-            outs[2][128:, at] = move(left_masks[lane * 16 : (lane + 1) * 16], choose[0])
-        outs[1][chunks * 512 :, :] = outs[2][...]
+            outs[2][:, at] = sum(parts[1:], parts[0]).astype(bf16)
+            row = (mask_tile + pos[0]) * 32 + lane * 16
+            outs[0][chunks * heights[0] :, at] = mask_rows[pl.ds(pl.multiple_of(row, 16), 16), :]
+        outs[1][chunks * heights[1] :, :] = outs[2][...]
+        outs[3][...] = one_hot(RD, TILE, lambda row, lane: lane == pos[1] * RD + row)
 
     def blocks(m):
         span = chunks * CHUNK
@@ -183,13 +191,13 @@
     def tile_blocks(m, tile):
         return pl.BlockSpec((m, 16, TILE), lambda _, pos: (0, 0, tile))
 
-    specs = [blocks(m) for m in sizes] * 2 + [tile_blocks(m, mask_tile) for m in sizes]
+    specs = [blocks(m) for held in sizes for m in held] + [tile_blocks(m, mask_tile) for m in sizes[0]]
     args = (*first, *second, *first)
-    shapes = [(chunks * heights[0], CHUNK), (chunks * heights[1] + extra, CHUNK)]
+    shapes = [(chunks * heights[half] + extra[half], CHUNK) for half in range(2)]
     if w_out is None:
-        specs += [tile_blocks(m, mask_tile + k) for k in (0, 2, 1) for m in sizes]
-        args += (*second, *second, *second)
-        shapes.append((extra, CHUNK))
+        specs += [tile_blocks(m, mask_tile + k) for k in (1, 0) for m in sizes[1]]
+        args += (*second, *second)
+        shapes += [(extra[1], CHUNK), (RD, TILE)]
     else:
         specs.append(whole(*w_out.shape))
         args += (w_out,)
@@ -201,6 +209,7 @@
             grid=(1,),
             in_specs=specs,
             out_specs=tuple(whole(*shape) for shape in shapes),
+            scratch_shapes=[pltpu.VMEM((512, TILE), bf16)],
         ),
         out_shape=tuple(jax.ShapeDtypeStruct(shape, bf16) for shape in shapes),
         compiler_params=vmem(),
@@ -232,14 +241,7 @@
             c = dst & 31
             return src == (c >> 4) * 128 + (c & 3) * 32 + (dst >> 5) * 4 + ((c >> 2) & 3)
 
-        held = move(one_hot(256, 256, regroup), jnp.concatenate(held, axis=0))
-        swap = one_hot(128, 128, lambda k, to: to == ((k >> 3) & 3) * 32 + (k >> 5) * 8 + (k & 7))
-        out_ref[:256, :] = move(held, swap)
-        out_ref[256:512, :] = held
-        masks = [sequences(slice(128, 144), lane) for lane in range(2)]
-        masks = [masks[lane][place] for place in range(4) for lane in range(2)]
-        choose = one_hot(16, TILE, lambda row, lane: lane == pos[0] * 8 + row)
-        out_ref[512:, :] = move(turn(choose, jnp.concatenate(masks, axis=0)), swap)
+        out_ref[...] = move(one_hot(256, 256, regroup), jnp.concatenate(held, axis=0))
 
     part = pl.BlockSpec((pl.Element(height), pl.Element(CHUNK)), lambda _, pos: (base, 0))
     return pl.pallas_call(
@@ -248,35 +250,38 @@
             num_scalar_prefetch=1,
             grid=(1,),
             in_specs=[whole(*own.shape), part, part, whole(*far.shape)],
-            out_specs=whole(528, 128),
+            out_specs=whole(256, 128),
         ),
-        out_shape=jax.ShapeDtypeStruct((528, 128), bf16),
+        out_shape=jax.ShapeDtypeStruct((256, 128), bf16),
         compiler_params=vmem(),
         name="arrange_left",
     )(position, own, before, after, far)
 
 
-def pair(left, weight, first, second, start, chunks, result, columns):
+def pair(left, weight, mine, masks, first, second, start, chunks, result, columns):
     out_width = weight.shape[0]
     earlier = () if result is None else (result,)
 
-    def kernel(left_ref, w_ref, *refs):
-        ins = refs[:8]
+    def kernel(left_ref, w_ref, mine_ref, *refs):
+        mask_refs, ins = refs[:4], refs[4:12]
         out_ref, outer, scale, l1, l2, row_mask = refs[-6:]
 
         @pl.when(pl.program_id(0) == 0)
         def _():
-            for device in range(4):
-                at = slice(device * 256, (device + 1) * 256)
-                l1[at, :] = left_ref[device, :256, :]
-                l2[at, :] = left_ref[device, 256:512, :]
-                row_mask[device * 8 : (device + 1) * 8, :] = left_ref[device, 512:, :].astype(f32)[:8]
+            l2[...] = left_ref[...].reshape(RD * 32, 128)
+            swap = one_hot(128, 128, lambda k, to: to == ((k >> 3) & 3) * 32 + (k >> 5) * 8 + (k & 7))
+            l1[...] = move(l2[...], swap)
+            parts = [r[:, lane * TILE : (lane + 1) * TILE] for r in mask_refs for lane in range(2)]
+            row_mask[...] = lax.dot_general(
+                mine_ref[...], jnp.concatenate(parts, axis=0), (((1,), (1,)), ((), ())),
+                preferred_element_type=f32,
+            ).astype(bf16)
 
         def sequences(half, row):
             at = slice(row * 32, row * 32 + 32)
             return jnp.concatenate([r[at, :] for r in ins[4 * half : 4 * half + 4]], axis=0)
 
-        count = jnp.dot(row_mask[...].astype(bf16), sequences(0, 16), preferred_element_type=f32)
+        count = jnp.dot(row_mask[...], sequences(0, 16), preferred_element_type=f32)
         scale[...] = 1.0 / (0.001 + count)
 
         def rows_of(group, _):
@@ -300,7 +305,8 @@
         kernel,
         grid=(chunks,),
         out_shape=jax.ShapeDtypeStruct((RD, columns, out_width), bf16),
-        in_specs=[whole(*left.shape), whole(*weight.shape)]
+        in_specs=[whole(*left.shape), whole(*weight.shape), whole(*mine.shape)]
+        + [pl.BlockSpec((16, CHUNK), lambda j: (2 * 544 // 16, 0))] * 4
         + blocks
         + [pl.BlockSpec(memory_space=pl.ANY)] * len(earlier),
         out_specs=pl.BlockSpec((RD, CHUNK, out_width), lambda j: (0, start + j, 0)),
@@ -309,12 +315,12 @@
             pltpu.VMEM((RD, CHUNK), f32),
             pltpu.VMEM((1024, 128), bf16),
             pltpu.VMEM((1024, 128), bf16),
-            pltpu.VMEM((RD, 128), f32),
+            pltpu.VMEM((RD, 128), bf16),
         ],
-        input_output_aliases={10: 0} if earlier else {},
+        input_output_aliases={15: 0} if earlier else {},
         compiler_params=vmem(),
         name="pair",
-    )(left, weight, *first, *second, *earlier)
+    )(left, weight, mine, *masks, *first, *second, *earlier)
 
 
 def send_both(blocks):
@@ -343,13 +349,17 @@
 
     halves = (
         right[:, :16, : columns + TILE],
-        jnp.concatenate([right[:, 16:], right[:, :16, columns + TILE :]], axis=2),
+        jnp.concatenate(
+            [right[:, 16:, :columns], right[:, 16:, columns + TILE :], right[:, :16, columns + TILE :]], axis=2
+        ),
     )
     got = send_both(((halves[0], "x"), (halves[1], "z")))
-    far = send_on([((before[:4], after[4:]), axis) for (before, after), axis in zip(got, "xz")])
-    held = [(halves[h], *got[h], *far[h]) for h in range(2)]
-
-    *early, left = interleave(position, *held, columns, 0, 2)
+    far = lax.ppermute(got[0][0], "x", ring(1))
+    before, after = got[1]
+    (passed,) = send_on([((before[:4], after[4:]), "z")])
+    held = (halves[0], *got[0], far), (halves[1], before, after, *passed)
+
+    *early, left, mine = interleave(position, *held, columns, 0, 2)
     *late, weight = interleave(position, *held, columns, 2, chunks - 2, w_out)
     left_far = lax.ppermute(left, "x", ring(2))
     got = send_both(((early[0], "z"), (early[1], "x")))
@@ -365,8 +375,9 @@
     far = [lax.ppermute(block, axis, ring(-1)) for block, axis in zip(after, "zx")]
     late = [(late[h], before[h], after[h], far[h]) for h in range(2)]
 
-    result = pair(left, weight, *early, 0, 2, None, columns)
-    return pair(left, weight, *late, 2, chunks - 2, result, columns)
+    fixed = left, weight, mine, early[0]
+    result = pair(*fixed, *early, 0, 2, None, columns)
+    return pair(*fixed, *late, 2, chunks - 2, result, columns)
 
 
 def solution(mesh):

time: 136 us -> 132 us (0.971)
  waiting for transfers between devices: 21.3 us -> 19.1 us
    ppermute x4, waiting for transfers between devices: 5.84 us -> 2.15 us  [send_both(): lax.ppermute(block, axis, ring(-1))]
    ppermute x4, starting transfers between devices: 9.42 us -> 6.3 us  [on_device(): lax.ppermute(block, axis, ring(-1))]
    ppermute x2 -> x1, starting transfers between devices: 6.59 us -> 3.76 us  [send_on(): lax.ppermute(high, axis, ring(-1))]
    ppermute x1, starting transfers between devices: 0.01 us -> 2.73 us  [on_device(): left_far = lax.ppermute(left, 'x', ring(2))]
    ppermute x4, starting transfers between devices: 10.2 us -> 7.67 us  [send_both(): lax.ppermute(block, axis, ring(-1))]
    ppermute x2, starting transfers between devices: 0.51 us -> 2.67 us  [on_device(): lax.ppermute(before, axis, ring(1))]
    ppermute x4, starting transfers between devices: 2.02 us -> 3.87 us  [send_both(): lax.ppermute(block, axis, ring(1))]
    ppermute x2, starting transfers between devices: 0.16 us -> 1.55 us  [on_device(): lax.ppermute(block, axis, ring(1))]
  transfers between devices with their start and end apart: 21 -> 20, of which waited for: 9 -> 9; matrix products, arithmetic and copies ran while one was open for 0% -> 1% of each run, Pallas kernels for 18% -> 18%
where the time goes in v6:
time: 132 us
  Pallas kernels  57.2 us (43%)
  starting transfers between devices  28.8 us (22%)
  blocking collectives  24.2 us (18%)
  waiting for transfers between devices  19.1 us (14%)
  local copies, waits for them, and re-layouts  1.57 us (1%)
    pallas_call x2, Pallas kernels, pair(): pl.pallas_call(kernel, grid=(chunks,), out_shape=jax.ShapeDtypeStruct((RD...  41.3 us
    all_to_all x1, blocking collectives, on_device(): lax.all_to_all(right.reshape(8, width, -1), COLUMN, 0, 0, tiled=True)  17.8 us
    ppermute x4, starting transfers between devices, send_both(): lax.ppermute(block, axis, ring(-1))  7.67 us
    pallas_call x2, Pallas kernels, interleave(): pl.pallas_call(kernel, grid_spec=pltpu.PrefetchScalarGridSpec(num_scalar_...  7.53 us
    all_gather x1, blocking collectives, on_device(): left = lax.all_gather(left, narrow, axis=0)  6.43 us
    ppermute x4, starting transfers between devices, on_device(): lax.ppermute(block, axis, ring(-1))  6.3 us
    pallas_call x1, Pallas kernels, project(): pl.pallas_call(kernel, grid=(4,), out_shape=jax.ShapeDtypeStruct((2, 4, w...  5.61 us
    ppermute x1, waiting for transfers between devices, on_device(): left_far = lax.ppermute(left, 'x', ring(2))  5.45 us
  transfers between devices with their start and end apart: 20, of which 9 were waited for; matrix products, arithmetic and copies ran while one was open for 1% of the time, Pallas kernels for 18%

profile of v6, /device:TPU:0, one launch (start us, length us, event | category | flops | bytes accessed | tf_op | source)
XLA Modules:
  0.0 131.7 jit_solution(10957549039911137281)
XLA Ops:
  0.0 5.6 %project.1 = bf16[2,4,32,1536]{3,2,1,0:T(8,128)(2,1)} custom-call(bf16[5120,256]{1,0:T(8,128)(2,1)} %bitcast.13, f32[4,1,1280]{2,1,0:T(1,128)} %bitcast.16, f32[1,256]{1,0:T(1,128)} %bitcast.19, f32[1,256]{1,0:T(1,128)} %bitcast.20, bf16[32,256]{1,0:T(8,128)(2,1)} %bitcast.17, f32[1,32]{1,0:T(1,128)} %bitcast.21, bf16[32,256]{1,0:T(8,128)(2,1)} %bitcast.18, ...), custom_call_target="tpu_custom_call" | custom-call | tf_op jit(solution)/shard_map/project/pallas_call | solution.py:99
  5.6 17.8 %all_to_all.5 = bf16[8,32,1536]{2,1,0:T(8,128)(2,1)S(1)} all-to-all(bf16[8,32,1536]{2,1,0:T(8,128)(2,1)} %bitcast.12), channel_id=1, replica_groups=mesh['x'=4,'z'=4,'yh'=2,'yl'=2,'core'=2] {'yh','yl','core'}, dimensions={0} | all-to-all | bytes 1572864 | tf_op jit(solution)/shard_map/all_to_all | solution.py:348
  23.5 1.6 %collective-permute-start = (bf16[8,16,1408]{2,1,0:T(8,128)(2,1)S(1)}, bf16[8,16,1408]{2,1,0:T(8,128)(2,1)S(1)}, u32[]{:S(2)}, u32[]{:S(2)}) collective-permute-start(bf16[8,16,1408]{2,1,0:T(8,128)(2,1)S(1)} %slice.24.refs_0_.refs_9_), channel_id=1, source_target_pairs={{0,32},{32,64},{64,96},{96,0},{1,33},{33,65},{65,97},{97,1},{2,34}... | collective-permute-start | bytes 1081352 | tf_op jit(solution)/shard_map/ppermute | solution.py:328
  25.1 4.1 %collective-permute-start.4 = (bf16[8,16,1536]{2,1,0:T(8,128)(2,1)S(1)}, bf16[8,16,1536]{2,1,0:T(8,128)(2,1)S(1)}, u32[]{:S(2)}, u32[]{:S(2)}) collective-permute-start(bf16[8,16,1536]{2,1,0:T(8,128)(2,1)S(1)} %pad_maximum_fusion.refs_4_.refs_13_.refs_18_), channel_id=1, source_target_pairs={{0,24},{8,0},{16,8},{24,16},{1,25},{9,1},{17,9},{25,17},{2,26},{10... | collective-permute-start | bytes 1179656 | tf_op jit(solution)/shard_map/ppermute | solution.py:328
  29.2 1.7 %collective-permute-start.1 = (bf16[8,16,1408]{2,1,0:T(8,128)(2,1)S(1)}, bf16[8,16,1408]{2,1,0:T(8,128)(2,1)S(1)}, u32[]{:S(2)}, u32[]{:S(2)}) collective-permute-start(bf16[8,16,1408]{2,1,0:T(8,128)(2,1)S(1)} %slice.24.refs_0_.refs_9_), channel_id=1, source_target_pairs={{0,96},{32,0},{64,32},{96,64},{1,97},{33,1},{65,33},{97,65},{2,98}... | collective-permute-start | bytes 1081352 | tf_op jit(solution)/shard_map/ppermute | solution.py:328
  31.0 3.6 %collective-permute-done.refs_1_.refs_10_ = bf16[8,16,1408]{2,1,0:T(8,128)(2,1)S(1)} collective-permute-done((bf16[8,16,1408]{2,1,0:T(8,128)(2,1)S(1)}, bf16[8,16,1408]{2,1,0:T(8,128)(2,1)S(1)}, u32[]{:S(2)}, u32[]{:S(2)}) %collective-permute-start) | collective-permute-done | bytes 360480 | tf_op jit(solution)/shard_map/ppermute | solution.py:328
  34.8 2.1 %collective-permute-done.4.refs_6_.refs_15_.refs_20_ = bf16[8,16,1536]{2,1,0:T(8,128)(2,1)S(1)} collective-permute-done((bf16[8,16,1536]{2,1,0:T(8,128)(2,1)S(1)}, bf16[8,16,1536]{2,1,0:T(8,128)(2,1)S(1)}, u32[]{:S(2)}, u32[]{:S(2)}) %collective-permute-start.4) | collective-permute-done | bytes 393248 | tf_op jit(solution)/shard_map/ppermute | solution.py:328
  37.0 3.8 %collective-permute-start.6 = (bf16[4,16,1536]{2,1,0:T(8,128)(2,1)S(1)}, bf16[4,16,1536]{2,1,0:T(8,128)(2,1)S(1)}, u32[]{:S(2)}, u32[]{:S(2)}) collective-permute-start(bf16[4,16,1536]{2,1,0:T(8,128)(2,1)S(1)} %slice.29), channel_id=1, source_target_pairs={{0,24},{8,0},{16,8},{24,16},{1,25},{9,1},{17,9},{25,17},{2,26},{10... | collective-permute-start | bytes 589832 | tf_op jit(solution)/shard_map/ppermute | solution.py:334
  40.8 0.8 copy-done.3
  41.5 0.6 pad_add_fusion.pos
  42.1 1.8 %collective-permute-done.6.refs_8_.refs_17_.refs_22_ = bf16[4,16,1536]{2,1,0:T(8,128)(2,1)S(1)} collective-permute-done((bf16[4,16,1536]{2,1,0:T(8,128)(2,1)S(1)}, bf16[4,16,1536]{2,1,0:T(8,128)(2,1)S(1)}, u32[]{:S(2)}, u32[]{:S(2)}) %collective-permute-start.6) | collective-permute-done | bytes 196640 | tf_op jit(solution)/shard_map/ppermute | solution.py:334
  43.9 4.5 %collective-permute-done.5.refs_7_.refs_16_.refs_21_ = bf16[4,16,1536]{2,1,0:T(8,128)(2,1)S(1)} collective-permute-done((bf16[4,16,1536]{2,1,0:T(8,128)(2,1)S(1)}, bf16[4,16,1536]{2,1,0:T(8,128)(2,1)S(1)}, u32[]{:S(2)}, u32[]{:S(2)}) %collective-permute-start.5) | collective-permute-done | bytes 196640 | tf_op jit(solution)/shard_map/ppermute | solution.py:334
  48.4 0.7 copy-done.8
  49.1 3.5 %interleave.2 = (bf16[1104,256]{1,0:T(8,128)(2,1)}, bf16[1152,256]{1,0:T(8,128)(2,1)}, bf16[128,256]{1,0:T(8,128)(2,1)}, bf16[32,128]{1,0:T(8,128)(2,1)}) custom-call(s32[2]{0:T(128)} %pad_add_fusion.pos, bf16[8,16,1408]{2,1,0:T(8,128)(2,1)} %copy-done.1, bf16[8,16,1408]{2,1,0:T(8,128)(2,1)} %copy-done.4, bf16[8,16,1408]{2,1,0:T(8,128)(2,1)} %copy-done.5, ...), custom_call_target="tpu_custom_call" | custom-call | tf_op jit(solution)/shard_map/interleave/pallas_call | solution.py:205
  52.6 1.8 %collective-permute-start.10 = (bf16[1152,256]{1,0:T(8,128)(2,1)}, bf16[1152,256]{1,0:T(8,128)(2,1)}, u32[]{:S(2)}, u32[]{:S(2)}) collective-permute-start(bf16[1152,256]{1,0:T(8,128)(2,1)} %get-tuple-element.28.refs_8_), channel_id=1, source_target_pairs={{0,96},{32,0},{64,32},{96,64},{1,97},{33,1},{65,33},{97,65},{2,98}... | collective-permute-start | bytes 1769480 | tf_op jit(solution)/shard_map/ppermute | solution.py:328
  54.5 0.3 collective-permute-start.9
  54.7 2.0 %collective-permute-start.7 = (bf16[1104,256]{1,0:T(8,128)(2,1)}, bf16[1104,256]{1,0:T(8,128)(2,1)}, u32[]{:S(2)}, u32[]{:S(2)}) collective-permute-start(bf16[1104,256]{1,0:T(8,128)(2,1)} %get-tuple-element.27.refs_0_.refs_4_), channel_id=1, source_target_pairs={{0,8},{8,16},{16,24},{24,0},{1,9},{9,17},{17,25},{25,1},{2,10},{10... | collective-permute-start | bytes 1695752 | tf_op jit(solution)/shard_map/ppermute | solution.py:328
  56.8 2.7 %collective-permute-start.11 = (bf16[128,256]{1,0:T(8,128)(2,1)}, bf16[128,256]{1,0:T(8,128)(2,1)S(1)}, u32[]{:S(2)}, u32[]{:S(2)}) collective-permute-start(bf16[128,256]{1,0:T(8,128)(2,1)} %get-tuple-element.31.refs_0_), channel_id=1, source_target_pairs={{0,64},{32,96},{64,0},{96,32},{1,65},{33,97},{65,1},{97,33},{2,66}... | collective-permute-start | bytes 196616 | tf_op jit(solution)/shard_map/ppermute | solution.py:364
  59.5 4.0 %interleave.3 = (bf16[1632,256]{1,0:T(8,128)(2,1)}, bf16[1536,256]{1,0:T(8,128)(2,1)}, bf16[128,1024]{1,0:T(8,128)(2,1)}) custom-call(s32[2]{0:T(128)} %pad_add_fusion.pos, bf16[8,16,1408]{2,1,0:T(8,128)(2,1)} %copy-done.1, bf16[8,16,1408]{2,1,0:T(8,128)(2,1)} %copy-done.4, bf16[8,16,1408]{2,1,0:T(8,128)(2,1)} %copy-done.5, ...), custom_call_target="tpu_custom_call" | custom-call | tf_op jit(solution)/shard_map/interleave/pallas_call | solution.py:205
  63.5 5.5 %collective-permute-done.11.refs_3_ = bf16[128,256]{1,0:T(8,128)(2,1)S(1)} collective-permute-done((bf16[128,256]{1,0:T(8,128)(2,1)}, bf16[128,256]{1,0:T(8,128)(2,1)S(1)}, u32[]{:S(2)}, u32[]{:S(2)}) %collective-permute-start.11) | collective-permute-done | bytes 65568 | tf_op jit(solution)/shard_map/ppermute | solution.py:364
  69.3 1.2 collective-permute-start.15
  70.6 0.8 collective-permute-start.13
  71.3 1.9 %collective-permute-start.12 = (bf16[1104,256]{1,0:T(8,128)(2,1)}, bf16[1104,256]{1,0:T(8,128)(2,1)}, u32[]{:S(2)}, u32[]{:S(2)}) collective-permute-start(bf16[1104,256]{1,0:T(8,128)(2,1)} %collective-permute-done.7.refs_1_.refs_5_), channel_id=1, source_target_pairs={{0,8},{8,16},{16,24},{24,0},{1,9},{9,17},{17,25},{25,1},{2,10},{10... | collective-permute-start | bytes 1695752 | tf_op jit(solution)/shard_map/ppermute | solution.py:367
  73.2 2.7 %arrange_left.1 = bf16[256,128]{1,0:T(8,128)(2,1)} custom-call(s32[2]{0:T(128)} %pad_add_fusion.pos, bf16[128,256]{1,0:T(8,128)(2,1)} %get-tuple-element.31.refs_0_, bf16[1152,256]{1,0:T(8,128)(2,1)} %collective-permute-done.9.refs_1_.refs_9_, bf16[1152,256]{1,0:T(8,128)(2,1)} %collective-permute-done.10.refs_2_.refs_10_, bf16[128,256]{1,0:T(8,128)(2,1)} %copy-done.9), custom_call_target="tpu_custom_call" | custom-call | tf_op jit(solution)/shard_map/arrange_left/pallas_call | solution.py:247
  75.9 6.4 %all-gather = bf16[1024,128]{1,0:T(8,128)(2,1)} all-gather(bf16[256,128]{1,0:T(8,128)(2,1)} %arrange_left.1), channel_id=2, replica_groups=mesh['x'=4,'z'=4,'yh'=2,'yl'=2,'core'=2] {'yl','core'}, dimensions={0}, use_global_device_ids=true | all-gather | bytes 327680 | tf_op jit(solution)/shard_map/all_gather | solution.py:370
  82.5 1.3 collective-permute-start.16
  83.8 0.7 collective-permute-done.15.refs_10_
  84.5 0.6 collective-permute-done.14.refs_6_
  85.1 1.9 %collective-permute-start.17 = (bf16[1632,256]{1,0:T(8,128)(2,1)}, bf16[1632,256]{1,0:T(8,128)(2,1)}, u32[]{:S(2)}, u32[]{:S(2)}) collective-permute-start(bf16[1632,256]{1,0:T(8,128)(2,1)} %collective-permute-done.14.refs_6_), channel_id=1, source_target_pairs={{0,24},{8,0},{16,8},{24,16},{1,25},{9,1},{17,9},{25,17},{2,26},{10... | collective-permute-start | bytes 2506760 | tf_op jit(solution)/shard_map/ppermute | solution.py:375
  87.3 3.0 %collective-permute-start.19 = (bf16[1536,256]{1,0:T(8,128)(2,1)}, bf16[1536,256]{1,0:T(8,128)(2,1)}, u32[]{:S(2)}, u32[]{:S(2)}) collective-permute-start(bf16[1536,256]{1,0:T(8,128)(2,1)} %collective-permute-done.15.refs_10_), channel_id=1, source_target_pairs={{0,96},{32,0},{64,32},{96,64},{1,97},{33,1},{65,33},{97,65},{2,98}... | collective-permute-start | bytes 2359304 | tf_op jit(solution)/shard_map/ppermute | solution.py:375
  90.3 17.0 %pair.2.refs_12_ = bf16[32,1280,128]{2,1,0:T(8,128)(2,1)} custom-call(bf16[4,256,128]{2,1,0:T(8,128)(2,1)} %bitcast.14, bf16[128,1024]{1,0:T(8,128)(2,1)} %get-tuple-element.40.w_ref, bf16[32,128]{1,0:T(8,128)(2,1)} %get-tuple-element.41.mine_ref, bf16[1104,256]{1,0:T(8,128)(2,1)} %get-tuple-element.27.refs_0_.refs_4_, ...), custom_call_target="tpu_custom_call" | custom-call | tf_op jit(solution)/shard_map/pair/pallas_call | solution.py:304
  107.3 24.4 %pair.3 = bf16[32,1280,128]{2,1,0:T(8,128)(2,1)} custom-call(bf16[4,256,128]{2,1,0:T(8,128)(2,1)} %bitcast.15, bf16[128,1024]{1,0:T(8,128)(2,1)} %get-tuple-element.40.w_ref, bf16[32,128]{1,0:T(8,128)(2,1)} %get-tuple-element.41.mine_ref, bf16[1104,256]{1,0:T(8,128)(2,1)} %get-tuple-element.27.refs_0_.refs_4_, ...), custom_call_target="tpu_custom_call", output_to_operand_aliasing={{}: (15, {})} | custom-call | tf_op jit(solution)/shard_map/pair/pallas_call | solution.py:304
  (43 shorter events, 1.2 us)
Async XLA Ops:
  23.5 25.6 %copy-start.1 = (bf16[8,16,1408]{2,1,0:T(8,128)(2,1)}, bf16[8,16,1408]{2,1,0:T(8,128)(2,1)S(1)}, u32[]{:S(2)}) copy-start(bf16[8,16,1408]{2,1,0:T(8,128)(2,1)S(1)} %slice.24.refs_0_.refs_9_) | copy-start | bytes 1081348
  23.5 11.1 %collective-permute-start = (bf16[8,16,1408]{2,1,0:T(8,128)(2,1)S(1)}, bf16[8,16,1408]{2,1,0:T(8,128)(2,1)S(1)}, u32[]{:S(2)}, u32[]{:S(2)}) collective-permute-start(bf16[8,16,1408]{2,1,0:T(8,128)(2,1)S(1)} %slice.24.refs_0_.refs_9_), channel_id=1, source_target_pairs={{0,32},{32,64},{64,96},{96,0},{1,33},{33,65},{65,97},{97,1},{2,34}... | collective-permute-start | bytes 1081352 | tf_op jit(solution)/shard_map/ppermute | solution.py:328
  25.1 24.0 %copy-start = (bf16[8,16,1536]{2,1,0:T(8,128)(2,1)}, bf16[8,16,1536]{2,1,0:T(8,128)(2,1)S(1)}, u32[]{:S(2)}) copy-start(bf16[8,16,1536]{2,1,0:T(8,128)(2,1)S(1)} %pad_maximum_fusion.refs_4_.refs_13_.refs_18_) | copy-start | bytes 1179652
  25.1 11.8 %collective-permute-start.4 = (bf16[8,16,1536]{2,1,0:T(8,128)(2,1)S(1)}, bf16[8,16,1536]{2,1,0:T(8,128)(2,1)S(1)}, u32[]{:S(2)}, u32[]{:S(2)}) collective-permute-start(bf16[8,16,1536]{2,1,0:T(8,128)(2,1)S(1)} %pad_maximum_fusion.refs_4_.refs_13_.refs_18_), channel_id=1, source_target_pairs={{0,24},{8,0},{16,8},{24,16},{1,25},{9,1},{17,9},{25,17},{2,26},{10... | collective-permute-start | bytes 1179656 | tf_op jit(solution)/shard_map/ppermute | solution.py:328
  29.2 11.5 %collective-permute-start.3 = (bf16[8,16,1536]{2,1,0:T(8,128)(2,1)S(1)}, bf16[8,16,1536]{2,1,0:T(8,128)(2,1)S(1)}, u32[]{:S(2)}, u32[]{:S(2)}) collective-permute-start(bf16[8,16,1536]{2,1,0:T(8,128)(2,1)S(1)} %pad_maximum_fusion.refs_4_.refs_13_.refs_18_), channel_id=1, source_target_pairs={{0,8},{8,16},{16,24},{24,0},{1,9},{9,17},{17,25},{25,1},{2,10},{10... | collective-permute-start | bytes 1179656 | tf_op jit(solution)/shard_map/ppermute | solution.py:328
  29.2 12.9 %collective-permute-start.1 = (bf16[8,16,1408]{2,1,0:T(8,128)(2,1)S(1)}, bf16[8,16,1408]{2,1,0:T(8,128)(2,1)S(1)}, u32[]{:S(2)}, u32[]{:S(2)}) collective-permute-start(bf16[8,16,1408]{2,1,0:T(8,128)(2,1)S(1)} %slice.24.refs_0_.refs_9_), channel_id=1, source_target_pairs={{0,96},{32,0},{64,32},{96,64},{1,97},{33,1},{65,33},{97,65},{2,98}... | collective-permute-start | bytes 1081352 | tf_op jit(solution)/shard_map/ppermute | solution.py:328
  34.5 7.6 %copy-start.4 = (bf16[8,16,1408]{2,1,0:T(8,128)(2,1)}, bf16[8,16,1408]{2,1,0:T(8,128)(2,1)S(1)}, u32[]{:S(2)}) copy-start(bf16[8,16,1408]{2,1,0:T(8,128)(2,1)S(1)} %collective-permute-done.refs_1_.refs_10_) | copy-start | bytes 1081348
  34.5 14.6 %collective-permute-start.2 = (bf16[8,16,1408]{2,1,0:T(8,128)(2,1)S(1)}, bf16[8,16,1408]{2,1,0:T(8,128)(2,1)}, u32[]{:S(2)}, u32[]{:S(2)}) collective-permute-start(bf16[8,16,1408]{2,1,0:T(8,128)(2,1)S(1)} %collective-permute-done.refs_1_.refs_10_), channel_id=1, source_target_pairs={{0,32},{32,64},{64,96},{96,0},{1,33},{33,65},{65,97},{97,1},{2,34}... | collective-permute-start | bytes 1081352 | tf_op jit(solution)/shard_map/ppermute | solution.py:357
  37.0 3.8 %copy-start.2 = (bf16[8,16,1536]{2,1,0:T(8,128)(2,1)}, bf16[8,16,1536]{2,1,0:T(8,128)(2,1)S(1)}, u32[]{:S(2)}) copy-start(bf16[8,16,1536]{2,1,0:T(8,128)(2,1)S(1)} %collective-permute-done.4.refs_6_.refs_15_.refs_20_) | copy-start | bytes 1179652
  37.0 6.9 %collective-permute-start.6 = (bf16[4,16,1536]{2,1,0:T(8,128)(2,1)S(1)}, bf16[4,16,1536]{2,1,0:T(8,128)(2,1)S(1)}, u32[]{:S(2)}, u32[]{:S(2)}) collective-permute-start(bf16[4,16,1536]{2,1,0:T(8,128)(2,1)S(1)} %slice.29), channel_id=1, source_target_pairs={{0,24},{8,0},{16,8},{24,16},{1,25},{9,1},{17,9},{25,17},{2,26},{10... | collective-permute-start | bytes 589832 | tf_op jit(solution)/shard_map/ppermute | solution.py:334
  40.7 0.8 copy-start.3
  41.5 6.9 %collective-permute-start.5 = (bf16[4,16,1536]{2,1,0:T(8,128)(2,1)S(1)}, bf16[4,16,1536]{2,1,0:T(8,128)(2,1)S(1)}, u32[]{:S(2)}, u32[]{:S(2)}) collective-permute-start(bf16[4,16,1536]{2,1,0:T(8,128)(2,1)S(1)} %slice.28), channel_id=1, source_target_pairs={{0,8},{8,16},{16,24},{24,0},{1,9},{9,17},{17,25},{25,1},{2,10},{10... | collective-permute-start | bytes 589832 | tf_op jit(solution)/shard_map/ppermute | solution.py:334
  42.1 1.8 %copy-start.5 = (bf16[8,16,1408]{2,1,0:T(8,128)(2,1)}, bf16[8,16,1408]{2,1,0:T(8,128)(2,1)S(1)}, u32[]{:S(2)}) copy-start(bf16[8,16,1408]{2,1,0:T(8,128)(2,1)S(1)} %collective-permute-done.1.refs_2_.refs_11_) | copy-start | bytes 1081348
  43.9 5.2 %copy-start.7 = (bf16[4,16,1536]{2,1,0:T(8,128)(2,1)}, bf16[4,16,1536]{2,1,0:T(8,128)(2,1)S(1)}, u32[]{:S(2)}) copy-start(bf16[4,16,1536]{2,1,0:T(8,128)(2,1)S(1)} %collective-permute-done.6.refs_8_.refs_17_.refs_22_) | copy-start | bytes 589828
  48.4 0.7 copy-start.8
  52.6 16.3 %collective-permute-start.10 = (bf16[1152,256]{1,0:T(8,128)(2,1)}, bf16[1152,256]{1,0:T(8,128)(2,1)}, u32[]{:S(2)}, u32[]{:S(2)}) collective-permute-start(bf16[1152,256]{1,0:T(8,128)(2,1)} %get-tuple-element.28.refs_8_), channel_id=1, source_target_pairs={{0,96},{32,0},{64,32},{96,64},{1,97},{33,1},{65,33},{97,65},{2,98}... | collective-permute-start | bytes 1769480 | tf_op jit(solution)/shard_map/ppermute | solution.py:328
  54.5 14.7 %collective-permute-start.9 = (bf16[1152,256]{1,0:T(8,128)(2,1)}, bf16[1152,256]{1,0:T(8,128)(2,1)}, u32[]{:S(2)}, u32[]{:S(2)}) collective-permute-start(bf16[1152,256]{1,0:T(8,128)(2,1)} %get-tuple-element.28.refs_8_), channel_id=1, source_target_pairs={{0,32},{32,64},{64,96},{96,0},{1,33},{33,65},{65,97},{97,1},{2,34}... | collective-permute-start | bytes 1769480 | tf_op jit(solution)/shard_map/ppermute | solution.py:328
  54.7 14.2 %collective-permute-start.8 = (bf16[1104,256]{1,0:T(8,128)(2,1)}, bf16[1104,256]{1,0:T(8,128)(2,1)S(1)}, u32[]{:S(2)}, u32[]{:S(2)}) collective-permute-start(bf16[1104,256]{1,0:T(8,128)(2,1)} %get-tuple-element.27.refs_0_.refs_4_), channel_id=1, source_target_pairs={{0,24},{8,0},{16,8},{24,16},{1,25},{9,1},{17,9},{25,17},{2,26},{10... | collective-permute-start | bytes 1695752 | tf_op jit(solution)/shard_map/ppermute | solution.py:328
  54.7 14.2 %collective-permute-start.7 = (bf16[1104,256]{1,0:T(8,128)(2,1)}, bf16[1104,256]{1,0:T(8,128)(2,1)}, u32[]{:S(2)}, u32[]{:S(2)}) collective-permute-start(bf16[1104,256]{1,0:T(8,128)(2,1)} %get-tuple-element.27.refs_0_.refs_4_), channel_id=1, source_target_pairs={{0,8},{8,16},{16,24},{24,0},{1,9},{9,17},{17,25},{25,1},{2,10},{10... | collective-permute-start | bytes 1695752 | tf_op jit(solution)/shard_map/ppermute | solution.py:328
  56.8 12.2 %collective-permute-start.11 = (bf16[128,256]{1,0:T(8,128)(2,1)}, bf16[128,256]{1,0:T(8,128)(2,1)S(1)}, u32[]{:S(2)}, u32[]{:S(2)}) collective-permute-start(bf16[128,256]{1,0:T(8,128)(2,1)} %get-tuple-element.31.refs_0_), channel_id=1, source_target_pairs={{0,64},{32,96},{64,0},{96,32},{1,65},{33,97},{65,1},{97,33},{2,66}... | collective-permute-start | bytes 196616 | tf_op jit(solution)/shard_map/ppermute | solution.py:364
  69.0 4.3 %copy-start.9 = (bf16[128,256]{1,0:T(8,128)(2,1)}, bf16[128,256]{1,0:T(8,128)(2,1)S(1)}, u32[]{:S(2)}) copy-start(bf16[128,256]{1,0:T(8,128)(2,1)S(1)} %collective-permute-done.11.refs_3_) | copy-start | bytes 196612
  69.0 21.3 %copy-start.6 = (bf16[1104,256]{1,0:T(8,128)(2,1)}, bf16[1104,256]{1,0:T(8,128)(2,1)S(1)}, u32[]{:S(2)}) copy-start(bf16[1104,256]{1,0:T(8,128)(2,1)S(1)} %collective-permute-done.8.refs_2_.refs_6_) | copy-start | bytes 1695748
  69.2 15.9 %collective-permute-start.14 = (bf16[1632,256]{1,0:T(8,128)(2,1)}, bf16[1632,256]{1,0:T(8,128)(2,1)}, u32[]{:S(2)}, u32[]{:S(2)}) collective-permute-start(bf16[1632,256]{1,0:T(8,128)(2,1)} %get-tuple-element.44.refs_4_), channel_id=1, source_target_pairs={{0,24},{8,0},{16,8},{24,16},{1,25},{9,1},{17,9},{25,17},{2,26},{10... | collective-permute-start | bytes 2506760 | tf_op jit(solution)/shard_map/ppermute | solution.py:368
  69.3 15.2 %collective-permute-start.15 = (bf16[1536,256]{1,0:T(8,128)(2,1)}, bf16[1536,256]{1,0:T(8,128)(2,1)}, u32[]{:S(2)}, u32[]{:S(2)}) collective-permute-start(bf16[1536,256]{1,0:T(8,128)(2,1)} %get-tuple-element.46.refs_8_), channel_id=1, source_target_pairs={{0,96},{32,0},{64,32},{96,64},{1,97},{33,1},{65,33},{97,65},{2,98}... | collective-permute-start | bytes 2359304 | tf_op jit(solution)/shard_map/ppermute | solution.py:368
  70.6 11.9 %collective-permute-start.13 = (bf16[1152,256]{1,0:T(8,128)(2,1)}, bf16[1152,256]{1,0:T(8,128)(2,1)}, u32[]{:S(2)}, u32[]{:S(2)}) collective-permute-start(bf16[1152,256]{1,0:T(8,128)(2,1)} %collective-permute-done.9.refs_1_.refs_9_), channel_id=1, source_target_pairs={{0,32},{32,64},{64,96},{96,0},{1,33},{33,65},{65,97},{97,1},{2,34}... | collective-permute-start | bytes 1769480 | tf_op jit(solution)/shard_map/ppermute | solution.py:367
  71.3 11.1 %collective-permute-start.12 = (bf16[1104,256]{1,0:T(8,128)(2,1)}, bf16[1104,256]{1,0:T(8,128)(2,1)}, u32[]{:S(2)}, u32[]{:S(2)}) collective-permute-start(bf16[1104,256]{1,0:T(8,128)(2,1)} %collective-permute-done.7.refs_1_.refs_5_), channel_id=1, source_target_pairs={{0,8},{8,16},{16,24},{24,0},{1,9},{9,17},{17,25},{25,1},{2,10},{10... | collective-permute-start | bytes 1695752 | tf_op jit(solution)/shard_map/ppermute | solution.py:367
  82.5 24.8 %collective-permute-start.16 = (bf16[1632,256]{1,0:T(8,128)(2,1)}, bf16[1632,256]{1,0:T(8,128)(2,1)}, u32[]{:S(2)}, u32[]{:S(2)}) collective-permute-start(bf16[1632,256]{1,0:T(8,128)(2,1)} %get-tuple-element.44.refs_4_), channel_id=1, source_target_pairs={{0,8},{8,16},{16,24},{24,0},{1,9},{9,17},{17,25},{25,1},{2,10},{10... | collective-permute-start | bytes 2506760 | tf_op jit(solution)/shard_map/ppermute | solution.py:373
  85.1 22.2 %collective-permute-start.17 = (bf16[1632,256]{1,0:T(8,128)(2,1)}, bf16[1632,256]{1,0:T(8,128)(2,1)}, u32[]{:S(2)}, u32[]{:S(2)}) collective-permute-start(bf16[1632,256]{1,0:T(8,128)(2,1)} %collective-permute-done.14.refs_6_), channel_id=1, source_target_pairs={{0,24},{8,0},{16,8},{24,16},{1,25},{9,1},{17,9},{25,17},{2,26},{10... | collective-permute-start | bytes 2506760 | tf_op jit(solution)/shard_map/ppermute | solution.py:375
  87.0 20.2 %collective-permute-start.18 = (bf16[1536,256]{1,0:T(8,128)(2,1)}, bf16[1536,256]{1,0:T(8,128)(2,1)}, u32[]{:S(2)}, u32[]{:S(2)}) collective-permute-start(bf16[1536,256]{1,0:T(8,128)(2,1)} %get-tuple-element.46.refs_8_), channel_id=1, source_target_pairs={{0,32},{32,64},{64,96},{96,0},{1,33},{33,65},{65,97},{97,1},{2,34}... | collective-permute-start | bytes 2359304 | tf_op jit(solution)/shard_map/ppermute | solution.py:373
  87.3 20.0 %collective-permute-start.19 = (bf16[1536,256]{1,0:T(8,128)(2,1)}, bf16[1536,256]{1,0:T(8,128)(2,1)}, u32[]{:S(2)}, u32[]{:S(2)}) collective-permute-start(bf16[1536,256]{1,0:T(8,128)(2,1)} %collective-permute-done.15.refs_10_), channel_id=1, source_target_pairs={{0,96},{32,0},{64,32},{96,64},{1,97},{33,1},{65,33},{97,65},{2,98}... | collective-permute-start | bytes 2359304 | tf_op jit(solution)/shard_map/ppermute | solution.py:375

commit v7 on v6

--- a/solution.py
+++ b/solution.py
@@ -212,7 +212,7 @@
             scratch_shapes=[pltpu.VMEM((512, TILE), bf16)],
         ),
         out_shape=tuple(jax.ShapeDtypeStruct(shape, bf16) for shape in shapes),
-        compiler_params=vmem(),
+        compiler_params=vmem(24),
         name="interleave",
     )(position, *args)
 
@@ -253,7 +253,7 @@
             out_specs=whole(256, 128),
         ),
         out_shape=jax.ShapeDtypeStruct((256, 128), bf16),
-        compiler_params=vmem(),
+        compiler_params=vmem(24),
         name="arrange_left",
     )(position, own, before, after, far)
 

time: 132 us -> 131 us (level)
  Pallas kernels: 57.2 us -> 51.6 us
  local copies, waits for them, and re-layouts: 1.57 us -> 4.82 us
  waiting for transfers between devices: 19.1 us -> 21.5 us
    pallas_call x2, Pallas kernels: 7.53 us -> 3.66 us  [interleave(): pl.pallas_call(kernel, grid_spec=pltpu.PrefetchScalarGridSpec(num_scalar_...]
    unnamed x20 -> x26, local copies, waits for them, and re-layouts: 1.48 us -> 4.05 us
    pallas_call x1, Pallas kernels: 2.71 us -> 1.01 us  [arrange_left(): pl.pallas_call(kernel, grid_spec=pltpu.PrefetchScalarGridSpec(num_scalar_...]
  transfers between devices with their start and end apart: 20 -> 20, of which waited for: 9 -> 8; matrix products, arithmetic and copies ran while one was open for 1% -> 1% of each run, Pallas kernels for 18% -> 16%
where the time goes in v7:
time: 131 us; the launch traced here: 130 us
  Pallas kernels  51.6 us (39%)
  starting transfers between devices  28.2 us (22%)
  blocking collectives  24 us (18%)
  waiting for transfers between devices  21.5 us (16%)
  local copies, waits for them, and re-layouts  4.82 us (4%)
    pallas_call x2, Pallas kernels, pair(): pl.pallas_call(kernel, grid=(chunks,), out_shape=jax.ShapeDtypeStruct((RD...  41.3 us
    all_to_all x1, blocking collectives, on_device(): lax.all_to_all(right.reshape(8, width, -1), COLUMN, 0, 0, tiled=True)  17.8 us
    ppermute x4, starting transfers between devices, send_both(): lax.ppermute(block, axis, ring(-1))  7.6 us
    ppermute x1, waiting for transfers between devices, on_device(): left_far = lax.ppermute(left, 'x', ring(2))  6.44 us
    all_gather x1, blocking collectives, on_device(): left = lax.all_gather(left, narrow, axis=0)  6.22 us
    ppermute x4, starting transfers between devices, on_device(): lax.ppermute(block, axis, ring(-1))  5.68 us
    pallas_call x1, Pallas kernels, project(): pl.pallas_call(kernel, grid=(4,), out_shape=jax.ShapeDtypeStruct((2, 4, w...  5.61 us
    ppermute x1, waiting for transfers between devices, send_on(): lax.ppermute(low, axis, ring(1))  4.6 us
  transfers between devices with their start and end apart: 20, of which 8 were waited for; matrix products, arithmetic and copies ran while one was open for 1% of the time, Pallas kernels for 16%

profile of v7, /device:TPU:0, one launch (start us, length us, event | category | flops | bytes accessed | tf_op | source)
XLA Modules:
  0.0 130.4 jit_solution(9706651412507605993)
XLA Ops:
  0.0 5.6 %project.1 = bf16[2,4,32,1536]{3,2,1,0:T(8,128)(2,1)} custom-call(bf16[5120,256]{1,0:T(8,128)(2,1)} %bitcast.13, f32[4,1,1280]{2,1,0:T(1,128)} %bitcast.16, f32[1,256]{1,0:T(1,128)} %bitcast.19, f32[1,256]{1,0:T(1,128)} %bitcast.20, bf16[32,256]{1,0:T(8,128)(2,1)} %bitcast.17, f32[1,32]{1,0:T(1,128)} %bitcast.21, bf16[32,256]{1,0:T(8,128)(2,1)} %bitcast.18, ...), custom_call_target="tpu_custom_call" | custom-call | tf_op jit(solution)/shard_map/project/pallas_call | solution.py:99
  5.6 17.8 %all_to_all.5 = bf16[8,32,1536]{2,1,0:T(8,128)(2,1)S(1)} all-to-all(bf16[8,32,1536]{2,1,0:T(8,128)(2,1)} %bitcast.12), channel_id=1, replica_groups=mesh['x'=4,'z'=4,'yh'=2,'yl'=2,'core'=2] {'yh','yl','core'}, dimensions={0} | all-to-all | bytes 1572864 | tf_op jit(solution)/shard_map/all_to_all | solution.py:348
  23.5 1.6 %collective-permute-start = (bf16[8,16,1408]{2,1,0:T(8,128)(2,1)S(1)}, bf16[8,16,1408]{2,1,0:T(8,128)(2,1)S(1)}, u32[]{:S(2)}, u32[]{:S(2)}) collective-permute-start(bf16[8,16,1408]{2,1,0:T(8,128)(2,1)S(1)} %slice.24.refs_0_.refs_9_), channel_id=1, source_target_pairs={{0,32},{32,64},{64,96},{96,0},{1,33},{33,65},{65,97},{97,1},{2,34}... | collective-permute-start | bytes 1081352 | tf_op jit(solution)/shard_map/ppermute | solution.py:328
  25.1 4.1 %collective-permute-start.4 = (bf16[8,16,1536]{2,1,0:T(8,128)(2,1)S(1)}, bf16[8,16,1536]{2,1,0:T(8,128)(2,1)S(1)}, u32[]{:S(2)}, u32[]{:S(2)}) collective-permute-start(bf16[8,16,1536]{2,1,0:T(8,128)(2,1)S(1)} %pad_maximum_fusion.refs_4_.refs_13_.refs_18_), channel_id=1, source_target_pairs={{0,24},{8,0},{16,8},{24,16},{1,25},{9,1},{17,9},{25,17},{2,26},{10... | collective-permute-start | bytes 1179656 | tf_op jit(solution)/shard_map/ppermute | solution.py:328
  29.2 1.7 %collective-permute-start.1 = (bf16[8,16,1408]{2,1,0:T(8,128)(2,1)S(1)}, bf16[8,16,1408]{2,1,0:T(8,128)(2,1)S(1)}, u32[]{:S(2)}, u32[]{:S(2)}) collective-permute-start(bf16[8,16,1408]{2,1,0:T(8,128)(2,1)S(1)} %slice.24.refs_0_.refs_9_), channel_id=1, source_target_pairs={{0,96},{32,0},{64,32},{96,64},{1,97},{33,1},{65,33},{97,65},{2,98}... | collective-permute-start | bytes 1081352 | tf_op jit(solution)/shard_map/ppermute | solution.py:328
  31.0 3.6 %collective-permute-done.refs_1_.refs_10_ = bf16[8,16,1408]{2,1,0:T(8,128)(2,1)S(1)} collective-permute-done((bf16[8,16,1408]{2,1,0:T(8,128)(2,1)S(1)}, bf16[8,16,1408]{2,1,0:T(8,128)(2,1)S(1)}, u32[]{:S(2)}, u32[]{:S(2)}) %collective-permute-start) | collective-permute-done | bytes 360480 | tf_op jit(solution)/shard_map/ppermute | solution.py:328
  34.8 2.1 %collective-permute-done.4.refs_6_.refs_15_.refs_20_ = bf16[8,16,1536]{2,1,0:T(8,128)(2,1)S(1)} collective-permute-done((bf16[8,16,1536]{2,1,0:T(8,128)(2,1)S(1)}, bf16[8,16,1536]{2,1,0:T(8,128)(2,1)S(1)}, u32[]{:S(2)}, u32[]{:S(2)}) %collective-permute-start.4) | collective-permute-done | bytes 393248 | tf_op jit(solution)/shard_map/ppermute | solution.py:328
  37.0 3.8 %collective-permute-start.6 = (bf16[4,16,1536]{2,1,0:T(8,128)(2,1)S(1)}, bf16[4,16,1536]{2,1,0:T(8,128)(2,1)S(1)}, u32[]{:S(2)}, u32[]{:S(2)}) collective-permute-start(bf16[4,16,1536]{2,1,0:T(8,128)(2,1)S(1)} %slice.29), channel_id=1, source_target_pairs={{0,24},{8,0},{16,8},{24,16},{1,25},{9,1},{17,9},{25,17},{2,26},{10... | collective-permute-start | bytes 589832 | tf_op jit(solution)/shard_map/ppermute | solution.py:334
  40.7 0.7 slice.28
  41.5 2.4 %collective-permute-done.6.refs_8_.refs_17_.refs_22_ = bf16[4,16,1536]{2,1,0:T(8,128)(2,1)S(1)} collective-permute-done((bf16[4,16,1536]{2,1,0:T(8,128)(2,1)S(1)}, bf16[4,16,1536]{2,1,0:T(8,128)(2,1)S(1)}, u32[]{:S(2)}, u32[]{:S(2)}) %collective-permute-start.6) | collective-permute-done | bytes 196640 | tf_op jit(solution)/shard_map/ppermute | solution.py:334
  43.9 4.6 %collective-permute-done.5.refs_7_.refs_16_.refs_21_ = bf16[4,16,1536]{2,1,0:T(8,128)(2,1)S(1)} collective-permute-done((bf16[4,16,1536]{2,1,0:T(8,128)(2,1)}, bf16[4,16,1536]{2,1,0:T(8,128)(2,1)S(1)}, u32[]{:S(2)}, u32[]{:S(2)}) %collective-permute-start.5) | collective-permute-done | bytes 196640 | tf_op jit(solution)/shard_map/ppermute | solution.py:334
  49.2 0.9 copy-done.2
  50.1 1.4 %interleave.2 = (bf16[1104,256]{1,0:T(8,128)(2,1)S(1)}, bf16[1152,256]{1,0:T(8,128)(2,1)S(1)}, bf16[128,256]{1,0:T(8,128)(2,1)S(1)}, bf16[32,128]{1,0:T(8,128)(2,1)S(1)}) custom-call(s32[2]{0:T(128)S(1)} %pad_add_fusion.pos, bf16[8,16,1408]{2,1,0:T(8,128)(2,1)S(1)} %slice.24.refs_0_.refs_9_, bf16[8,16,1408]{2,1,0:T(8,128)(2,1)S(1)} %collective-permute-done.refs_1_.refs_10_, ...), custom_call_target="tpu_custom_call" | custom-call | tf_op jit(solution)/shard_map/interleave/pallas_call | solution.py:205
  52.1 1.7 %collective-permute-start.10 = (bf16[1152,256]{1,0:T(8,128)(2,1)S(1)}, bf16[1152,256]{1,0:T(8,128)(2,1)S(1)}, u32[]{:S(2)}, u32[]{:S(2)}) collective-permute-start(bf16[1152,256]{1,0:T(8,128)(2,1)S(1)} %get-tuple-element.28.refs_8_), channel_id=1, source_target_pairs={{0,96},{32,0},{64,32},{96,64},{1,97},{33,1},{65,33},{97,65},{2,98}... | collective-permute-start | bytes 1769480 | tf_op jit(solution)/shard_map/ppermute | solution.py:328
  54.1 2.0 %collective-permute-start.7 = (bf16[1104,256]{1,0:T(8,128)(2,1)S(1)}, bf16[1104,256]{1,0:T(8,128)(2,1)S(1)}, u32[]{:S(2)}, u32[]{:S(2)}) collective-permute-start(bf16[1104,256]{1,0:T(8,128)(2,1)S(1)} %get-tuple-element.27.refs_0_.refs_4_), channel_id=1, source_target_pairs={{0,8},{8,16},{16,24},{24,0},{1,9},{9,17},{17,25},{25,1},{2,10},{10... | collective-permute-start | bytes 1695752 | tf_op jit(solution)/shard_map/ppermute | solution.py:328
  56.2 2.7 %collective-permute-start.11 = (bf16[128,256]{1,0:T(8,128)(2,1)S(1)}, bf16[128,256]{1,0:T(8,128)(2,1)S(1)}, u32[]{:S(2)}, u32[]{:S(2)}) collective-permute-start(bf16[128,256]{1,0:T(8,128)(2,1)S(1)} %get-tuple-element.31.refs_0_), channel_id=1, source_target_pairs={{0,64},{32,96},{64,0},{96,32},{1,65},{33,97},{65,1},{97,33},{2,66}... | collective-permute-start | bytes 196616 | tf_op jit(solution)/shard_map/ppermute | solution.py:364
  58.9 0.9 copy-done.7
  59.8 2.3 %interleave.3 = (bf16[1632,256]{1,0:T(8,128)(2,1)}, bf16[1536,256]{1,0:T(8,128)(2,1)}, bf16[128,1024]{1,0:T(8,128)(2,1)S(1)}) custom-call(s32[2]{0:T(128)S(1)} %pad_add_fusion.pos, bf16[8,16,1408]{2,1,0:T(8,128)(2,1)S(1)} %slice.24.refs_0_.refs_9_, bf16[8,16,1408]{2,1,0:T(8,128)(2,1)S(1)} %collective-permute-done.refs_1_.refs_10_, ...), custom_call_target="tpu_custom_call" | custom-call | tf_op jit(solution)/shard_map/interleave/pallas_call | solution.py:205
  62.1 6.4 %collective-permute-done.11.refs_3_ = bf16[128,256]{1,0:T(8,128)(2,1)S(1)} collective-permute-done((bf16[128,256]{1,0:T(8,128)(2,1)S(1)}, bf16[128,256]{1,0:T(8,128)(2,1)S(1)}, u32[]{:S(2)}, u32[]{:S(2)}) %collective-permute-start.11) | collective-permute-done | bytes 65568 | tf_op jit(solution)/shard_map/ppermute | solution.py:364
  68.7 1.2 collective-permute-start.15
  69.9 0.9 collective-permute-start.13
  70.8 1.9 %collective-permute-start.12 = (bf16[1104,256]{1,0:T(8,128)(2,1)S(1)}, bf16[1104,256]{1,0:T(8,128)(2,1)S(1)}, u32[]{:S(2)}, u32[]{:S(2)}) collective-permute-start(bf16[1104,256]{1,0:T(8,128)(2,1)S(1)} %collective-permute-done.7.refs_1_.refs_5_), channel_id=1, source_target_pairs={{0,8},{8,16},{16,24},{24,0},{1,9},{9,17},{17,25},{25,1},{2,10},{10... | collective-permute-start | bytes 1695752 | tf_op jit(solution)/shard_map/ppermute | solution.py:367
  72.7 1.0 arrange_left.1
  73.8 0.9 copy-done.3
  74.6 6.2 %all-gather = bf16[1024,128]{1,0:T(8,128)(2,1)} all-gather(bf16[256,128]{1,0:T(8,128)(2,1)S(1)} %arrange_left.1), channel_id=2, replica_groups=mesh['x'=4,'z'=4,'yh'=2,'yl'=2,'core'=2] {'yl','core'}, dimensions={0}, use_global_device_ids=true | all-gather | bytes 327680 | tf_op jit(solution)/shard_map/all_gather | solution.py:370
  80.8 0.8 collective-permute-done.12.refs_3_.refs_7_
  81.6 1.1 collective-permute-start.16
  83.4 1.0 collective-permute-done.14.refs_6_
  84.3 1.5 %collective-permute-start.17 = (bf16[1632,256]{1,0:T(8,128)(2,1)}, bf16[1632,256]{1,0:T(8,128)(2,1)}, u32[]{:S(2)}, u32[]{:S(2)}) collective-permute-start(bf16[1632,256]{1,0:T(8,128)(2,1)} %collective-permute-done.14.refs_6_), channel_id=1, source_target_pairs={{0,24},{8,0},{16,8},{24,16},{1,25},{9,1},{17,9},{25,17},{2,26},{10... | collective-permute-start | bytes 2506760 | tf_op jit(solution)/shard_map/ppermute | solution.py:375
  86.1 2.9 %collective-permute-start.19 = (bf16[1536,256]{1,0:T(8,128)(2,1)}, bf16[1536,256]{1,0:T(8,128)(2,1)}, u32[]{:S(2)}, u32[]{:S(2)}) collective-permute-start(bf16[1536,256]{1,0:T(8,128)(2,1)} %collective-permute-done.15.refs_10_), channel_id=1, source_target_pairs={{0,96},{32,0},{64,32},{96,64},{1,97},{33,1},{65,33},{97,65},{2,98}... | collective-permute-start | bytes 2359304 | tf_op jit(solution)/shard_map/ppermute | solution.py:375
  89.1 17.0 %pair.2.refs_12_ = bf16[32,1280,128]{2,1,0:T(8,128)(2,1)} custom-call(bf16[4,256,128]{2,1,0:T(8,128)(2,1)} %bitcast.14, bf16[128,1024]{1,0:T(8,128)(2,1)} %copy-done.5, bf16[32,128]{1,0:T(8,128)(2,1)} %copy-done.8, bf16[1104,256]{1,0:T(8,128)(2,1)} %copy-done, bf16[1104,256]{1,0:T(8,128)(2,1)} %copy-done.10, bf16[1104,256]{1,0:T(8,128)(2,1)} %copy-done.9, ...), custom_call_target="tpu_custom_call" | custom-call | tf_op jit(solution)/shard_map/pair/pallas_call | solution.py:304
  106.1 24.4 %pair.3 = bf16[32,1280,128]{2,1,0:T(8,128)(2,1)} custom-call(bf16[4,256,128]{2,1,0:T(8,128)(2,1)} %bitcast.15, bf16[128,1024]{1,0:T(8,128)(2,1)} %copy-done.5, bf16[32,128]{1,0:T(8,128)(2,1)} %copy-done.8, bf16[1104,256]{1,0:T(8,128)(2,1)} %copy-done, bf16[1104,256]{1,0:T(8,128)(2,1)} %copy-done.10, ...), custom_call_target="tpu_custom_call", output_to_operand_aliasing={{}: (15, {})} | custom-call | tf_op jit(solution)/shard_map/pair/pallas_call | solution.py:304
  (49 shorter events, 3.1 us)
Async XLA Ops:
  23.5 11.1 %collective-permute-start = (bf16[8,16,1408]{2,1,0:T(8,128)(2,1)S(1)}, bf16[8,16,1408]{2,1,0:T(8,128)(2,1)S(1)}, u32[]{:S(2)}, u32[]{:S(2)}) collective-permute-start(bf16[8,16,1408]{2,1,0:T(8,128)(2,1)S(1)} %slice.24.refs_0_.refs_9_), channel_id=1, source_target_pairs={{0,32},{32,64},{64,96},{96,0},{1,33},{33,65},{65,97},{97,1},{2,34}... | collective-permute-start | bytes 1081352 | tf_op jit(solution)/shard_map/ppermute | solution.py:328
  25.1 11.8 %collective-permute-start.4 = (bf16[8,16,1536]{2,1,0:T(8,128)(2,1)S(1)}, bf16[8,16,1536]{2,1,0:T(8,128)(2,1)S(1)}, u32[]{:S(2)}, u32[]{:S(2)}) collective-permute-start(bf16[8,16,1536]{2,1,0:T(8,128)(2,1)S(1)} %pad_maximum_fusion.refs_4_.refs_13_.refs_18_), channel_id=1, source_target_pairs={{0,24},{8,0},{16,8},{24,16},{1,25},{9,1},{17,9},{25,17},{2,26},{10... | collective-permute-start | bytes 1179656 | tf_op jit(solution)/shard_map/ppermute | solution.py:328
  29.2 11.5 %collective-permute-start.3 = (bf16[8,16,1536]{2,1,0:T(8,128)(2,1)S(1)}, bf16[8,16,1536]{2,1,0:T(8,128)(2,1)S(1)}, u32[]{:S(2)}, u32[]{:S(2)}) collective-permute-start(bf16[8,16,1536]{2,1,0:T(8,128)(2,1)S(1)} %pad_maximum_fusion.refs_4_.refs_13_.refs_18_), channel_id=1, source_target_pairs={{0,8},{8,16},{16,24},{24,0},{1,9},{9,17},{17,25},{25,1},{2,10},{10... | collective-permute-start | bytes 1179656 | tf_op jit(solution)/shard_map/ppermute | solution.py:328
  29.2 12.3 %collective-permute-start.1 = (bf16[8,16,1408]{2,1,0:T(8,128)(2,1)S(1)}, bf16[8,16,1408]{2,1,0:T(8,128)(2,1)S(1)}, u32[]{:S(2)}, u32[]{:S(2)}) collective-permute-start(bf16[8,16,1408]{2,1,0:T(8,128)(2,1)S(1)} %slice.24.refs_0_.refs_9_), channel_id=1, source_target_pairs={{0,96},{32,0},{64,32},{96,64},{1,97},{33,1},{65,33},{97,65},{2,98}... | collective-permute-start | bytes 1081352 | tf_op jit(solution)/shard_map/ppermute | solution.py:328
  34.5 14.7 %collective-permute-start.2 = (bf16[8,16,1408]{2,1,0:T(8,128)(2,1)S(1)}, bf16[8,16,1408]{2,1,0:T(8,128)(2,1)S(1)}, u32[]{:S(2)}, u32[]{:S(2)}) collective-permute-start(bf16[8,16,1408]{2,1,0:T(8,128)(2,1)S(1)} %collective-permute-done.refs_1_.refs_10_), channel_id=1, source_target_pairs={{0,32},{32,64},{64,96},{96,0},{1,33},{33,65},{65,97},{97,1},{2,34}... | collective-permute-start | bytes 1081352 | tf_op jit(solution)/shard_map/ppermute | solution.py:357
  37.0 6.9 %collective-permute-start.6 = (bf16[4,16,1536]{2,1,0:T(8,128)(2,1)S(1)}, bf16[4,16,1536]{2,1,0:T(8,128)(2,1)S(1)}, u32[]{:S(2)}, u32[]{:S(2)}) collective-permute-start(bf16[4,16,1536]{2,1,0:T(8,128)(2,1)S(1)} %slice.29), channel_id=1, source_target_pairs={{0,24},{8,0},{16,8},{24,16},{1,25},{9,1},{17,9},{25,17},{2,26},{10... | collective-permute-start | bytes 589832 | tf_op jit(solution)/shard_map/ppermute | solution.py:334
  41.4 7.1 %collective-permute-start.5 = (bf16[4,16,1536]{2,1,0:T(8,128)(2,1)}, bf16[4,16,1536]{2,1,0:T(8,128)(2,1)S(1)}, u32[]{:S(2)}, u32[]{:S(2)}) collective-permute-start(bf16[4,16,1536]{2,1,0:T(8,128)(2,1)} %slice.28), channel_id=1, source_target_pairs={{0,8},{8,16},{16,24},{24,0},{1,9},{9,17},{17,25},{25,1},{2,10},{10... | collective-permute-start | bytes 589832 | tf_op jit(solution)/shard_map/ppermute | solution.py:334
  48.5 0.7 copy-start.1
  49.2 0.9 copy-start.2
  52.1 29.5 %copy-start.6 = (bf16[1152,256]{1,0:T(8,128)(2,1)}, bf16[1152,256]{1,0:T(8,128)(2,1)S(1)}, u32[]{:S(2)}) copy-start(bf16[1152,256]{1,0:T(8,128)(2,1)S(1)} %get-tuple-element.28.refs_8_) | copy-start | bytes 1769476
  52.1 37.0 %copy-start = (bf16[1104,256]{1,0:T(8,128)(2,1)}, bf16[1104,256]{1,0:T(8,128)(2,1)S(1)}, u32[]{:S(2)}) copy-start(bf16[1104,256]{1,0:T(8,128)(2,1)S(1)} %get-tuple-element.27.refs_0_.refs_4_) | copy-start | bytes 1695748
  52.1 16.5 %collective-permute-start.10 = (bf16[1152,256]{1,0:T(8,128)(2,1)S(1)}, bf16[1152,256]{1,0:T(8,128)(2,1)S(1)}, u32[]{:S(2)}, u32[]{:S(2)}) collective-permute-start(bf16[1152,256]{1,0:T(8,128)(2,1)S(1)} %get-tuple-element.28.refs_8_), channel_id=1, source_target_pairs={{0,96},{32,0},{64,32},{96,64},{1,97},{33,1},{65,33},{97,65},{2,98}... | collective-permute-start | bytes 1769480 | tf_op jit(solution)/shard_map/ppermute | solution.py:328
  53.9 14.7 %collective-permute-start.9 = (bf16[1152,256]{1,0:T(8,128)(2,1)S(1)}, bf16[1152,256]{1,0:T(8,128)(2,1)S(1)}, u32[]{:S(2)}, u32[]{:S(2)}) collective-permute-start(bf16[1152,256]{1,0:T(8,128)(2,1)S(1)} %get-tuple-element.28.refs_8_), channel_id=1, source_target_pairs={{0,32},{32,64},{64,96},{96,0},{1,33},{33,65},{65,97},{97,1},{2,34}... | collective-permute-start | bytes 1769480 | tf_op jit(solution)/shard_map/ppermute | solution.py:328
  54.1 14.4 %collective-permute-start.8 = (bf16[1104,256]{1,0:T(8,128)(2,1)S(1)}, bf16[1104,256]{1,0:T(8,128)(2,1)S(1)}, u32[]{:S(2)}, u32[]{:S(2)}) collective-permute-start(bf16[1104,256]{1,0:T(8,128)(2,1)S(1)} %get-tuple-element.27.refs_0_.refs_4_), channel_id=1, source_target_pairs={{0,24},{8,0},{16,8},{24,16},{1,25},{9,1},{17,9},{25,17},{2,26},{10... | collective-permute-start | bytes 1695752 | tf_op jit(solution)/shard_map/ppermute | solution.py:328
  54.1 14.4 %collective-permute-start.7 = (bf16[1104,256]{1,0:T(8,128)(2,1)S(1)}, bf16[1104,256]{1,0:T(8,128)(2,1)S(1)}, u32[]{:S(2)}, u32[]{:S(2)}) collective-permute-start(bf16[1104,256]{1,0:T(8,128)(2,1)S(1)} %get-tuple-element.27.refs_0_.refs_4_), channel_id=1, source_target_pairs={{0,8},{8,16},{16,24},{24,0},{1,9},{9,17},{17,25},{25,1},{2,10},{10... | collective-permute-start | bytes 1695752 | tf_op jit(solution)/shard_map/ppermute | solution.py:328
  56.2 12.4 %collective-permute-start.11 = (bf16[128,256]{1,0:T(8,128)(2,1)S(1)}, bf16[128,256]{1,0:T(8,128)(2,1)S(1)}, u32[]{:S(2)}, u32[]{:S(2)}) collective-permute-start(bf16[128,256]{1,0:T(8,128)(2,1)S(1)} %get-tuple-element.31.refs_0_), channel_id=1, source_target_pairs={{0,64},{32,96},{64,0},{96,32},{1,65},{33,97},{65,1},{97,33},{2,66}... | collective-permute-start | bytes 196616 | tf_op jit(solution)/shard_map/ppermute | solution.py:364
  58.9 0.9 copy-start.7
  62.1 19.5 %copy-start.5 = (bf16[128,1024]{1,0:T(8,128)(2,1)}, bf16[128,1024]{1,0:T(8,128)(2,1)S(1)}, u32[]{:S(2)}) copy-start(bf16[128,1024]{1,0:T(8,128)(2,1)S(1)} %get-tuple-element.40.w_ref) | copy-start | bytes 786436
  68.5 14.2 %copy-start.9 = (bf16[1104,256]{1,0:T(8,128)(2,1)}, bf16[1104,256]{1,0:T(8,128)(2,1)S(1)}, u32[]{:S(2)}) copy-start(bf16[1104,256]{1,0:T(8,128)(2,1)S(1)} %collective-permute-done.8.refs_2_.refs_6_) | copy-start | bytes 1695748
  68.6 14.8 %copy-start.10 = (bf16[1104,256]{1,0:T(8,128)(2,1)}, bf16[1104,256]{1,0:T(8,128)(2,1)S(1)}, u32[]{:S(2)}) copy-start(bf16[1104,256]{1,0:T(8,128)(2,1)S(1)} %collective-permute-done.7.refs_1_.refs_5_) | copy-start | bytes 1695748
  68.6 5.1 %copy-start.4 = (bf16[1152,256]{1,0:T(8,128)(2,1)}, bf16[1152,256]{1,0:T(8,128)(2,1)S(1)}, u32[]{:S(2)}) copy-start(bf16[1152,256]{1,0:T(8,128)(2,1)S(1)} %collective-permute-done.9.refs_1_.refs_9_) | copy-start | bytes 1769476
  68.6 15.7 %collective-permute-start.14 = (bf16[1632,256]{1,0:T(8,128)(2,1)}, bf16[1632,256]{1,0:T(8,128)(2,1)}, u32[]{:S(2)}, u32[]{:S(2)}) collective-permute-start(bf16[1632,256]{1,0:T(8,128)(2,1)} %get-tuple-element.44.refs_4_), channel_id=1, source_target_pairs={{0,24},{8,0},{16,8},{24,16},{1,25},{9,1},{17,9},{25,17},{2,26},{10... | collective-permute-start | bytes 2506760 | tf_op jit(solution)/shard_map/ppermute | solution.py:368
  68.7 14.7 %collective-permute-start.15 = (bf16[1536,256]{1,0:T(8,128)(2,1)}, bf16[1536,256]{1,0:T(8,128)(2,1)}, u32[]{:S(2)}, u32[]{:S(2)}) collective-permute-start(bf16[1536,256]{1,0:T(8,128)(2,1)} %get-tuple-element.46.refs_8_), channel_id=1, source_target_pairs={{0,96},{32,0},{64,32},{96,64},{1,97},{33,1},{65,33},{97,65},{2,98}... | collective-permute-start | bytes 2359304 | tf_op jit(solution)/shard_map/ppermute | solution.py:368
  69.9 11.8 %collective-permute-start.13 = (bf16[1152,256]{1,0:T(8,128)(2,1)S(1)}, bf16[1152,256]{1,0:T(8,128)(2,1)S(1)}, u32[]{:S(2)}, u32[]{:S(2)}) collective-permute-start(bf16[1152,256]{1,0:T(8,128)(2,1)S(1)} %collective-permute-done.9.refs_1_.refs_9_), channel_id=1, source_target_pairs={{0,32},{32,64},{64,96},{96,0},{1,33},{33,65},{65,97},{97,1},{2,34}... | collective-permute-start | bytes 1769480 | tf_op jit(solution)/shard_map/ppermute | solution.py:367
  70.8 10.8 %collective-permute-start.12 = (bf16[1104,256]{1,0:T(8,128)(2,1)S(1)}, bf16[1104,256]{1,0:T(8,128)(2,1)S(1)}, u32[]{:S(2)}, u32[]{:S(2)}) collective-permute-start(bf16[1104,256]{1,0:T(8,128)(2,1)S(1)} %collective-permute-done.7.refs_1_.refs_5_), channel_id=1, source_target_pairs={{0,8},{8,16},{16,24},{24,0},{1,9},{9,17},{17,25},{25,1},{2,10},{10... | collective-permute-start | bytes 1695752 | tf_op jit(solution)/shard_map/ppermute | solution.py:367
  73.7 0.9 copy-start.3
  81.6 2.7 %copy-start.11 = (bf16[1104,256]{1,0:T(8,128)(2,1)}, bf16[1104,256]{1,0:T(8,128)(2,1)S(1)}, u32[]{:S(2)}) copy-start(bf16[1104,256]{1,0:T(8,128)(2,1)S(1)} %collective-permute-done.12.refs_3_.refs_7_) | copy-start | bytes 1695748
  81.6 4.2 %copy-start.12 = (bf16[1152,256]{1,0:T(8,128)(2,1)}, bf16[1152,256]{1,0:T(8,128)(2,1)S(1)}, u32[]{:S(2)}) copy-start(bf16[1152,256]{1,0:T(8,128)(2,1)S(1)} %collective-permute-done.13.refs_11_) | copy-start | bytes 1769476
  81.6 24.4 %collective-permute-start.16 = (bf16[1632,256]{1,0:T(8,128)(2,1)}, bf16[1632,256]{1,0:T(8,128)(2,1)}, u32[]{:S(2)}, u32[]{:S(2)}) collective-permute-start(bf16[1632,256]{1,0:T(8,128)(2,1)} %get-tuple-element.44.refs_4_), channel_id=1, source_target_pairs={{0,8},{8,16},{16,24},{24,0},{1,9},{9,17},{17,25},{25,1},{2,10},{10... | collective-permute-start | bytes 2506760 | tf_op jit(solution)/shard_map/ppermute | solution.py:373
  84.3 21.8 %collective-permute-start.17 = (bf16[1632,256]{1,0:T(8,128)(2,1)}, bf16[1632,256]{1,0:T(8,128)(2,1)}, u32[]{:S(2)}, u32[]{:S(2)}) collective-permute-start(bf16[1632,256]{1,0:T(8,128)(2,1)} %collective-permute-done.14.refs_6_), channel_id=1, source_target_pairs={{0,24},{8,0},{16,8},{24,16},{1,25},{9,1},{17,9},{25,17},{2,26},{10... | collective-permute-start | bytes 2506760 | tf_op jit(solution)/shard_map/ppermute | solution.py:375
  85.8 20.2 %collective-permute-start.18 = (bf16[1536,256]{1,0:T(8,128)(2,1)}, bf16[1536,256]{1,0:T(8,128)(2,1)}, u32[]{:S(2)}, u32[]{:S(2)}) collective-permute-start(bf16[1536,256]{1,0:T(8,128)(2,1)} %get-tuple-element.46.refs_8_), channel_id=1, source_target_pairs={{0,32},{32,64},{64,96},{96,0},{1,33},{33,65},{65,97},{97,1},{2,34}... | collective-permute-start | bytes 2359304 | tf_op jit(solution)/shard_map/ppermute | solution.py:373
  86.1 19.9 %collective-permute-start.19 = (bf16[1536,256]{1,0:T(8,128)(2,1)}, bf16[1536,256]{1,0:T(8,128)(2,1)}, u32[]{:S(2)}, u32[]{:S(2)}) collective-permute-start(bf16[1536,256]{1,0:T(8,128)(2,1)} %collective-permute-done.15.refs_10_), channel_id=1, source_target_pairs={{0,96},{32,0},{64,32},{96,64},{1,97},{33,1},{65,33},{97,65},{2,98}... | collective-permute-start | bytes 2359304 | tf_op jit(solution)/shard_map/ppermute | solution.py:375
  (1 other events, 0.6 us)

commit v8 on v7

--- a/solution.py
+++ b/solution.py
@@ -318,7 +318,7 @@
             pltpu.VMEM((RD, 128), bf16),
         ],
         input_output_aliases={15: 0} if earlier else {},
-        compiler_params=vmem(),
+        compiler_params=vmem(40),
         name="pair",
     )(left, weight, mine, *masks, *first, *second, *earlier)
 

time: 131 us -> 125 us (0.954)
  waiting for transfers between devices: 21.5 us -> 26.2 us
  Pallas kernels: 51.6 us -> 47 us
  local copies, waits for them, and re-layouts: 4.82 us -> 0.77 us
  starting transfers between devices: 28.2 us -> 26.6 us
    unnamed x26 -> x2, local copies, waits for them, and re-layouts: 4.05 us -> 0.01 us
    pallas_call x2, Pallas kernels: 41.3 us -> 37.6 us  [pair(): pl.pallas_call(kernel, grid=(chunks,), out_shape=jax.ShapeDtypeStruct((RD...]
    ppermute x4, starting transfers between devices: 5.68 us -> 3.85 us  [on_device(): lax.ppermute(block, axis, ring(-1))]
    ppermute x2, waiting for transfers between devices: 0.76 us -> 2.44 us  [on_device(): lax.ppermute(before, axis, ring(1))]
    ppermute x4, waiting for transfers between devices: 1.6 us -> 3.09 us  [on_device(): lax.ppermute(block, axis, ring(-1))]
    ppermute x1, waiting for transfers between devices: 6.44 us -> 7.83 us  [on_device(): left_far = lax.ppermute(left, 'x', ring(2))]
  transfers between devices with their start and end apart: 20 -> 20, of which waited for: 8 -> 10; matrix products, arithmetic and copies ran while one was open for 1% -> 1% of each run, Pallas kernels for 16% -> 14%
where the time goes in v8:
time: 125 us; the launch traced here: 124 us
  Pallas kernels  47 us (38%)
  starting transfers between devices  26.6 us (21%)
  waiting for transfers between devices  26.2 us (21%)
  blocking collectives  23.6 us (19%)
    pallas_call x2, Pallas kernels, pair(): pl.pallas_call(kernel, grid=(chunks,), out_shape=jax.ShapeDtypeStruct((RD...  37.6 us
    all_to_all x1, blocking collectives, on_device(): lax.all_to_all(right.reshape(8, width, -1), COLUMN, 0, 0, tiled=True)  17.8 us
    ppermute x1, waiting for transfers between devices, on_device(): left_far = lax.ppermute(left, 'x', ring(2))  7.83 us
    ppermute x4, starting transfers between devices, send_both(): lax.ppermute(block, axis, ring(-1))  7.8 us
    all_gather x1, blocking collectives, on_device(): left = lax.all_gather(left, narrow, axis=0)  5.79 us
    pallas_call x1, Pallas kernels, project(): pl.pallas_call(kernel, grid=(4,), out_shape=jax.ShapeDtypeStruct((2, 4, w...  5.65 us
    ppermute x1, waiting for transfers between devices, send_on(): lax.ppermute(low, axis, ring(1))  4.6 us
    ppermute x4, starting transfers between devices, on_device(): lax.ppermute(block, axis, ring(-1))  3.85 us
  transfers between devices with their start and end apart: 20, of which 10 were waited for; matrix products, arithmetic and copies ran while one was open for 1% of the time, Pallas kernels for 14%

profile of v8, /device:TPU:0, one launch (start us, length us, event | category | flops | bytes accessed | tf_op | source)
XLA Modules:
  0.0 124.4 jit_solution(16798527418342715605)
XLA Ops:
  0.0 5.7 %project.1 = bf16[2,4,32,1536]{3,2,1,0:T(8,128)(2,1)} custom-call(bf16[5120,256]{1,0:T(8,128)(2,1)} %bitcast.15, f32[4,1,1280]{2,1,0:T(1,128)} %bitcast.16, f32[1,256]{1,0:T(1,128)} %bitcast.19, f32[1,256]{1,0:T(1,128)} %bitcast.20, bf16[32,256]{1,0:T(8,128)(2,1)} %bitcast.17, f32[1,32]{1,0:T(1,128)} %bitcast.21, bf16[32,256]{1,0:T(8,128)(2,1)} %bitcast.18, ...), custom_call_target="tpu_custom_call" | custom-call | tf_op jit(solution)/shard_map/project/pallas_call | solution.py:99
  5.7 17.8 %all_to_all.5 = bf16[8,32,1536]{2,1,0:T(8,128)(2,1)S(1)} all-to-all(bf16[8,32,1536]{2,1,0:T(8,128)(2,1)} %bitcast.14), channel_id=1, replica_groups=mesh['x'=4,'z'=4,'yh'=2,'yl'=2,'core'=2] {'yh','yl','core'}, dimensions={0} | all-to-all | bytes 1572864 | tf_op jit(solution)/shard_map/all_to_all | solution.py:348
  23.5 1.6 %collective-permute-start = (bf16[8,16,1408]{2,1,0:T(8,128)(2,1)S(1)}, bf16[8,16,1408]{2,1,0:T(8,128)(2,1)S(1)}, u32[]{:S(2)}, u32[]{:S(2)}) collective-permute-start(bf16[8,16,1408]{2,1,0:T(8,128)(2,1)S(1)} %slice.24.refs_0_.refs_9_), channel_id=1, source_target_pairs={{0,32},{32,64},{64,96},{96,0},{1,33},{33,65},{65,97},{97,1},{2,34}... | collective-permute-start | bytes 1081352 | tf_op jit(solution)/shard_map/ppermute | solution.py:328
  25.1 4.1 %collective-permute-start.4 = (bf16[8,16,1536]{2,1,0:T(8,128)(2,1)S(1)}, bf16[8,16,1536]{2,1,0:T(8,128)(2,1)S(1)}, u32[]{:S(2)}, u32[]{:S(2)}) collective-permute-start(bf16[8,16,1536]{2,1,0:T(8,128)(2,1)S(1)} %pad_maximum_fusion.refs_4_.refs_13_.refs_18_), channel_id=1, source_target_pairs={{0,24},{8,0},{16,8},{24,16},{1,25},{9,1},{17,9},{25,17},{2,26},{10... | collective-permute-start | bytes 1179656 | tf_op jit(solution)/shard_map/ppermute | solution.py:328
  29.3 1.7 %collective-permute-start.1 = (bf16[8,16,1408]{2,1,0:T(8,128)(2,1)S(1)}, bf16[8,16,1408]{2,1,0:T(8,128)(2,1)S(1)}, u32[]{:S(2)}, u32[]{:S(2)}) collective-permute-start(bf16[8,16,1408]{2,1,0:T(8,128)(2,1)S(1)} %slice.24.refs_0_.refs_9_), channel_id=1, source_target_pairs={{0,96},{32,0},{64,32},{96,64},{1,97},{33,1},{65,33},{97,65},{2,98}... | collective-permute-start | bytes 1081352 | tf_op jit(solution)/shard_map/ppermute | solution.py:328
  31.0 3.6 %collective-permute-done.refs_1_.refs_10_ = bf16[8,16,1408]{2,1,0:T(8,128)(2,1)S(1)} collective-permute-done((bf16[8,16,1408]{2,1,0:T(8,128)(2,1)S(1)}, bf16[8,16,1408]{2,1,0:T(8,128)(2,1)S(1)}, u32[]{:S(2)}, u32[]{:S(2)}) %collective-permute-start) | collective-permute-done | bytes 360480 | tf_op jit(solution)/shard_map/ppermute | solution.py:328
  34.6 0.3 collective-permute-start.2
  34.8 2.1 %collective-permute-done.4.refs_6_.refs_15_.refs_20_ = bf16[8,16,1536]{2,1,0:T(8,128)(2,1)S(1)} collective-permute-done((bf16[8,16,1536]{2,1,0:T(8,128)(2,1)S(1)}, bf16[8,16,1536]{2,1,0:T(8,128)(2,1)S(1)}, u32[]{:S(2)}, u32[]{:S(2)}) %collective-permute-start.4) | collective-permute-done | bytes 393248 | tf_op jit(solution)/shard_map/ppermute | solution.py:328
  37.0 3.8 %collective-permute-start.6 = (bf16[4,16,1536]{2,1,0:T(8,128)(2,1)S(1)}, bf16[4,16,1536]{2,1,0:T(8,128)(2,1)S(1)}, u32[]{:S(2)}, u32[]{:S(2)}) collective-permute-start(bf16[4,16,1536]{2,1,0:T(8,128)(2,1)S(1)} %slice.29), channel_id=1, source_target_pairs={{0,24},{8,0},{16,8},{24,16},{1,25},{9,1},{17,9},{25,17},{2,26},{10... | collective-permute-start | bytes 589832 | tf_op jit(solution)/shard_map/ppermute | solution.py:334
  40.8 0.7 slice.28
  41.5 2.4 %collective-permute-done.6.refs_8_.refs_17_.refs_22_ = bf16[4,16,1536]{2,1,0:T(8,128)(2,1)S(1)} collective-permute-done((bf16[4,16,1536]{2,1,0:T(8,128)(2,1)S(1)}, bf16[4,16,1536]{2,1,0:T(8,128)(2,1)S(1)}, u32[]{:S(2)}, u32[]{:S(2)}) %collective-permute-start.6) | collective-permute-done | bytes 196640 | tf_op jit(solution)/shard_map/ppermute | solution.py:334
  43.9 4.6 %collective-permute-done.5.refs_7_.refs_16_.refs_21_ = bf16[4,16,1536]{2,1,0:T(8,128)(2,1)S(1)} collective-permute-done((bf16[4,16,1536]{2,1,0:T(8,128)(2,1)}, bf16[4,16,1536]{2,1,0:T(8,128)(2,1)S(1)}, u32[]{:S(2)}, u32[]{:S(2)}) %collective-permute-start.5) | collective-permute-done | bytes 196640 | tf_op jit(solution)/shard_map/ppermute | solution.py:334
  48.5 1.4 %interleave.2 = (bf16[1104,256]{1,0:T(8,128)(2,1)S(1)}, bf16[1152,256]{1,0:T(8,128)(2,1)S(1)}, bf16[128,256]{1,0:T(8,128)(2,1)S(1)}, bf16[32,128]{1,0:T(8,128)(2,1)S(1)}) custom-call(s32[2]{0:T(128)S(1)} %pad_add_fusion.pos, bf16[8,16,1408]{2,1,0:T(8,128)(2,1)S(1)} %slice.24.refs_0_.refs_9_, bf16[8,16,1408]{2,1,0:T(8,128)(2,1)S(1)} %collective-permute-done.refs_1_.refs_10_, ...), custom_call_target="tpu_custom_call" | custom-call | tf_op jit(solution)/shard_map/interleave/pallas_call | solution.py:205
  49.9 1.8 %collective-permute-start.10 = (bf16[1152,256]{1,0:T(8,128)(2,1)S(1)}, bf16[1152,256]{1,0:T(8,128)(2,1)S(1)}, u32[]{:S(2)}, u32[]{:S(2)}) collective-permute-start(bf16[1152,256]{1,0:T(8,128)(2,1)S(1)} %get-tuple-element.28.refs_8_), channel_id=1, source_target_pairs={{0,96},{32,0},{64,32},{96,64},{1,97},{33,1},{65,33},{97,65},{2,98}... | collective-permute-start | bytes 1769480 | tf_op jit(solution)/shard_map/ppermute | solution.py:328
  52.2 1.9 %collective-permute-start.7 = (bf16[1104,256]{1,0:T(8,128)(2,1)S(1)}, bf16[1104,256]{1,0:T(8,128)(2,1)S(1)}, u32[]{:S(2)}, u32[]{:S(2)}) collective-permute-start(bf16[1104,256]{1,0:T(8,128)(2,1)S(1)} %get-tuple-element.27.refs_0_.refs_4_), channel_id=1, source_target_pairs={{0,8},{8,16},{16,24},{24,0},{1,9},{9,17},{17,25},{25,1},{2,10},{10... | collective-permute-start | bytes 1695752 | tf_op jit(solution)/shard_map/ppermute | solution.py:328
  54.1 2.7 %collective-permute-start.11 = (bf16[128,256]{1,0:T(8,128)(2,1)S(1)}, bf16[128,256]{1,0:T(8,128)(2,1)S(1)}, u32[]{:S(2)}, u32[]{:S(2)}) collective-permute-start(bf16[128,256]{1,0:T(8,128)(2,1)S(1)} %get-tuple-element.31.refs_0_), channel_id=1, source_target_pairs={{0,64},{32,96},{64,0},{96,32},{1,65},{33,97},{65,1},{97,33},{2,66}... | collective-permute-start | bytes 196616 | tf_op jit(solution)/shard_map/ppermute | solution.py:364
  56.8 1.4 %interleave.3 = (bf16[1632,256]{1,0:T(8,128)(2,1)S(1)}, bf16[1536,256]{1,0:T(8,128)(2,1)S(1)}, bf16[128,1024]{1,0:T(8,128)(2,1)S(1)}) custom-call(s32[2]{0:T(128)S(1)} %pad_add_fusion.pos, bf16[8,16,1408]{2,1,0:T(8,128)(2,1)S(1)} %slice.24.refs_0_.refs_9_, bf16[8,16,1408]{2,1,0:T(8,128)(2,1)S(1)} %collective-permute-done.refs_1_.refs_10_, ...), custom_call_target="tpu_custom_call" | custom-call | tf_op jit(solution)/shard_map/interleave/pallas_call | solution.py:205
  58.2 7.8 %collective-permute-done.11.refs_3_ = bf16[128,256]{1,0:T(8,128)(2,1)S(1)} collective-permute-done((bf16[128,256]{1,0:T(8,128)(2,1)S(1)}, bf16[128,256]{1,0:T(8,128)(2,1)S(1)}, u32[]{:S(2)}, u32[]{:S(2)}) %collective-permute-start.11) | collective-permute-done | bytes 65568 | tf_op jit(solution)/shard_map/ppermute | solution.py:364
  66.2 1.4 %collective-permute-start.15 = (bf16[1536,256]{1,0:T(8,128)(2,1)S(1)}, bf16[1536,256]{1,0:T(8,128)(2,1)S(1)}, u32[]{:S(2)}, u32[]{:S(2)}) collective-permute-start(bf16[1536,256]{1,0:T(8,128)(2,1)S(1)} %get-tuple-element.46.refs_8_), channel_id=1, source_target_pairs={{0,96},{32,0},{64,32},{96,64},{1,97},{33,1},{65,33},{97,65},{2,98}... | collective-permute-start | bytes 2359304 | tf_op jit(solution)/shard_map/ppermute | solution.py:368
  67.6 0.7 collective-permute-start.13
  68.3 2.0 %collective-permute-start.12 = (bf16[1104,256]{1,0:T(8,128)(2,1)S(1)}, bf16[1104,256]{1,0:T(8,128)(2,1)S(1)}, u32[]{:S(2)}, u32[]{:S(2)}) collective-permute-start(bf16[1104,256]{1,0:T(8,128)(2,1)S(1)} %collective-permute-done.7.refs_1_.refs_5_), channel_id=1, source_target_pairs={{0,8},{8,16},{16,24},{24,0},{1,9},{9,17},{17,25},{25,1},{2,10},{10... | collective-permute-start | bytes 1695752 | tf_op jit(solution)/shard_map/ppermute | solution.py:367
  70.2 1.0 arrange_left.1
  71.2 5.8 %all-gather = bf16[1024,128]{1,0:T(8,128)(2,1)S(1)} all-gather(bf16[256,128]{1,0:T(8,128)(2,1)S(1)} %arrange_left.1), channel_id=2, replica_groups=mesh['x'=4,'z'=4,'yh'=2,'yl'=2,'core'=2] {'yl','core'}, dimensions={0}, use_global_device_ids=true | all-gather | bytes 327680 | tf_op jit(solution)/shard_map/all_gather | solution.py:370
  77.0 2.1 %collective-permute-done.12.refs_3_.refs_7_ = bf16[1104,256]{1,0:T(8,128)(2,1)S(1)} collective-permute-done((bf16[1104,256]{1,0:T(8,128)(2,1)S(1)}, bf16[1104,256]{1,0:T(8,128)(2,1)S(1)}, u32[]{:S(2)}, u32[]{:S(2)}) %collective-permute-start.12) | collective-permute-done | bytes 565280 | tf_op jit(solution)/shard_map/ppermute | solution.py:367
  79.1 0.4 collective-permute-done.13.refs_11_
  79.5 1.0 collective-permute-start.16
  80.5 0.4 collective-permute-done.15.refs_10_
  80.9 2.6 %collective-permute-done.14.refs_6_ = bf16[1632,256]{1,0:T(8,128)(2,1)S(1)} collective-permute-done((bf16[1632,256]{1,0:T(8,128)(2,1)S(1)}, bf16[1632,256]{1,0:T(8,128)(2,1)S(1)}, u32[]{:S(2)}, u32[]{:S(2)}) %collective-permute-start.14) | collective-permute-done | bytes 835616 | tf_op jit(solution)/shard_map/ppermute | solution.py:368
  83.6 0.8 collective-permute-start.18
  84.4 2.4 %collective-permute-start.19 = (bf16[1536,256]{1,0:T(8,128)(2,1)S(1)}, bf16[1536,256]{1,0:T(8,128)(2,1)S(1)}, u32[]{:S(2)}, u32[]{:S(2)}) collective-permute-start(bf16[1536,256]{1,0:T(8,128)(2,1)S(1)} %collective-permute-done.15.refs_10_), channel_id=1, source_target_pairs={{0,96},{32,0},{64,32},{96,64},{1,97},{33,1},{65,33},{97,65},{2,98}... | collective-permute-start | bytes 2359304 | tf_op jit(solution)/shard_map/ppermute | solution.py:375
  86.8 15.2 %pair.2.refs_12_ = bf16[32,1280,128]{2,1,0:T(8,128)(2,1)} custom-call(bf16[4,256,128]{2,1,0:T(8,128)(2,1)S(1)} %bitcast.12, bf16[128,1024]{1,0:T(8,128)(2,1)S(1)} %get-tuple-element.40.w_ref, bf16[32,128]{1,0:T(8,128)(2,1)S(1)} %get-tuple-element.41.mine_ref, bf16[1104,256]{1,0:T(8,128)(2,1)S(1)} %get-tuple-element.27.refs_0_.refs_4_, ...), custom_call_target="tpu_custom_call" | custom-call | tf_op jit(solution)/shard_map/pair/pallas_call | solution.py:304
  102.0 22.4 %pair.3 = bf16[32,1280,128]{2,1,0:T(8,128)(2,1)} custom-call(bf16[4,256,128]{2,1,0:T(8,128)(2,1)S(1)} %bitcast.13, bf16[128,1024]{1,0:T(8,128)(2,1)S(1)} %get-tuple-element.40.w_ref, bf16[32,128]{1,0:T(8,128)(2,1)S(1)} %get-tuple-element.41.mine_ref, bf16[1104,256]{1,0:T(8,128)(2,1)S(1)} %get-tuple-element.27.refs_0_.refs_4_, ...), custom_call_target="tpu_custom_call", output_to_operand_aliasing={{}: (15, {})} | custom-call | tf_op jit(solution)/shard_map/pair/pallas_call | solution.py:304
  (25 shorter events, 0.7 us)
Async XLA Ops:
  0.0 56.8 %copy-start = (bf16[1024,128]{1,0:T(8,128)(2,1)S(1)}, bf16[1024,128]{1,0:T(8,128)(2,1)}, u32[]{:S(2)}) copy-start(bf16[1024,128]{1,0:T(8,128)(2,1)} %refs_13_.1) | copy-start | bytes 786436
  23.5 11.1 %collective-permute-start = (bf16[8,16,1408]{2,1,0:T(8,128)(2,1)S(1)}, bf16[8,16,1408]{2,1,0:T(8,128)(2,1)S(1)}, u32[]{:S(2)}, u32[]{:S(2)}) collective-permute-start(bf16[8,16,1408]{2,1,0:T(8,128)(2,1)S(1)} %slice.24.refs_0_.refs_9_), channel_id=1, source_target_pairs={{0,32},{32,64},{64,96},{96,0},{1,33},{33,65},{65,97},{97,1},{2,34}... | collective-permute-start | bytes 1081352 | tf_op jit(solution)/shard_map/ppermute | solution.py:328
  25.1 11.8 %collective-permute-start.4 = (bf16[8,16,1536]{2,1,0:T(8,128)(2,1)S(1)}, bf16[8,16,1536]{2,1,0:T(8,128)(2,1)S(1)}, u32[]{:S(2)}, u32[]{:S(2)}) collective-permute-start(bf16[8,16,1536]{2,1,0:T(8,128)(2,1)S(1)} %pad_maximum_fusion.refs_4_.refs_13_.refs_18_), channel_id=1, source_target_pairs={{0,24},{8,0},{16,8},{24,16},{1,25},{9,1},{17,9},{25,17},{2,26},{10... | collective-permute-start | bytes 1179656 | tf_op jit(solution)/shard_map/ppermute | solution.py:328
  29.2 11.5 %collective-permute-start.3 = (bf16[8,16,1536]{2,1,0:T(8,128)(2,1)S(1)}, bf16[8,16,1536]{2,1,0:T(8,128)(2,1)S(1)}, u32[]{:S(2)}, u32[]{:S(2)}) collective-permute-start(bf16[8,16,1536]{2,1,0:T(8,128)(2,1)S(1)} %pad_maximum_fusion.refs_4_.refs_13_.refs_18_), channel_id=1, source_target_pairs={{0,8},{8,16},{16,24},{24,0},{1,9},{9,17},{17,25},{25,1},{2,10},{10... | collective-permute-start | bytes 1179656 | tf_op jit(solution)/shard_map/ppermute | solution.py:328
  29.3 12.3 %collective-permute-start.1 = (bf16[8,16,1408]{2,1,0:T(8,128)(2,1)S(1)}, bf16[8,16,1408]{2,1,0:T(8,128)(2,1)S(1)}, u32[]{:S(2)}, u32[]{:S(2)}) collective-permute-start(bf16[8,16,1408]{2,1,0:T(8,128)(2,1)S(1)} %slice.24.refs_0_.refs_9_), channel_id=1, source_target_pairs={{0,96},{32,0},{64,32},{96,64},{1,97},{33,1},{65,33},{97,65},{2,98}... | collective-permute-start | bytes 1081352 | tf_op jit(solution)/shard_map/ppermute | solution.py:328
  34.6 14.0 %collective-permute-start.2 = (bf16[8,16,1408]{2,1,0:T(8,128)(2,1)S(1)}, bf16[8,16,1408]{2,1,0:T(8,128)(2,1)S(1)}, u32[]{:S(2)}, u32[]{:S(2)}) collective-permute-start(bf16[8,16,1408]{2,1,0:T(8,128)(2,1)S(1)} %collective-permute-done.refs_1_.refs_10_), channel_id=1, source_target_pairs={{0,32},{32,64},{64,96},{96,0},{1,33},{33,65},{65,97},{97,1},{2,34}... | collective-permute-start | bytes 1081352 | tf_op jit(solution)/shard_map/ppermute | solution.py:357
  37.0 6.9 %collective-permute-start.6 = (bf16[4,16,1536]{2,1,0:T(8,128)(2,1)S(1)}, bf16[4,16,1536]{2,1,0:T(8,128)(2,1)S(1)}, u32[]{:S(2)}, u32[]{:S(2)}) collective-permute-start(bf16[4,16,1536]{2,1,0:T(8,128)(2,1)S(1)} %slice.29), channel_id=1, source_target_pairs={{0,24},{8,0},{16,8},{24,16},{1,25},{9,1},{17,9},{25,17},{2,26},{10... | collective-permute-start | bytes 589832 | tf_op jit(solution)/shard_map/ppermute | solution.py:334
  41.4 7.1 %collective-permute-start.5 = (bf16[4,16,1536]{2,1,0:T(8,128)(2,1)}, bf16[4,16,1536]{2,1,0:T(8,128)(2,1)S(1)}, u32[]{:S(2)}, u32[]{:S(2)}) collective-permute-start(bf16[4,16,1536]{2,1,0:T(8,128)(2,1)} %slice.28), channel_id=1, source_target_pairs={{0,8},{8,16},{16,24},{24,0},{1,9},{9,17},{17,25},{25,1},{2,10},{10... | collective-permute-start | bytes 589832 | tf_op jit(solution)/shard_map/ppermute | solution.py:334
  49.9 16.1 %collective-permute-start.10 = (bf16[1152,256]{1,0:T(8,128)(2,1)S(1)}, bf16[1152,256]{1,0:T(8,128)(2,1)S(1)}, u32[]{:S(2)}, u32[]{:S(2)}) collective-permute-start(bf16[1152,256]{1,0:T(8,128)(2,1)S(1)} %get-tuple-element.28.refs_8_), channel_id=1, source_target_pairs={{0,96},{32,0},{64,32},{96,64},{1,97},{33,1},{65,33},{97,65},{2,98}... | collective-permute-start | bytes 1769480 | tf_op jit(solution)/shard_map/ppermute | solution.py:328
  51.8 14.4 %collective-permute-start.9 = (bf16[1152,256]{1,0:T(8,128)(2,1)S(1)}, bf16[1152,256]{1,0:T(8,128)(2,1)S(1)}, u32[]{:S(2)}, u32[]{:S(2)}) collective-permute-start(bf16[1152,256]{1,0:T(8,128)(2,1)S(1)} %get-tuple-element.28.refs_8_), channel_id=1, source_target_pairs={{0,32},{32,64},{64,96},{96,0},{1,33},{33,65},{65,97},{97,1},{2,34}... | collective-permute-start | bytes 1769480 | tf_op jit(solution)/shard_map/ppermute | solution.py:328
  52.0 14.0 %collective-permute-start.8 = (bf16[1104,256]{1,0:T(8,128)(2,1)S(1)}, bf16[1104,256]{1,0:T(8,128)(2,1)S(1)}, u32[]{:S(2)}, u32[]{:S(2)}) collective-permute-start(bf16[1104,256]{1,0:T(8,128)(2,1)S(1)} %get-tuple-element.27.refs_0_.refs_4_), channel_id=1, source_target_pairs={{0,24},{8,0},{16,8},{24,16},{1,25},{9,1},{17,9},{25,17},{2,26},{10... | collective-permute-start | bytes 1695752 | tf_op jit(solution)/shard_map/ppermute | solution.py:328
  52.2 13.9 %collective-permute-start.7 = (bf16[1104,256]{1,0:T(8,128)(2,1)S(1)}, bf16[1104,256]{1,0:T(8,128)(2,1)S(1)}, u32[]{:S(2)}, u32[]{:S(2)}) collective-permute-start(bf16[1104,256]{1,0:T(8,128)(2,1)S(1)} %get-tuple-element.27.refs_0_.refs_4_), channel_id=1, source_target_pairs={{0,8},{8,16},{16,24},{24,0},{1,9},{9,17},{17,25},{25,1},{2,10},{10... | collective-permute-start | bytes 1695752 | tf_op jit(solution)/shard_map/ppermute | solution.py:328
  54.1 12.0 %collective-permute-start.11 = (bf16[128,256]{1,0:T(8,128)(2,1)S(1)}, bf16[128,256]{1,0:T(8,128)(2,1)S(1)}, u32[]{:S(2)}, u32[]{:S(2)}) collective-permute-start(bf16[128,256]{1,0:T(8,128)(2,1)S(1)} %get-tuple-element.31.refs_0_), channel_id=1, source_target_pairs={{0,64},{32,96},{64,0},{96,32},{1,65},{33,97},{65,1},{97,33},{2,66}... | collective-permute-start | bytes 196616 | tf_op jit(solution)/shard_map/ppermute | solution.py:364
  66.2 17.4 %collective-permute-start.14 = (bf16[1632,256]{1,0:T(8,128)(2,1)S(1)}, bf16[1632,256]{1,0:T(8,128)(2,1)S(1)}, u32[]{:S(2)}, u32[]{:S(2)}) collective-permute-start(bf16[1632,256]{1,0:T(8,128)(2,1)S(1)} %get-tuple-element.44.refs_4_), channel_id=1, source_target_pairs={{0,24},{8,0},{16,8},{24,16},{1,25},{9,1},{17,9},{25,17},{2,26},{10... | collective-permute-start | bytes 2506760 | tf_op jit(solution)/shard_map/ppermute | solution.py:368
  66.2 14.7 %collective-permute-start.15 = (bf16[1536,256]{1,0:T(8,128)(2,1)S(1)}, bf16[1536,256]{1,0:T(8,128)(2,1)S(1)}, u32[]{:S(2)}, u32[]{:S(2)}) collective-permute-start(bf16[1536,256]{1,0:T(8,128)(2,1)S(1)} %get-tuple-element.46.refs_8_), channel_id=1, source_target_pairs={{0,96},{32,0},{64,32},{96,64},{1,97},{33,1},{65,33},{97,65},{2,98}... | collective-permute-start | bytes 2359304 | tf_op jit(solution)/shard_map/ppermute | solution.py:368
  67.6 11.9 %collective-permute-start.13 = (bf16[1152,256]{1,0:T(8,128)(2,1)S(1)}, bf16[1152,256]{1,0:T(8,128)(2,1)S(1)}, u32[]{:S(2)}, u32[]{:S(2)}) collective-permute-start(bf16[1152,256]{1,0:T(8,128)(2,1)S(1)} %collective-permute-done.9.refs_1_.refs_9_), channel_id=1, source_target_pairs={{0,32},{32,64},{64,96},{96,0},{1,33},{33,65},{65,97},{97,1},{2,34}... | collective-permute-start | bytes 1769480 | tf_op jit(solution)/shard_map/ppermute | solution.py:367
  68.3 10.8 %collective-permute-start.12 = (bf16[1104,256]{1,0:T(8,128)(2,1)S(1)}, bf16[1104,256]{1,0:T(8,128)(2,1)S(1)}, u32[]{:S(2)}, u32[]{:S(2)}) collective-permute-start(bf16[1104,256]{1,0:T(8,128)(2,1)S(1)} %collective-permute-done.7.refs_1_.refs_5_), channel_id=1, source_target_pairs={{0,8},{8,16},{16,24},{24,0},{1,9},{9,17},{17,25},{25,1},{2,10},{10... | collective-permute-start | bytes 1695752 | tf_op jit(solution)/shard_map/ppermute | solution.py:367
  79.5 22.6 %collective-permute-start.16 = (bf16[1632,256]{1,0:T(8,128)(2,1)S(1)}, bf16[1632,256]{1,0:T(8,128)(2,1)S(1)}, u32[]{:S(2)}, u32[]{:S(2)}) collective-permute-start(bf16[1632,256]{1,0:T(8,128)(2,1)S(1)} %get-tuple-element.44.refs_4_), channel_id=1, source_target_pairs={{0,8},{8,16},{16,24},{24,0},{1,9},{9,17},{17,25},{25,1},{2,10},{10... | collective-permute-start | bytes 2506760 | tf_op jit(solution)/shard_map/ppermute | solution.py:373
  83.6 18.5 %collective-permute-start.17 = (bf16[1632,256]{1,0:T(8,128)(2,1)S(1)}, bf16[1632,256]{1,0:T(8,128)(2,1)S(1)}, u32[]{:S(2)}, u32[]{:S(2)}) collective-permute-start(bf16[1632,256]{1,0:T(8,128)(2,1)S(1)} %collective-permute-done.14.refs_6_), channel_id=1, source_target_pairs={{0,24},{8,0},{16,8},{24,16},{1,25},{9,1},{17,9},{25,17},{2,26},{10... | collective-permute-start | bytes 2506760 | tf_op jit(solution)/shard_map/ppermute | solution.py:375
  83.6 18.5 %collective-permute-start.18 = (bf16[1536,256]{1,0:T(8,128)(2,1)S(1)}, bf16[1536,256]{1,0:T(8,128)(2,1)S(1)}, u32[]{:S(2)}, u32[]{:S(2)}) collective-permute-start(bf16[1536,256]{1,0:T(8,128)(2,1)S(1)} %get-tuple-element.46.refs_8_), channel_id=1, source_target_pairs={{0,32},{32,64},{64,96},{96,0},{1,33},{33,65},{65,97},{97,1},{2,34}... | collective-permute-start | bytes 2359304 | tf_op jit(solution)/shard_map/ppermute | solution.py:373
  84.4 17.7 %collective-permute-start.19 = (bf16[1536,256]{1,0:T(8,128)(2,1)S(1)}, bf16[1536,256]{1,0:T(8,128)(2,1)S(1)}, u32[]{:S(2)}, u32[]{:S(2)}) collective-permute-start(bf16[1536,256]{1,0:T(8,128)(2,1)S(1)} %collective-permute-done.15.refs_10_), channel_id=1, source_target_pairs={{0,96},{32,0},{64,32},{96,64},{1,97},{33,1},{65,33},{97,65},{2,98}... | collective-permute-start | bytes 2359304 | tf_op jit(solution)/shard_map/ppermute | solution.py:375
